TPU v7x, 256 devices: a whole 4x4x8 slice. The times are simulated.
256 devices in a mesh: gx: 4 (over y), gy: 8 (over z), gz: 8 (over x, core).
Axes of the slice: x: 4, y: 4, z: 8, core: 2. Of those that a mesh axis runs over, the one named last changes fastest.
Arguments:
- right_side: float32 [64, 256, 1024], P('gx', 'gy', 'gz'), may hold values from -6 to 6
- conductivity: float32 [64, 256, 1024], P('gx', 'gy', 'gz'), may hold values from 0.2 to 5
- screening: float32 [64, 256, 1024], P('gx', 'gy', 'gz'), may hold values from 0.01 to 0.2
Outputs:
- solution_field: float32 [64, 256, 1024], P('gx', 'gy', 'gz')
All inputs are finite; a program needn't handle non-finite values.
Results may differ from a plain program's by a relative error of at most 0.0001.
Values sent between devices are 32-bit elements; how exact they have to be, the bound alone decides.
No kernel may reach another device: no remote copies, remote signals or barrier semaphores. Data moves between devices by JAX's collectives and lax.ppermute only.
A program may use at most 128 MiB of HBM per device.

v0:
```python
import jax
import jax.numpy as jnp
from jax import lax
from jax.sharding import PartitionSpec as P

SWEEPS = 2
COARSE_SWEEPS = 8


damping = 2.0 / 3.0


def extended(x, sides, width):
    for axis, dim in sides:
        size, length = (lax.axis_size(axis), x.shape[dim])
        up = [(i, (i + 1) % size) for i in range(size - 1)]
        down = [(j, i) for i, j in up]
        last = lax.slice_in_dim(x, length - width, length, axis=dim)
        first = lax.slice_in_dim(x, 0, width, axis=dim)
        before = lax.ppermute(last, axis, up)
        after = lax.ppermute(first, axis, down)
        x = jnp.concatenate([before, x, after], axis=dim)
    return x


def neighbour_views():
    inner = slice(1, -1)
    return [
        (slice(2, None), inner, inner),
        (slice(0, -2), inner, inner),
        (inner, slice(2, None), inner),
        (inner, slice(0, -2), inner),
        (inner, inner, slice(2, None)),
        (inner, inner, slice(0, -2)),
    ]


def operate(field_pad, cond_pad, field, conduct, mass_term, spacing):
    result = mass_term * field
    diagonal = mass_term
    for window in neighbour_views():
        face_weight = spacing * 0.5 * (conduct + cond_pad[window])
        result = result + face_weight * (field - field_pad[window])
        diagonal = diagonal + face_weight
    return (result, diagonal)


def coarsen(field):
    return field.reshape(
        field.shape[0] // 2, 2, field.shape[1] // 2, 2, field.shape[2] // 2, 2
    ).mean(axis=(1, 3, 5))


def refine(field):
    return jnp.repeat(jnp.repeat(jnp.repeat(field, 2, 0), 2, 1), 2, 2)


def relax(field, field_pad, source, cond_pad, conduct, mass_term, spacing):
    result, diagonal = operate(field_pad, cond_pad, field, conduct, mass_term, spacing)
    return field + damping * (source - result) / diagonal


def smooth(field, source, cond_pad, conduct, mass_term, spacing):
    field_pad = extended(field, (("gx", 0), ("gy", 1), ("gz", 2)), 1)
    return relax(field, field_pad, source, cond_pad, conduct, mass_term, spacing)


def assemble(stacked, count_x, count_y, count_z):
    size_a, size_b, size_c = (stacked.shape[1], stacked.shape[2], stacked.shape[3])
    grid = stacked.reshape(count_x, count_y, count_z, size_a, size_b, size_c)
    return grid.transpose(0, 3, 1, 4, 2, 5).reshape(
        count_x * size_a, count_y * size_b, count_z * size_c
    )


def per_device(right_side, conductivity, screening):
    conducts = [conductivity]
    masses = [screening]
    for level_index in range(3):
        conducts.append(coarsen(conducts[level_index]))
        masses.append(coarsen(masses[level_index]))
    sources = [right_side]
    fields = []
    pads = []
    for level_index in range(3):
        pads.append(extended(conducts[level_index], (("gx", 0), ("gy", 1), ("gz", 2)), 1))
    for level_index in range(3):
        spacing = 0.25**level_index
        field = jnp.zeros_like(sources[level_index])
        for sweep_index in range(SWEEPS):
            field = smooth(
                field,
                sources[level_index],
                pads[level_index],
                conducts[level_index],
                masses[level_index],
                spacing,
            )
        field_pad = extended(field, (("gx", 0), ("gy", 1), ("gz", 2)), 1)
        result, diagonal = operate(
            field_pad, pads[level_index], field, conducts[level_index], masses[level_index], spacing
        )
        fields.append(field)
        sources.append(coarsen(sources[level_index] - result))
    coarse_spacing = 0.25**3
    stack_src, stack_cond, stack_mass = (
        lax.all_gather(sources[3][None], ("gx", "gy", "gz"), axis=0, tiled=True),
        lax.all_gather(conducts[3][None], ("gx", "gy", "gz"), axis=0, tiled=True),
        lax.all_gather(masses[3][None], ("gx", "gy", "gz"), axis=0, tiled=True),
    )
    count_x, count_y, count_z = (lax.axis_size("gx"), lax.axis_size("gy"), lax.axis_size("gz"))
    whole_src = assemble(stack_src, count_x, count_y, count_z)
    whole_cond = assemble(stack_cond, count_x, count_y, count_z)
    whole_mass = assemble(stack_mass, count_x, count_y, count_z)
    whole_cond_pad = jnp.pad(whole_cond, 1)
    whole_field = jnp.zeros_like(whole_src)
    for sweep_index in range(COARSE_SWEEPS):
        whole_field = relax(
            whole_field,
            jnp.pad(whole_field, 1),
            whole_src,
            whole_cond_pad,
            whole_cond,
            whole_mass,
            coarse_spacing,
        )
    size_a, size_b, size_c = sources[3].shape
    starts = (
        lax.axis_index("gx") * size_a,
        lax.axis_index("gy") * size_b,
        lax.axis_index("gz") * size_c,
    )
    field = lax.dynamic_slice(whole_field, starts, (size_a, size_b, size_c))
    for level_index in (2, 1, 0):
        spacing = 0.25**level_index
        field = fields[level_index] + refine(field)
        for sweep_index in range(SWEEPS):
            field = smooth(
                field,
                sources[level_index],
                pads[level_index],
                conducts[level_index],
                masses[level_index],
                spacing,
            )
    return field


def solution(mesh):
    placed = (P("gx", "gy", "gz"), P("gx", "gy", "gz"), P("gx", "gy", "gz"))
    return jax.shard_map(
        per_device, mesh=mesh, in_specs=placed, out_specs=P("gx", "gy", "gz"), check_vma=False
    )
```

profile of v0, /device:TPU:153, one launch (start us, length us, event | category | flops | bytes accessed | tf_op | source)
XLA Modules:
  0.0 705.3 jit_solution(15229721502254910816)
XLA Ops:
  3.7 4.0 collective-permute-start.49
  9.7 4.1 collective-permute-start
  13.8 18.9 %reshape.105 = f32[8,2,16,2,64,2]{5,4,3,2,1,0:T(8,128)} reshape(f32[16,32,128]{2,1,0:T(8,128)} %param.4) | data formatting | bytes 524288 | tf_op jit(solution)/shard_map/reshape | solution.py:49
  32.7 7.0 reduce_sum.83
  42.3 18.1 %reshape.104 = f32[8,2,16,2,64,2]{5,4,3,2,1,0:T(8,128)} reshape(f32[16,32,128]{2,1,0:T(8,128)S(1)} %copy-done.1) | data formatting | bytes 524288 | tf_op jit(solution)/shard_map/reshape | solution.py:49
  60.4 7.0 reduce_sum.82
  96.3 4.3 collective-permute-start.4
  102.8 8.8 %collective-permute-start.11 = (f32[18,34,1]{2,1,0:T(8,128)S(1)}, f32[18,34,1]{2,1,0:T(8,128)S(1)}, u32[]{:S(2)}, u32[]{:S(2)}) collective-permute-start(f32[18,34,1]{2,1,0:T(8,128)S(1)} %get-tuple-element.36), channel_id=1, source_target_pairs={{0,1},{1,2},{2,3},{3,4},{4,5},{5,6},{6,7},{8,9},{9,10},{10,11},{11... | collective-permute-start | bytes 7352 | tf_op jit(solution)/shard_map/ppermute | solution.py:20
  115.7 3.6 collective-permute-start.10
  121.3 4.3 collective-permute-start.24
  129.7 4.0 collective-permute-start.12
  135.0 4.9 collective-permute-start.29
  141.9 4.6 collective-permute-start.14
  148.4 4.6 collective-permute-start.28
  155.7 4.7 collective-permute-start.17
  164.8 4.4 collective-permute-done.16
  169.8 4.2 collective-permute-start.18
  180.7 4.9 collective-permute-start.20
  187.6 3.8 collective-permute-done.21
  191.6 5.0 collective-permute-start.23
  207.8 18.1 %reshape.103 = f32[8,2,16,2,64,2]{5,4,3,2,1,0:T(8,128)} reshape(f32[16,32,128]{2,1,0:T(8,128)S(1)} %fusion.60) | data formatting | bytes 524288 | tf_op jit(solution)/shard_map/reshape | solution.py:49
  225.9 7.0 reduce_sum.81
  257.6 4.5 collective-permute-start.41
  264.1 4.2 collective-permute-done.40
  285.3 4.3 collective-permute-start.47
  291.7 4.1 collective-permute-done.46
  299.3 4.3 collective-permute-start.60
  304.9 60.9 %all-gather.1 = f32[512,4,16]{2,1,0:T(4,128)S(1)} all-gather(f32[2,4,16]{2,1,0:T(4,128)} %broadcast_multiply_fusion.5), channel_id=3, replica_groups=mesh['gx'=4,'gy'=8,'gz'=8] {'gx','gy','gz'}, dimensions={0}, use_global_device_ids=true | all-gather | bytes 131584 | tf_op jit(solution)/shard_map/all_gather | solution.py:109
  367.8 61.4 %all-gather.2 = f32[512,4,16]{2,1,0:T(4,128)S(1)} all-gather(f32[2,4,16]{2,1,0:T(4,128)} %broadcast_multiply_fusion.4), channel_id=4, replica_groups=mesh['gx'=4,'gy'=8,'gz'=8] {'gx','gy','gz'}, dimensions={0}, use_global_device_ids=true | all-gather | bytes 131584 | tf_op jit(solution)/shard_map/all_gather | solution.py:108
  450.9 4.6 collective-permute-start.68
  456.3 4.3 collective-permute-start.70
  460.6 4.4 collective-permute-start.71
  470.0 63.3 %all-gather = f32[512,4,16]{2,1,0:T(4,128)S(1)} all-gather(f32[2,4,16]{2,1,0:T(4,128)S(1)} %broadcast_multiply_fusion.6), channel_id=2, replica_groups=mesh['gx'=4,'gy'=8,'gz'=8] {'gx','gy','gz'}, dimensions={0}, use_global_device_ids=true | all-gather | bytes 131584 | tf_op jit(solution)/shard_map/all_gather | solution.py:107
  547.0 4.1 collective-permute-start.74
  552.0 4.6 collective-permute-start.76
  569.8 5.1 collective-permute-start.80
  575.8 4.3 collective-permute-start.82
  580.1 4.0 collective-permute-start.83
  594.1 5.1 collective-permute-start.86
  601.1 3.6 collective-permute-done.87
  604.9 7.1 %collective-permute-start.89 = (f32[10,18,1]{2,1,0:T(8,128)S(1)}, f32[10,18,1]{2,1,0:T(8,128)S(1)}, u32[]{:S(2)}, u32[]{:S(2)}) collective-permute-start(f32[10,18,1]{2,1,0:T(8,128)S(1)} %get-tuple-element.65), channel_id=1, source_target_pairs={{0,1},{1,2},{2,3},{3,4},{4,5},{5,6},{6,7},{8,9},{9,10},{10,11},{11... | collective-permute-start | bytes 2168 | tf_op jit(solution)/shard_map/ppermute | solution.py:20
  613.9 4.3 collective-permute-done.88
  633.0 4.4 collective-permute-start.95
  639.5 4.0 collective-permute-done.94
  661.4 4.4 collective-permute-start.101
  670.2 4.4 collective-permute-done.100
  690.0 4.3 collective-permute-start.107
  698.7 4.4 collective-permute-done.106
  (455 shorter events, 263.4 us)
Async XLA Ops:
  0.0 90.8 %collective-permute-start.1 = (f32[1,32,128]{2,1,0:T(8,128)S(1)}, f32[1,32,128]{2,1,0:T(8,128)S(1)}, u32[]{:S(2)}, u32[]{:S(2)}) collective-permute-start(f32[1,32,128]{2,1,0:T(8,128)S(1)} %broadcast.117), channel_id=1, source_target_pairs={{64,0},{128,64},{192,128},{65,1},{129,65},{193,129},{66,2},{130,66... | collective-permute-start | bytes 49160 | tf_op jit(solution)/shard_map/ppermute | solution.py:21
  2.4 88.4 %collective-permute-start.3 = (f32[1,32,128]{2,1,0:T(8,128)S(1)}, f32[1,32,128]{2,1,0:T(8,128)S(1)}, u32[]{:S(2)}, u32[]{:S(2)}) collective-permute-start(f32[1,32,128]{2,1,0:T(8,128)S(1)} %broadcast.117), channel_id=1, source_target_pairs={{0,64},{64,128},{128,192},{1,65},{65,129},{129,193},{2,66},{66,130... | collective-permute-start | bytes 49160 | tf_op jit(solution)/shard_map/ppermute | solution.py:20
  3.7 67.8 %collective-permute-start.49 = (f32[1,8,32]{2,1,0:T(8,128)S(1)}, f32[1,8,32]{2,1,0:T(8,128)S(1)}, u32[]{:S(2)}, u32[]{:S(2)}) collective-permute-start(f32[1,8,32]{2,1,0:T(8,128)S(1)} %broadcast.124), channel_id=1, source_target_pairs={{64,0},{128,64},{192,128},{65,1},{129,65},{193,129},{66,2},{130,66... | collective-permute-start | bytes 3080 | tf_op jit(solution)/shard_map/ppermute | solution.py:21
  7.7 65.9 %collective-permute-start.51 = (f32[1,8,32]{2,1,0:T(8,128)S(1)}, f32[1,8,32]{2,1,0:T(8,128)S(1)}, u32[]{:S(2)}, u32[]{:S(2)}) collective-permute-start(f32[1,8,32]{2,1,0:T(8,128)S(1)} %broadcast.124), channel_id=1, source_target_pairs={{0,64},{64,128},{128,192},{1,65},{65,129},{129,193},{2,66},{66,130... | collective-permute-start | bytes 3080 | tf_op jit(solution)/shard_map/ppermute | solution.py:20
  9.7 86.5 %collective-permute-start = (f32[1,32,128]{2,1,0:T(8,128)S(1)}, f32[1,32,128]{2,1,0:T(8,128)S(1)}, u32[]{:S(2)}, u32[]{:S(2)}) collective-permute-start(f32[1,32,128]{2,1,0:T(8,128)S(1)} %get-tuple-element.58), channel_id=1, source_target_pairs={{64,0},{128,64},{192,128},{65,1},{129,65},{193,129},{66,2},{130,66... | collective-permute-start | bytes 49160 | tf_op jit(solution)/shard_map/ppermute | solution.py:21
  74.9 21.2 %collective-permute-start.2 = (f32[1,32,128]{2,1,0:T(8,128)S(1)}, f32[1,32,128]{2,1,0:T(8,128)S(1)}, u32[]{:S(2)}, u32[]{:S(2)}) collective-permute-start(f32[1,32,128]{2,1,0:T(8,128)S(1)} %get-tuple-element.57), channel_id=1, source_target_pairs={{0,64},{64,128},{128,192},{1,65},{65,129},{129,193},{2,66},{66,130... | collective-permute-start | bytes 49160 | tf_op jit(solution)/shard_map/ppermute | solution.py:20
  87.8 41.9 %collective-permute-start.25 = (f32[1,16,64]{2,1,0:T(8,128)S(1)}, f32[1,16,64]{2,1,0:T(8,128)S(1)}, u32[]{:S(2)}, u32[]{:S(2)}) collective-permute-start(f32[1,16,64]{2,1,0:T(8,128)S(1)} %broadcast.120), channel_id=1, source_target_pairs={{64,0},{128,64},{192,128},{65,1},{129,65},{193,129},{66,2},{130,66... | collective-permute-start | bytes 12296 | tf_op jit(solution)/shard_map/ppermute | solution.py:21
  90.8 11.7 %collective-permute-start.5 = (f32[18,1,128]{2,1,0:T(1,128)S(1)}, f32[18,1,128]{2,1,0:T(1,128)S(1)}, u32[]{:S(2)}, u32[]{:S(2)}) collective-permute-start(f32[18,1,128]{2,1,0:T(1,128)S(1)} %get-tuple-element.48), channel_id=1, source_target_pairs={{8,0},{16,8},{24,16},{32,24},{40,32},{48,40},{56,48},{9,1},{17,9},... | collective-permute-start | bytes 27656 | tf_op jit(solution)/shard_map/ppermute | solution.py:21
  94.0 8.6 %collective-permute-start.7 = (f32[18,1,128]{2,1,0:T(1,128)S(1)}, f32[18,1,128]{2,1,0:T(1,128)S(1)}, u32[]{:S(2)}, u32[]{:S(2)}) collective-permute-start(f32[18,1,128]{2,1,0:T(1,128)S(1)} %get-tuple-element.47), channel_id=1, source_target_pairs={{0,8},{8,16},{16,24},{24,32},{32,40},{40,48},{48,56},{1,9},{9,17},... | collective-permute-start | bytes 27656 | tf_op jit(solution)/shard_map/ppermute | solution.py:20
  96.3 17.3 %collective-permute-start.4 = (f32[18,1,128]{2,1,0:T(1,128)S(1)}, f32[18,1,128]{2,1,0:T(1,128)S(1)}, u32[]{:S(2)}, u32[]{:S(2)}) collective-permute-start(f32[18,1,128]{2,1,0:T(1,128)S(1)} %get-tuple-element.46), channel_id=1, source_target_pairs={{8,0},{16,8},{24,16},{32,24},{40,32},{48,40},{56,48},{9,1},{17,9},... | collective-permute-start | bytes 27656 | tf_op jit(solution)/shard_map/ppermute | solution.py:21
  100.7 12.9 %collective-permute-start.6 = (f32[18,1,128]{2,1,0:T(1,128)S(1)}, f32[18,1,128]{2,1,0:T(1,128)S(1)}, u32[]{:S(2)}, u32[]{:S(2)}) collective-permute-start(f32[18,1,128]{2,1,0:T(1,128)S(1)} %get-tuple-element.45), channel_id=1, source_target_pairs={{0,8},{8,16},{16,24},{24,32},{32,40},{40,48},{48,56},{1,9},{9,17},... | collective-permute-start | bytes 27656 | tf_op jit(solution)/shard_map/ppermute | solution.py:20
  102.8 17.2 %collective-permute-start.11 = (f32[18,34,1]{2,1,0:T(8,128)S(1)}, f32[18,34,1]{2,1,0:T(8,128)S(1)}, u32[]{:S(2)}, u32[]{:S(2)}) collective-permute-start(f32[18,34,1]{2,1,0:T(8,128)S(1)} %get-tuple-element.36), channel_id=1, source_target_pairs={{0,1},{1,2},{2,3},{3,4},{4,5},{5,6},{6,7},{8,9},{9,10},{10,11},{11... | collective-permute-start | bytes 7352 | tf_op jit(solution)/shard_map/ppermute | solution.py:20
  111.6 9.7 %collective-permute-start.9 = (f32[18,34,1]{2,1,0:T(8,128)S(1)}, f32[18,34,1]{2,1,0:T(8,128)S(1)}, u32[]{:S(2)}, u32[]{:S(2)}) collective-permute-start(f32[18,34,1]{2,1,0:T(8,128)S(1)} %get-tuple-element.35), channel_id=1, source_target_pairs={{1,0},{2,1},{3,2},{4,3},{5,4},{6,5},{7,6},{9,8},{10,9},{11,10},{12... | collective-permute-start | bytes 7352 | tf_op jit(solution)/shard_map/ppermute | solution.py:21
  113.8 11.8 %collective-permute-start.8 = (f32[18,34,1]{2,1,0:T(8,128)S(1)}, f32[18,34,1]{2,1,0:T(8,128)S(1)}, u32[]{:S(2)}, u32[]{:S(2)}) collective-permute-start(f32[18,34,1]{2,1,0:T(8,128)S(1)} %get-tuple-element.34), channel_id=1, source_target_pairs={{1,0},{2,1},{3,2},{4,3},{5,4},{6,5},{7,6},{9,8},{10,9},{11,10},{12... | collective-permute-start | bytes 7352 | tf_op jit(solution)/shard_map/ppermute | solution.py:21
  115.7 11.2 %collective-permute-start.10 = (f32[18,34,1]{2,1,0:T(8,128)S(1)}, f32[18,34,1]{2,1,0:T(8,128)S(1)}, u32[]{:S(2)}, u32[]{:S(2)}) collective-permute-start(f32[18,34,1]{2,1,0:T(8,128)S(1)} %get-tuple-element.33), channel_id=1, source_target_pairs={{0,1},{1,2},{2,3},{3,4},{4,5},{5,6},{6,7},{8,9},{9,10},{10,11},{11... | collective-permute-start | bytes 7352 | tf_op jit(solution)/shard_map/ppermute | solution.py:20
  120.0 13.7 %collective-permute-start.27 = (f32[1,16,64]{2,1,0:T(8,128)S(1)}, f32[1,16,64]{2,1,0:T(8,128)S(1)}, u32[]{:S(2)}, u32[]{:S(2)}) collective-permute-start(f32[1,16,64]{2,1,0:T(8,128)S(1)} %broadcast.120), channel_id=1, source_target_pairs={{0,64},{64,128},{128,192},{1,65},{65,129},{129,193},{2,66},{66,130... | collective-permute-start | bytes 12296 | tf_op jit(solution)/shard_map/ppermute | solution.py:20
  121.3 20.6 %collective-permute-start.24 = (f32[1,16,64]{2,1,0:T(8,128)S(1)}, f32[1,16,64]{2,1,0:T(8,128)S(1)}, u32[]{:S(2)}, u32[]{:S(2)}) collective-permute-start(f32[1,16,64]{2,1,0:T(8,128)S(1)} %get-tuple-element.95), channel_id=1, source_target_pairs={{64,0},{128,64},{192,128},{65,1},{129,65},{193,129},{66,2},{130,66... | collective-permute-start | bytes 12296 | tf_op jit(solution)/shard_map/ppermute | solution.py:21
  125.6 20.9 %collective-permute-start.26 = (f32[1,16,64]{2,1,0:T(8,128)S(1)}, f32[1,16,64]{2,1,0:T(8,128)S(1)}, u32[]{:S(2)}, u32[]{:S(2)}) collective-permute-start(f32[1,16,64]{2,1,0:T(8,128)S(1)} %get-tuple-element.94), channel_id=1, source_target_pairs={{0,64},{64,128},{128,192},{1,65},{65,129},{129,193},{2,66},{66,130... | collective-permute-start | bytes 12296 | tf_op jit(solution)/shard_map/ppermute | solution.py:20
  126.9 118.3 %collective-permute-start.54 = (f32[6,1,32]{2,1,0:T(1,128)}, f32[6,1,32]{2,1,0:T(1,128)}, u32[]{:S(2)}, u32[]{:S(2)}) collective-permute-start(f32[6,1,32]{2,1,0:T(1,128)} %get-tuple-element.129), channel_id=1, source_target_pairs={{0,8},{8,16},{16,24},{24,32},{32,40},{40,48},{48,56},{1,9},{9,17},... | collective-permute-start | bytes 2312 | tf_op jit(solution)/shard_map/ppermute | solution.py:20
  135.0 20.6 %collective-permute-start.29 = (f32[10,1,64]{2,1,0:T(1,128)S(1)}, f32[10,1,64]{2,1,0:T(1,128)S(1)}, u32[]{:S(2)}, u32[]{:S(2)}) collective-permute-start(f32[10,1,64]{2,1,0:T(1,128)S(1)} %get-tuple-element.85), channel_id=1, source_target_pairs={{8,0},{16,8},{24,16},{32,24},{40,32},{48,40},{56,48},{9,1},{17,9},... | collective-permute-start | bytes 7688 | tf_op jit(solution)/shard_map/ppermute | solution.py:21
  139.9 20.5 %collective-permute-start.31 = (f32[10,1,64]{2,1,0:T(1,128)S(1)}, f32[10,1,64]{2,1,0:T(1,128)S(1)}, u32[]{:S(2)}, u32[]{:S(2)}) collective-permute-start(f32[10,1,64]{2,1,0:T(1,128)S(1)} %get-tuple-element.84), channel_id=1, source_target_pairs={{0,8},{8,16},{16,24},{24,32},{32,40},{40,48},{48,56},{1,9},{9,17},... | collective-permute-start | bytes 7688 | tf_op jit(solution)/shard_map/ppermute | solution.py:20
  148.4 32.3 %collective-permute-start.28 = (f32[10,1,64]{2,1,0:T(1,128)S(1)}, f32[10,1,64]{2,1,0:T(1,128)S(1)}, u32[]{:S(2)}, u32[]{:S(2)}) collective-permute-start(f32[10,1,64]{2,1,0:T(1,128)S(1)} %get-tuple-element.83), channel_id=1, source_target_pairs={{8,0},{16,8},{24,16},{32,24},{40,32},{48,40},{56,48},{9,1},{17,9},... | collective-permute-start | bytes 7688 | tf_op jit(solution)/shard_map/ppermute | solution.py:21
  153.0 32.6 %collective-permute-start.30 = (f32[10,1,64]{2,1,0:T(1,128)S(1)}, f32[10,1,64]{2,1,0:T(1,128)S(1)}, u32[]{:S(2)}, u32[]{:S(2)}) collective-permute-start(f32[10,1,64]{2,1,0:T(1,128)S(1)} %get-tuple-element.82), channel_id=1, source_target_pairs={{0,8},{8,16},{16,24},{24,32},{32,40},{40,48},{48,56},{1,9},{9,17},... | collective-permute-start | bytes 7688 | tf_op jit(solution)/shard_map/ppermute | solution.py:20
  155.7 9.1 %collective-permute-start.17 = (f32[18,34,1]{2,1,0:T(8,128)S(1)}, f32[18,34,1]{2,1,0:T(8,128)S(1)}, u32[]{:S(2)}, u32[]{:S(2)}) collective-permute-start(f32[18,34,1]{2,1,0:T(8,128)S(1)} %get-tuple-element.32), channel_id=1, source_target_pairs={{0,1},{1,2},{2,3},{3,4},{4,5},{5,6},{6,7},{8,9},{9,10},{10,11},{11... | collective-permute-start | bytes 7352 | tf_op jit(solution)/shard_map/ppermute | solution.py:20
  160.4 8.8 %collective-permute-start.16 = (f32[18,34,1]{2,1,0:T(8,128)S(1)}, f32[18,34,1]{2,1,0:T(8,128)S(1)}, u32[]{:S(2)}, u32[]{:S(2)}) collective-permute-start(f32[18,34,1]{2,1,0:T(8,128)S(1)} %get-tuple-element.31), channel_id=1, source_target_pairs={{1,0},{2,1},{3,2},{4,3},{5,4},{6,5},{7,6},{9,8},{10,9},{11,10},{12... | collective-permute-start | bytes 7352 | tf_op jit(solution)/shard_map/ppermute | solution.py:21
  175.4 57.5 %collective-permute-start.35 = (f32[10,18,1]{2,1,0:T(8,128)S(1)}, f32[10,18,1]{2,1,0:T(8,128)}, u32[]{:S(2)}, u32[]{:S(2)}) collective-permute-start(f32[10,18,1]{2,1,0:T(8,128)S(1)} %get-tuple-element.73), channel_id=1, source_target_pairs={{0,1},{1,2},{2,3},{3,4},{4,5},{5,6},{6,7},{8,9},{9,10},{10,11},{11... | collective-permute-start | bytes 2168 | tf_op jit(solution)/shard_map/ppermute | solution.py:20
  178.8 56.1 %collective-permute-start.33 = (f32[10,18,1]{2,1,0:T(8,128)S(1)}, f32[10,18,1]{2,1,0:T(8,128)}, u32[]{:S(2)}, u32[]{:S(2)}) collective-permute-start(f32[10,18,1]{2,1,0:T(8,128)S(1)} %get-tuple-element.72), channel_id=1, source_target_pairs={{1,0},{2,1},{3,2},{4,3},{5,4},{6,5},{7,6},{9,8},{10,9},{11,10},{12... | collective-permute-start | bytes 2168 | tf_op jit(solution)/shard_map/ppermute | solution.py:21
  191.6 9.4 %collective-permute-start.23 = (f32[18,34,1]{2,1,0:T(8,128)S(1)}, f32[18,34,1]{2,1,0:T(8,128)S(1)}, u32[]{:S(2)}, u32[]{:S(2)}) collective-permute-start(f32[18,34,1]{2,1,0:T(8,128)S(1)} %get-tuple-element.30), channel_id=1, source_target_pairs={{0,1},{1,2},{2,3},{3,4},{4,5},{5,6},{6,7},{8,9},{9,10},{10,11},{11... | collective-permute-start | bytes 7352 | tf_op jit(solution)/shard_map/ppermute | solution.py:20
  196.5 8.8 %collective-permute-start.22 = (f32[18,34,1]{2,1,0:T(8,128)S(1)}, f32[18,34,1]{2,1,0:T(8,128)S(1)}, u32[]{:S(2)}, u32[]{:S(2)}) collective-permute-start(f32[18,34,1]{2,1,0:T(8,128)S(1)} %get-tuple-element.29), channel_id=1, source_target_pairs={{1,0},{2,1},{3,2},{4,3},{5,4},{6,5},{7,6},{9,8},{10,9},{11,10},{12... | collective-permute-start | bytes 7352 | tf_op jit(solution)/shard_map/ppermute | solution.py:21
  201.0 36.4 %collective-permute-start.32 = (f32[10,18,1]{2,1,0:T(8,128)}, f32[10,18,1]{2,1,0:T(8,128)}, u32[]{:S(2)}, u32[]{:S(2)}) collective-permute-start(f32[10,18,1]{2,1,0:T(8,128)} %get-tuple-element.71), channel_id=1, source_target_pairs={{1,0},{2,1},{3,2},{4,3},{5,4},{6,5},{7,6},{9,8},{10,9},{11,10},{12... | collective-permute-start | bytes 2168 | tf_op jit(solution)/shard_map/ppermute | solution.py:21
  205.4 35.4 %collective-permute-start.34 = (f32[10,18,1]{2,1,0:T(8,128)}, f32[10,18,1]{2,1,0:T(8,128)S(1)}, u32[]{:S(2)}, u32[]{:S(2)}) collective-permute-start(f32[10,18,1]{2,1,0:T(8,128)} %get-tuple-element.70), channel_id=1, source_target_pairs={{0,1},{1,2},{2,3},{3,4},{4,5},{5,6},{6,7},{8,9},{9,10},{10,11},{11... | collective-permute-start | bytes 2168 | tf_op jit(solution)/shard_map/ppermute | solution.py:20
  233.0 31.1 %collective-permute-start.52 = (f32[6,1,32]{2,1,0:T(1,128)S(1)}, f32[6,1,32]{2,1,0:T(1,128)S(1)}, u32[]{:S(2)}, u32[]{:S(2)}) collective-permute-start(f32[6,1,32]{2,1,0:T(1,128)S(1)} %copy-done.50), channel_id=1, source_target_pairs={{8,0},{16,8},{24,16},{32,24},{40,32},{48,40},{56,48},{9,1},{17,9},... | collective-permute-start | bytes 2312 | tf_op jit(solution)/shard_map/ppermute | solution.py:21
  234.9 44.5 %collective-permute-start.57 = (f32[6,10,1]{2,0,1:T(8,128)S(1)}, f32[6,10,1]{2,0,1:T(8,128)S(1)}, u32[]{:S(2)}, u32[]{:S(2)}) collective-permute-start(f32[6,10,1]{2,0,1:T(8,128)S(1)} %copy-done.42), channel_id=1, source_target_pairs={{1,0},{2,1},{3,2},{4,3},{5,4},{6,5},{7,6},{9,8},{10,9},{11,10},{12... | collective-permute-start | bytes 728 | tf_op jit(solution)/shard_map/ppermute | solution.py:21
  237.3 45.5 %collective-permute-start.59 = (f32[6,10,1]{2,0,1:T(8,128)S(1)}, f32[6,10,1]{2,0,1:T(8,128)S(1)}, u32[]{:S(2)}, u32[]{:S(2)}) collective-permute-start(f32[6,10,1]{2,0,1:T(8,128)S(1)} %get-tuple-element.119), channel_id=1, source_target_pairs={{0,1},{1,2},{2,3},{3,4},{4,5},{5,6},{6,7},{8,9},{9,10},{10,11},{11... | collective-permute-start | bytes 728 | tf_op jit(solution)/shard_map/ppermute | solution.py:20
  273.2 18.4 %collective-permute-start.58 = (f32[6,10,1]{2,0,1:T(8,128)S(1)}, f32[6,10,1]{2,0,1:T(8,128)S(1)}, u32[]{:S(2)}, u32[]{:S(2)}) collective-permute-start(f32[6,10,1]{2,0,1:T(8,128)S(1)} %get-tuple-element.114), channel_id=1, source_target_pairs={{0,1},{1,2},{2,3},{3,4},{4,5},{5,6},{6,7},{8,9},{9,10},{10,11},{11... | collective-permute-start | bytes 728 | tf_op jit(solution)/shard_map/ppermute | solution.py:20
  275.2 16.3 %collective-permute-start.56 = (f32[6,10,1]{2,0,1:T(8,128)S(1)}, f32[6,10,1]{2,0,1:T(8,128)S(1)}, u32[]{:S(2)}, u32[]{:S(2)}) collective-permute-start(f32[6,10,1]{2,0,1:T(8,128)S(1)} %get-tuple-element.115), channel_id=1, source_target_pairs={{1,0},{2,1},{3,2},{4,3},{5,4},{6,5},{7,6},{9,8},{10,9},{11,10},{12... | collective-permute-start | bytes 728 | tf_op jit(solution)/shard_map/ppermute | solution.py:21
  299.3 66.5 %collective-permute-start.60 = (f32[1,8,32]{2,1,0:T(8,128)S(1)}, f32[1,8,32]{2,1,0:T(8,128)S(1)}, u32[]{:S(2)}, u32[]{:S(2)}) collective-permute-start(f32[1,8,32]{2,1,0:T(8,128)S(1)} %get-tuple-element.139), channel_id=1, source_target_pairs={{64,0},{128,64},{192,128},{65,1},{129,65},{193,129},{66,2},{130,66... | collective-permute-start | bytes 3080 | tf_op jit(solution)/shard_map/ppermute | solution.py:21
  303.6 62.2 %collective-permute-start.61 = (f32[1,8,32]{2,1,0:T(8,128)S(1)}, f32[1,8,32]{2,1,0:T(8,128)S(1)}, u32[]{:S(2)}, u32[]{:S(2)}) collective-permute-start(f32[1,8,32]{2,1,0:T(8,128)S(1)} %get-tuple-element.138), channel_id=1, source_target_pairs={{0,64},{64,128},{128,192},{1,65},{65,129},{129,193},{2,66},{66,130... | collective-permute-start | bytes 3080 | tf_op jit(solution)/shard_map/ppermute | solution.py:20
  365.8 66.6 %collective-permute-start.63 = (f32[6,1,32]{2,1,0:T(1,128)S(1)}, f32[6,1,32]{2,1,0:T(1,128)S(1)}, u32[]{:S(2)}, u32[]{:S(2)}) collective-permute-start(f32[6,1,32]{2,1,0:T(1,128)S(1)} %get-tuple-element.127), channel_id=1, source_target_pairs={{0,8},{8,16},{16,24},{24,32},{32,40},{40,48},{48,56},{1,9},{9,17},... | collective-permute-start | bytes 2312 | tf_op jit(solution)/shard_map/ppermute | solution.py:20
  456.3 8.7 %collective-permute-start.70 = (f32[6,10,1]{2,0,1:T(8,128)S(1)}, f32[6,10,1]{2,0,1:T(8,128)S(1)}, u32[]{:S(2)}, u32[]{:S(2)}) collective-permute-start(f32[6,10,1]{2,0,1:T(8,128)S(1)} %get-tuple-element.106), channel_id=1, source_target_pairs={{1,0},{2,1},{3,2},{4,3},{5,4},{6,5},{7,6},{9,8},{10,9},{11,10},{12... | collective-permute-start | bytes 728 | tf_op jit(solution)/shard_map/ppermute | solution.py:21
  567.9 7.1 %collective-permute-start.81 = (f32[6,1,32]{2,1,0:T(1,128)S(1)}, f32[6,1,32]{2,1,0:T(1,128)S(1)}, u32[]{:S(2)}, u32[]{:S(2)}) collective-permute-start(f32[6,1,32]{2,1,0:T(1,128)S(1)} %get-tuple-element.121), channel_id=1, source_target_pairs={{0,8},{8,16},{16,24},{24,32},{32,40},{40,48},{48,56},{1,9},{9,17},... | collective-permute-start | bytes 2312 | tf_op jit(solution)/shard_map/ppermute | solution.py:20
  575.8 8.3 %collective-permute-start.82 = (f32[6,10,1]{2,0,1:T(8,128)S(1)}, f32[6,10,1]{2,0,1:T(8,128)S(1)}, u32[]{:S(2)}, u32[]{:S(2)}) collective-permute-start(f32[6,10,1]{2,0,1:T(8,128)S(1)} %get-tuple-element.98), channel_id=1, source_target_pairs={{1,0},{2,1},{3,2},{4,3},{5,4},{6,5},{7,6},{9,8},{10,9},{11,10},{12... | collective-permute-start | bytes 728 | tf_op jit(solution)/shard_map/ppermute | solution.py:21
  594.1 7.1 %collective-permute-start.86 = (f32[10,1,64]{2,1,0:T(1,128)S(1)}, f32[10,1,64]{2,1,0:T(1,128)S(1)}, u32[]{:S(2)}, u32[]{:S(2)}) collective-permute-start(f32[10,1,64]{2,1,0:T(1,128)S(1)} %get-tuple-element.77), channel_id=1, source_target_pairs={{8,0},{16,8},{24,16},{32,24},{40,32},{48,40},{56,48},{9,1},{17,9},... | collective-permute-start | bytes 7688 | tf_op jit(solution)/shard_map/ppermute | solution.py:21
  604.9 9.0 %collective-permute-start.89 = (f32[10,18,1]{2,1,0:T(8,128)S(1)}, f32[10,18,1]{2,1,0:T(8,128)S(1)}, u32[]{:S(2)}, u32[]{:S(2)}) collective-permute-start(f32[10,18,1]{2,1,0:T(8,128)S(1)} %get-tuple-element.65), channel_id=1, source_target_pairs={{0,1},{1,2},{2,3},{3,4},{4,5},{5,6},{6,7},{8,9},{9,10},{10,11},{11... | collective-permute-start | bytes 2168 | tf_op jit(solution)/shard_map/ppermute | solution.py:20
  661.4 8.8 %collective-permute-start.101 = (f32[18,34,1]{2,1,0:T(8,128)S(1)}, f32[18,34,1]{2,1,0:T(8,128)S(1)}, u32[]{:S(2)}, u32[]{:S(2)}) collective-permute-start(f32[18,34,1]{2,1,0:T(8,128)S(1)} %get-tuple-element.28), channel_id=1, source_target_pairs={{0,1},{1,2},{2,3},{3,4},{4,5},{5,6},{6,7},{8,9},{9,10},{10,11},{11... | collective-permute-start | bytes 7352 | tf_op jit(solution)/shard_map/ppermute | solution.py:20
  665.7 8.8 %collective-permute-start.100 = (f32[18,34,1]{2,1,0:T(8,128)S(1)}, f32[18,34,1]{2,1,0:T(8,128)S(1)}, u32[]{:S(2)}, u32[]{:S(2)}) collective-permute-start(f32[18,34,1]{2,1,0:T(8,128)S(1)} %get-tuple-element.27), channel_id=1, source_target_pairs={{1,0},{2,1},{3,2},{4,3},{5,4},{6,5},{7,6},{9,8},{10,9},{11,10},{12... | collective-permute-start | bytes 7352 | tf_op jit(solution)/shard_map/ppermute | solution.py:21
  690.0 8.8 %collective-permute-start.107 = (f32[18,34,1]{2,1,0:T(8,128)S(1)}, f32[18,34,1]{2,1,0:T(8,128)S(1)}, u32[]{:S(2)}, u32[]{:S(2)}) collective-permute-start(f32[18,34,1]{2,1,0:T(8,128)S(1)} %get-tuple-element.26), channel_id=1, source_target_pairs={{0,1},{1,2},{2,3},{3,4},{4,5},{5,6},{6,7},{8,9},{9,10},{10,11},{11... | collective-permute-start | bytes 7352 | tf_op jit(solution)/shard_map/ppermute | solution.py:20
  694.3 8.8 %collective-permute-start.106 = (f32[18,34,1]{2,1,0:T(8,128)S(1)}, f32[18,34,1]{2,1,0:T(8,128)S(1)}, u32[]{:S(2)}, u32[]{:S(2)}) collective-permute-start(f32[18,34,1]{2,1,0:T(8,128)S(1)} %get-tuple-element.25), channel_id=1, source_target_pairs={{1,0},{2,1},{3,2},{4,3},{5,4},{6,5},{7,6},{9,8},{10,9},{11,10},{12... | collective-permute-start | bytes 7352 | tf_op jit(solution)/shard_map/ppermute | solution.py:21
  (111 other events, 5764.0 us)
where the time goes:
time: 718 us; the launch traced here: 705 us
  starting transfers between devices  300 us (42%)
  blocking collectives  186 us (26%)
  waiting for transfers between devices  99 us (14%)
  local copies, waits for them, and re-layouts  75.3 us (10%)
  other arithmetic  41.9 us (6%)
    ppermute x54, starting transfers between devices, extended(): after = lax.ppermute(first, axis, down)  160 us
    ppermute x54, starting transfers between devices, extended(): before = lax.ppermute(last, axis, up)  140 us
    all_gather x1, blocking collectives, per_device(): lax.all_gather(sources[3][None], ('gx', 'gy', 'gz'), axis=0, tiled=True)  63.3 us
    all_gather x1, blocking collectives, per_device(): lax.all_gather(conducts[3][None], ('gx', 'gy', 'gz'), axis=0, tiled=True)  61.4 us
    all_gather x1, blocking collectives, per_device(): lax.all_gather(masses[3][None], ('gx', 'gy', 'gz'), axis=0, tiled=True)  60.9 us
    ppermute x54, waiting for transfers between devices, extended(): before = lax.ppermute(last, axis, up)  60.4 us
    reshape x5, local copies, waits for them, and re-layouts, coarsen(): field.reshape(field.shape[0] // 2, 2, field.shape[1] // 2, 2, field.shape...  58.1 us
    ppermute x54, waiting for transfers between devices, extended(): after = lax.ppermute(first, axis, down)  38.6 us
  transfers between devices with their start and end apart: 108, of which 39 were waited for; matrix products, arithmetic and copies ran while one was open for 13% of the time, Pallas kernels for 0%

commit v1 on v0

v1 whole, which is shorter than its diff:
```python
import functools

import jax
import jax.numpy as jnp
from jax import lax
from jax.experimental import pallas as pl
from jax.experimental.pallas import tpu as pltpu
from jax.sharding import PartitionSpec as P

SWEEPS = 2
COARSE_SWEEPS = 8
OMEGA = 2.0 / 3.0
KEEP = 1.0 - OMEGA
OUTSIDE = 1e30
LIMIT = 1e29
F32 = jnp.float32
HIGH = lax.Precision.HIGHEST


def dot(a, b):
    return jnp.dot(a, b, precision=HIGH, preferred_element_type=F32)


def iota(shape, dim):
    return lax.broadcasted_iota(jnp.int32, shape, dim)


def roll(x, shift, axis):
    size = x.shape[axis]
    shift = shift % size
    return x if shift == 0 else pltpu.roll(x, shift, axis)


def after(x, axis):
    return roll(x, -1, axis)


def before(x, axis):
    return roll(x, 1, axis)


def planes(low, high, body, unroll=2):
    def step(p, carry):
        body(p)
        return carry

    lax.fori_loop(low, high, step, 0, unroll=unroll)


def coefficients(low, high, spacing, k, f, m, d, w, g, cy, cz):
    half = 0.5 * spacing

    def body(p):
        here = k[p]
        y = half * (here + after(here, 0))
        z = half * (here + after(here, 1))
        diagonal = m[p] + half * (k[p - 1] + here) + half * (here + k[p + 1])
        diagonal = diagonal + y + before(y, 0) + z + before(z, 1)
        weight = jnp.where(m[p] < LIMIT, OMEGA / diagonal, 0.0)
        if d is not None:
            d[p] = diagonal
        w[p] = weight
        g[p] = weight * f[p]
        cy[p] = y
        cz[p] = z

    planes(low, high, body)


def neighbours(p, half, k, cy, cz, v):
    here, centre, y, z = k[p], v[p], cy[p], cz[p]
    total = half * (k[p - 1] + here) * v[p - 1] + half * (here + k[p + 1]) * v[p + 1]
    total = total + y * after(centre, 0) + before(y * centre, 0)
    total = total + z * after(centre, 1) + before(z * centre, 1)
    return total, centre


def sweep(low, high, spacing, k, w, g, cy, cz, v, out):
    half = 0.5 * spacing

    def body(p):
        total, centre = neighbours(p, half, k, cy, cz, v)
        out[p] = KEEP * centre + g[p] + w[p] * total

    planes(low, high, body)


def pack_y_kernel(f, k, m, xl, xr, up, down):
    for p in range(24):
        for out, lo3, lo4 in ((up, 29, 28), (down, 0, 0)):
            base = 10 * p
            if p < 4:
                kk = xl[6 + p, lo4 : lo4 + 4]
            elif p < 20:
                kk = k[p - 4, lo4 : lo4 + 4]
            else:
                kk = xr[6 + p - 20, lo4 : lo4 + 4]
            if 1 <= p < 4:
                ff, mm = xl[p - 1, lo3 : lo3 + 3], xl[2 + p, lo3 : lo3 + 3]
            elif 4 <= p < 20:
                ff, mm = f[p - 4, lo3 : lo3 + 3], m[p - 4, lo3 : lo3 + 3]
            elif 20 <= p < 23:
                ff, mm = xr[p - 20, lo3 : lo3 + 3], xr[p - 17, lo3 : lo3 + 3]
            else:
                ff = mm = jnp.zeros((3, 128), F32)
            out[base : base + 3] = ff
            out[base + 3 : base + 6] = mm
            out[base + 6 : base + 10] = kk


def pack_z_kernel(f, k, m, xl, xr, yl, yr, fa, ka, ma, up, down):
    lane = iota((40, 128), 1)
    zero = jnp.zeros((32, 128), F32)
    for g in range(2):
        acc_up = jnp.zeros((40, 128), F32)
        acc_down = jnp.zeros((40, 128), F32)
        for i in range(12):
            p = 12 * g + i
            base = 10 * p
            if p < 4:
                own = (xl[p - 1] if p else zero, xl[2 + p] if p else zero, xl[6 + p])
            elif p < 20:
                own = (f[p - 4], m[p - 4], k[p - 4])
            else:
                own = (xr[p - 20] if p < 23 else zero, xr[p - 17] if p < 23 else zero, xr[p - 14])
            for a, out in enumerate((fa, ma, ka)):
                width = 4 if a == 2 else 3
                out[p, 0:32] = own[a]
                out[p, 32:40] = jnp.zeros((8, 128), F32)
                out[p, 32 : 32 + width] = yr[base + 3 * a : base + 3 * a + width]
                out[p, 40 - width : 40] = yl[base + 3 * a : base + 3 * a + width]
                whole = out[p]
                first = 10 * i + 3 * a
                mask = (lane >= first) & (lane < first + width)
                acc_up = jnp.where(mask, roll(whole, first - (128 - width), 1), acc_up)
                acc_down = jnp.where(mask, roll(whole, first, 1), acc_down)
        up[g] = acc_up
        down[g] = acc_down


def pair_matrix(columns):
    return jnp.where(iota((128, columns), 0) // 2 == iota((128, columns), 1) % 64, 0.125, 0.0)


def fine_kernel(
    pos, fa, ka, ma, zl, zr, message, v_out, w, g, k, cy, cz, f, m, d, tall
):
    ix, iy, iz = pos[0], pos[1], pos[2]
    row = iota((40, 128), 0)
    lane = iota((40, 128), 1)
    far = ((row >= 32) & (row < 36) & (iy == 7)) | ((row >= 36) & (iy == 0))
    beside = ((lane < 4) & (iz < 7)) | ((lane >= 124) & (iz > 0))
    row_inner = (row < 35) | (row > 36)
    inner = (lane < 3) | (lane > 124)
    for p in range(24):
        group, i = p // 12, p % 12
        absent = False
        if p < 4:
            absent = ix == 0
        elif p >= 20:
            absent = ix == 3
        gone = far | absent
        for a, (src, out) in enumerate(((fa, f), (ma, m), (ka, k))):
            width = 4 if a == 2 else 3
            first = 10 * i + 3 * a
            right = roll(zr[group], -first, 1)
            left = roll(zl[group], 128 - width - first, 1)
            side = jnp.where(lane < 64, right, left)
            fill = OUTSIDE if a == 1 else 0.0
            if a == 1 and p in (0, 23):
                out[p] = jnp.full((40, 256), OUTSIDE, F32)
                continue
            if a == 2:
                here, there = gone, gone | ~beside
            else:
                here = gone | ~row_inner
                there = here | ~(beside & inner)
            out[p, :, 0:128] = jnp.where(here, fill, src[p])
            out[p, :, 128:256] = jnp.where(there, fill, side)
    coefficients(1, 23, 1.0, k, f, m, d, w, g, cy, cz)
    sweep(2, 22, 1.0, k, w, g, cy, cz, g, v_out)
    pairs = pair_matrix(128)
    lane16 = iota((16, 128), 1)

    def emit(slot, rows_of):
        for i in range(8):
            tall[32 * i : 32 * i + 32] = rows_of(2 * i + 4) + rows_of(2 * i + 5)
        halves = tall[pl.ds(0, 128, stride=2), :] + tall[pl.ds(1, 128, stride=2), :]
        coarse = dot(halves, pairs)
        for i in range(4):
            message[4 * slot + i] = jnp.where(
                lane16 < 64, coarse[16 * i : 16 * i + 16], coarse[16 * i + 64 : 16 * i + 80]
            )

    def residual(p):
        total, centre = neighbours(p, 0.5, k, cy, cz, v_out)
        return (f[p] + total - d[p] * centre)[0:32, 0:128]

    emit(0, residual)
    emit(1, lambda p: m[p, 0:32, 0:128])
    emit(2, lambda p: k[p, 0:32, 0:128])


def pack_z1_kernel(own, yl, yr, up, down):
    lane = iota((16, 128), 1) % 64
    for b in range(4):
        for a in range(3):
            for part, src in enumerate((own, yr, yl)):
                acc_up = jnp.zeros((16, 128), F32)
                acc_down = jnp.zeros((16, 128), F32)
                for q in range(4):
                    pair = src[12 * b + 4 * a + q]
                    mask = (lane >= 16 * q) & (lane < 16 * q + 16)
                    acc_up = jnp.where(mask, roll(pair, 16 * q - 48, 1), acc_up)
                    acc_down = jnp.where(mask, roll(pair, 16 * q, 1), acc_down)
                up[3 * b + a, 16 * part : 16 * part + 16] = acc_up
                down[3 * b + a, 16 * part : 16 * part + 16] = acc_down


def middle_kernel(
    pos, own, yl, yr, zl, zr,
    message, v1, w1, g1, k1, cy1, cz1, v2, w2, g2, k2, cy2, cz2,
    f1, m1, d1, f2, m2, d2, tall, small,
):
    ix, iy, iz = pos[0], pos[1], pos[2]
    row = iota((48, 128), 0)
    lane = iota((48, 128), 1)
    gone = ((row >= 16) & (row < 32) & (iy == 7)) | ((row >= 32) & (iy == 0))
    gone = gone | ((lane >= 64) & (lane < 80) & (iz == 7)) | ((lane >= 112) & (iz == 0))
    gone = gone | ((lane >= 80) & (lane < 112))
    for ref in (k1, g1, v1, k2, g2, v2):
        ref[0] = jnp.zeros(ref.shape[1:], F32)
        ref[ref.shape[0] - 1] = jnp.zeros(ref.shape[1:], F32)
    for b in range(4):
        block = 8 * jnp.bitwise_xor(ix, b) + 1
        for a, (out, fill) in enumerate(((f1, 0.0), (m1, OUTSIDE), (k1, 0.0))):
            left, right = zl[3 * b + a], zr[3 * b + a]
            for q in range(4):
                s = 12 * b + 4 * a + q
                pair = jnp.concatenate([own[s], yr[s], yl[s]], axis=0)
                for h in range(2):
                    at = 16 * (q + 4 * h)
                    side = jnp.where(lane < 96, roll(right, 64 - at, 1), roll(left, 112 - at, 1))
                    value = jnp.where(lane < 64, roll(pair, 64 * h, 1), side)
                    out[block + q + 4 * h] = jnp.where(gone, fill, value)
    coefficients(1, 33, 0.25, k1, f1, m1, d1, w1, g1, cy1, cz1)
    sweep(1, 33, 0.25, k1, w1, g1, cy1, cz1, g1, v1)

    column = iota((128, 128), 1)
    known = (column < 40) | (column >= 120)
    pairs = jnp.where(known, pair_matrix(128), 0.0)
    lane24 = iota((24, 128), 1)
    unknown = (lane24 >= 40) & (lane24 < 120)

    def to_second(out, value_of, fill):
        for i in range(16):
            tall[48 * i : 48 * i + 48] = value_of(2 * i + 1) + value_of(2 * i + 2)
        halves = tall[pl.ds(0, 384, stride=2), :] + tall[pl.ds(1, 384, stride=2), :]
        coarse = dot(halves, pairs)
        for i in range(16):
            out[i + 1] = jnp.where(unknown, fill, coarse[24 * i : 24 * i + 24])

    def residual1(p):
        total, centre = neighbours(p, 0.125, k1, cy1, cz1, v1)
        return jnp.where(gone, 0.0, f1[p] + total - d1[p] * centre)

    to_second(f2, residual1, 0.0)
    to_second(m2, lambda p: m1[p], OUTSIDE)
    to_second(k2, lambda p: k1[p], 0.0)
    coefficients(1, 17, 0.0625, k2, f2, m2, d2, w2, g2, cy2, cz2)
    sweep(1, 17, 0.0625, k2, w2, g2, cy2, cz2, g2, v2)

    spread = jnp.where(iota((128, 128), 0) // 2 == column % 16, 0.125, 0.0)
    group = iota((12, 128), 1) // 16

    def to_third(slot, value_of):
        for i in range(8):
            tall[24 * i : 24 * i + 24] = value_of(2 * i + 1) + value_of(2 * i + 2)
        halves = tall[pl.ds(0, 96, stride=2), :] + tall[pl.ds(1, 96, stride=2), :]
        small[0:96] = dot(halves, spread)
        packed = jnp.zeros((12, 128), F32)
        for i in range(8):
            packed = jnp.where(group == i, small[12 * i : 12 * i + 12], packed)
        small[0:12] = packed
        message[slot, 0:2] = small[10:12]
        message[slot, 2:8] = small[0:6]

    row24 = iota((24, 128), 0)
    gone2 = ((row24 >= 8) & (row24 < 16) & (iy == 7)) | ((row24 >= 16) & (iy == 0))

    def residual2(p):
        total, centre = neighbours(p, 0.03125, k2, cy2, cz2, v2)
        return jnp.where(gone2, 0.0, f2[p] + total - d2[p] * centre)

    to_third(0, residual2)
    to_third(1, lambda p: m2[p])
    to_third(2, lambda p: k2[p])


def last_kernel(
    pos, own, first, second, v0, w0, g0, k0, cy0, cz0, v1, w1, g1, k1, cy1, cz1, v2, w2, g2, k2, cy2, cz2,
    out,
    k3, f3, m3, w3, g3, cy3, cz3, a3, b3, rows, dup, a2, b2, a1, b1, wide, low, high, a0, b0,
):
    ix, iy, iz = pos[0], pos[1], pos[2]
    row = iota((24, 128), 0) + 4 * iy - 10
    lane = iota((24, 128), 1)
    gone = (row < 0) | (row >= 32) | ((lane >= 32) & (lane < 112))
    gone = gone | ((lane >= 16) & (lane < 32) & (iz == 7)) | ((lane >= 112) & (iz == 0))
    for ref in (k3, g3, a3, b3, a2, b2, a1, b1):
        ref[0] = jnp.zeros(ref.shape[1:], F32)
        ref[ref.shape[0] - 1] = jnp.zeros(ref.shape[1:], F32)
    crossed = (iy == 2) | (iy == 6)

    def stack(index):
        one, two = first[index], second[index]
        ahead, behind = jnp.where(crossed, two, one), jnp.where(crossed, one, two)
        ahead = jnp.where(iy == 1, roll(ahead, 4, 0), ahead)
        behind = jnp.where(iy == 6, roll(behind, 4, 0), behind)
        return jnp.concatenate([ahead, own[index], behind], axis=0)

    for a, (ref, fill) in enumerate(((f3, 0.0), (m3, OUTSIDE), (k3, 0.0))):
        here, left, right = (stack(3 * z + a) for z in range(3))
        for x in range(8):
            value = jnp.where(
                lane < 16,
                roll(here, -16 * x, 1),
                jnp.where(lane < 64, roll(right, 16 - 16 * x, 1), roll(left, 112 - 16 * x, 1)),
            )
            ref[x + 1] = jnp.where(gone, fill, value)
    spacing = 0.25**3
    coefficients(1, 9, spacing, k3, f3, m3, None, w3, g3, cy3, cz3)
    source = g3
    for index in range(COARSE_SWEEPS - 1):
        target = (a3, b3)[index % 2]
        sweep(1, 9, spacing, k3, w3, g3, cy3, cz3, source, target)
        source = target

    src, column = iota((128, 128), 0), iota((128, 128), 1)
    to2 = jnp.where(
        ((column < 40) & (src == column // 2)) | ((column >= 120) & (src == 64 + column // 2)), 1.0, 0.0
    )
    for x in range(8):
        rows[24 * x : 24 * x + 24] = source[x + 1]
    rows[0:192] = dot(rows[0:192], to2)
    for x in range(8):
        dup[0:24] = jnp.zeros((24, 128), F32)
        mid = rows[24 * x + 10 : 24 * x + 16]
        dup[pl.ds(0, 6, stride=2), :] = mid
        dup[pl.ds(1, 6, stride=2), :] = mid
        ahead = rows[24 * x + 8 : 24 * x + 10]
        dup[pl.ds(20, 2, stride=2), :] = ahead
        dup[pl.ds(21, 2, stride=2), :] = ahead
        both = dup[0:24]
        a2[2 * x + 1] = v2[2 * x + 1] + both
        a2[2 * x + 2] = v2[2 * x + 2] + both
    sweep(1, 17, 0.0625, k2, w2, g2, cy2, cz2, a2, b2)
    sweep(1, 17, 0.0625, k2, w2, g2, cy2, cz2, b2, a2)

    to1 = jnp.where(
        ((column < 80) & (src == column // 2)) | ((column >= 112) & (src == 64 + column // 2)), 1.0, 0.0
    )
    for x in range(16):
        rows[24 * x : 24 * x + 24] = a2[x + 1]
    fine = dot(rows[0:384], to1)
    dup[pl.ds(0, 384, stride=2), :] = fine
    dup[pl.ds(1, 384, stride=2), :] = fine
    for x in range(16):
        both = dup[48 * x : 48 * x + 48]
        a1[2 * x + 1] = v1[2 * x + 1] + both
        a1[2 * x + 2] = v1[2 * x + 2] + both
    sweep(1, 33, 0.25, k1, w1, g1, cy1, cz1, a1, b1)
    sweep(1, 33, 0.25, k1, w1, g1, cy1, cz1, b1, a1)

    to0 = jnp.where(iota((128, 256), 0) == iota((128, 256), 1) // 2, 1.0, 0.0)
    for x in range(10):
        rows[48 * x : 48 * x + 48] = a1[8 * ix + x]
    wide[...] = dot(rows[0:480], to0)
    for x in range(10):
        for half, lanes in ((low, slice(0, 128)), (high, slice(128, 256))):
            mid = wide[48 * x : 48 * x + 18, lanes]
            half[pl.ds(0, 18, stride=2), :] = mid
            half[pl.ds(1, 18, stride=2), :] = mid
            ahead = wide[48 * x + 46 : 48 * x + 48, lanes]
            half[pl.ds(36, 2, stride=2), :] = ahead
            half[pl.ds(37, 2, stride=2), :] = ahead
            for p in (2 * x + 2, 2 * x + 3):
                a0[p, :, lanes] = v0[p, :, lanes] + half[...]
    sweep(3, 21, 1.0, k0, w0, g0, cy0, cz0, a0, b0)

    def body(p):
        total, centre = neighbours(p, 0.5, k0, cy0, cz0, b0)
        value = KEEP * centre + g0[p] + w0[p] * total
        out[p - 4] = value[0:32, 0:128]

    planes(4, 20, body)


VMEM = pl.BlockSpec(memory_space=pltpu.VMEM)
SMEM = pl.BlockSpec(memory_space=pltpu.SMEM)


COARSE_TARGETS = ((1, 3, 4, 5, 2, 7, 0, 6), (2, 7, 0, 1, 6, 3, 4, 5))


def call(kernel, outs, scratch, *args, pos=None):
    specs = [VMEM] * len(args)
    if pos is not None:
        args = (pos,) + args
        specs = [SMEM] + specs
    return pl.pallas_call(
        kernel,
        out_shape=[jax.ShapeDtypeStruct(s, F32) for s in outs],
        in_specs=specs,
        out_specs=[VMEM] * len(outs),
        scratch_shapes=[pltpu.VMEM(s, F32) for s in scratch],
        compiler_params=pltpu.CompilerParams(vmem_limit_bytes=48 * 1024 * 1024),
        name=kernel.__name__,
    )(*args)


def shift(x, axis, step):
    size = lax.axis_size(axis)
    return lax.ppermute(x, axis, [(i, (i + step) % size) for i in range(size)])


def swap(x, axis, bits):
    size = lax.axis_size(axis)
    return lax.ppermute(x, axis, [(i, i ^ bits) for i in range(size)])


def per_device(f, k, m):
    pos = jnp.stack([lax.axis_index("gx"), lax.axis_index("gy"), lax.axis_index("gz")])
    pos = pos.astype(jnp.int32)
    xl = shift(jnp.concatenate([f[13:], m[13:], k[12:]]), "gx", 1)
    xr = shift(jnp.concatenate([f[:3], m[:3], k[:4]]), "gx", -1)
    up, down = call(pack_y_kernel, [(240, 128)] * 2, [], f, k, m, xl, xr)
    yl, yr = shift(up, "gy", 1), shift(down, "gy", -1)
    fa, ka, ma, up, down = call(
        pack_z_kernel, [(24, 40, 128)] * 3 + [(2, 40, 128)] * 2, [], f, k, m, xl, xr, yl, yr
    )
    zl, zr = shift(up, "gz", 1), shift(down, "gz", -1)
    full = (24, 40, 256)
    message, *level0 = call(
        fine_kernel,
        [(12, 16, 128)] + [full] * 6,
        [full] * 3 + [(256, 128)],
        fa, ka, ma, zl, zr,
        pos=pos,
    )
    own = jnp.concatenate([message] + [swap(message, "gx", bits) for bits in (1, 2, 3)])
    yl, yr = shift(own, "gy", 1), shift(own, "gy", -1)
    up, down = call(pack_z1_kernel, [(12, 48, 128)] * 2, [], own, yl, yr)
    zl, zr = shift(up, "gz", 1), shift(down, "gz", -1)
    one, two = (34, 48, 128), (18, 24, 128)
    message, *rest = call(
        middle_kernel,
        [(3, 8, 128)] + [one] * 6 + [two] * 6,
        [one] * 3 + [two] * 3 + [(768, 128), (96, 128)],
        own, yl, yr, zl, zr,
        pos=pos,
    )
    level1, level2 = rest[:6], rest[6:]
    own = jnp.concatenate([message, shift(message, "gz", 1), shift(message, "gz", -1)])
    first, second = (lax.ppermute(own, "gy", list(enumerate(t))) for t in COARSE_TARGETS)
    three = (10, 24, 128)
    return call(
        last_kernel,
        [(16, 32, 128)],
        [three] * 9 + [(480, 128), (768, 128)] + [two] * 2 + [one] * 2
        + [(480, 256), (40, 128), (40, 128)] + [full] * 2,
        own, first, second, *level0, *level1, *level2,
        pos=pos,
    )[0]


def solution(mesh):
    placed = (P("gx", "gy", "gz"), P("gx", "gy", "gz"), P("gx", "gy", "gz"))
    return jax.shard_map(
        per_device, mesh=mesh, in_specs=placed, out_specs=P("gx", "gy", "gz"), check_vma=False
    )
```

time: 718 us -> 107 us (0.15)
  the two profiles are of different devices: /device:TPU:153 before, /device:TPU:64 now
where the time goes in v1:
time: 107 us; the launch traced here: 105 us
  waiting for transfers between devices  37.4 us (35%)
  Pallas kernels  33.6 us (31%)
  starting transfers between devices  27.6 us (26%)
  local copies, waits for them, and re-layouts  6.14 us (6%)
    pallas_call x6, Pallas kernels, call(): pl.pallas_call(kernel, out_shape=[jax.ShapeDtypeStruct(s, F32) for s in o...  33.6 us
    ppermute x12, waiting for transfers between devices, shift(): return lax.ppermute(x, axis, [(i, (i + step) % size) for i in range(size)])  27.6 us
    ppermute x12, starting transfers between devices, shift(): return lax.ppermute(x, axis, [(i, (i + step) % size) for i in range(size)])  18 us
    ppermute x3, waiting for transfers between devices, swap(): return lax.ppermute(x, axis, [(i, i ^ bits) for i in range(size)])  5.99 us
    ppermute x2, starting transfers between devices, per_device(): lax.ppermute(own, 'gy', list(enumerate(t)))  5.48 us
    unnamed x23, local copies, waits for them, and re-layouts  4.37 us
    ppermute x3, starting transfers between devices, swap(): return lax.ppermute(x, axis, [(i, i ^ bits) for i in range(size)])  4.12 us
    ppermute x2, waiting for transfers between devices, per_device(): lax.ppermute(own, 'gy', list(enumerate(t)))  3.84 us
  transfers between devices with their start and end apart: 17, of which 11 were waited for; matrix products, arithmetic and copies ran while one was open for 0% of the time, Pallas kernels for 0%

profile of v1, /device:TPU:64, one launch (start us, length us, event | category | flops | bytes accessed | tf_op | source)
XLA Modules:
  0.0 105.1 jit_solution(5631012061773485083)
XLA Ops:
  0.0 0.9 fusion.2
  0.9 0.1 copy-done.1
  1.0 0.8 fusion
  1.9 0.0 copy-start
  1.9 0.0 copy-start.2
  1.9 1.7 %collective-permute-start = (f32[10,32,128]{2,1,0:T(8,128)S(1)}, f32[10,32,128]{2,1,0:T(8,128)S(1)}, u32[]{:S(2)}, u32[]{:S(2)}) collective-permute-start(f32[10,32,128]{2,1,0:T(8,128)S(1)} %pad_maximum_fusion), channel_id=1, source_target_pairs={{0,64},{64,128},{128,192},{192,0},{1,65},{65,129},{129,193},{193,1... | collective-permute-start | bytes 491528 | tf_op jit(solution)/shard_map/ppermute | solution.py:424
  3.6 1.7 %collective-permute-start.1 = (f32[10,32,128]{2,1,0:T(8,128)S(1)}, f32[10,32,128]{2,1,0:T(8,128)S(1)}, u32[]{:S(2)}, u32[]{:S(2)}) collective-permute-start(f32[10,32,128]{2,1,0:T(8,128)S(1)} %pad_maximum_fusion.1), channel_id=1, source_target_pairs={{0,192},{64,0},{128,64},{192,128},{1,193},{65,1},{129,65},{193,129... | collective-permute-start | bytes 491528 | tf_op jit(solution)/shard_map/ppermute | solution.py:424
  5.3 3.9 %collective-permute-done.xl = f32[10,32,128]{2,1,0:T(8,128)S(1)} collective-permute-done((f32[10,32,128]{2,1,0:T(8,128)S(1)}, f32[10,32,128]{2,1,0:T(8,128)S(1)}, u32[]{:S(2)}, u32[]{:S(2)}) %collective-permute-start) | collective-permute-done | bytes 163872 | tf_op jit(solution)/shard_map/ppermute | solution.py:424
  9.2 0.1 collective-permute-done.1.xr
  9.3 0.1 pack_y_kernel.1
  9.4 2.0 %collective-permute-start.2 = (f32[240,128]{1,0:T(8,128)S(1)}, f32[240,128]{1,0:T(8,128)S(1)}, u32[]{:S(2)}, u32[]{:S(2)}) collective-permute-start(f32[240,128]{1,0:T(8,128)S(1)} %get-tuple-element.34), channel_id=1, source_target_pairs={{0,8},{8,16},{16,24},{24,32},{32,40},{40,48},{48,56},{56,0},{1,9},... | collective-permute-start | bytes 368648 | tf_op jit(solution)/shard_map/ppermute | solution.py:424
  11.4 0.1 collective-permute-start.3
  11.5 2.9 %collective-permute-done.2.yl = f32[240,128]{1,0:T(8,128)S(1)} collective-permute-done((f32[240,128]{1,0:T(8,128)S(1)}, f32[240,128]{1,0:T(8,128)S(1)}, u32[]{:S(2)}, u32[]{:S(2)}) %collective-permute-start.2) | collective-permute-done | bytes 122912 | tf_op jit(solution)/shard_map/ppermute | solution.py:424
  14.3 3.0 %collective-permute-done.3.yr = f32[240,128]{1,0:T(8,128)S(1)} collective-permute-done((f32[240,128]{1,0:T(8,128)S(1)}, f32[240,128]{1,0:T(8,128)S(1)}, u32[]{:S(2)}, u32[]{:S(2)}) %collective-permute-start.3) | collective-permute-done | bytes 122912 | tf_op jit(solution)/shard_map/ppermute | solution.py:424
  17.3 0.9 pack_z_kernel.1
  18.2 0.0 collective-permute-start.4
  18.2 2.9 %collective-permute-start.5 = (f32[2,40,128]{2,1,0:T(8,128)S(1)}, f32[2,40,128]{2,1,0:T(8,128)S(1)}, u32[]{:S(2)}, u32[]{:S(2)}) collective-permute-start(f32[2,40,128]{2,1,0:T(8,128)S(1)} %get-tuple-element.40), channel_id=1, source_target_pairs={{0,7},{1,0},{2,1},{3,2},{4,3},{5,4},{6,5},{7,6},{8,15},{9,8},{10,9... | collective-permute-start | bytes 122888 | tf_op jit(solution)/shard_map/ppermute | solution.py:424
  21.2 0.1 pad_add_fusion.pos
  21.3 1.6 %collective-permute-done.4.zl = f32[2,40,128]{2,1,0:T(8,128)S(1)} collective-permute-done((f32[2,40,128]{2,1,0:T(8,128)S(1)}, f32[2,40,128]{2,1,0:T(8,128)S(1)}, u32[]{:S(2)}, u32[]{:S(2)}) %collective-permute-start.4) | collective-permute-done | bytes 40992 | tf_op jit(solution)/shard_map/ppermute | solution.py:424
  22.9 0.0 collective-permute-done.5.zr
  22.9 5.8 %fine_kernel.1 = (f32[12,16,128]{2,1,0:T(8,128)S(1)}, f32[24,40,256]{2,1,0:T(8,128)S(1)}, f32[24,40,256]{2,1,0:T(8,128)S(1)}, f32[24,40,256]{2,1,0:T(8,128)S(1)}...) custom-call(s32[3]{0:T(128)S(1)} %pad_add_fusion.pos, ...), custom_call_target="tpu_custom_call" | custom-call | tf_op jit(solution)/shard_map/fine_kernel/pallas_call | solution.py:411
  28.7 1.0 copy-done.3
  29.7 1.0 copy-done.6
  30.6 3.0 %collective-permute-start.8 = (f32[12,16,128]{2,1,0:T(8,128)S(1)}, f32[12,16,128]{2,1,0:T(8,128)S(1)}, u32[]{:S(2)}, u32[]{:S(2)}) collective-permute-start(f32[12,16,128]{2,1,0:T(8,128)S(1)} %get-tuple-element.41), channel_id=1, source_target_pairs={{0,192},{64,128},{128,64},{192,0},{1,193},{65,129},{129,65},{193,1... | collective-permute-start | bytes 294920 | tf_op jit(solution)/shard_map/ppermute | solution.py:429
  33.6 0.7 collective-permute-start.7
  34.3 0.4 collective-permute-start.6
  34.8 4.9 %collective-permute-done.6 = f32[12,16,128]{2,1,0:T(8,128)S(1)} collective-permute-done((f32[12,16,128]{2,1,0:T(8,128)S(1)}, f32[12,16,128]{2,1,0:T(8,128)S(1)}, u32[]{:S(2)}, u32[]{:S(2)}) %collective-permute-start.6) | collective-permute-done | bytes 98336 | tf_op jit(solution)/shard_map/ppermute | solution.py:429
  39.7 1.1 %collective-permute-done.7 = f32[12,16,128]{2,1,0:T(8,128)S(1)} collective-permute-done((f32[12,16,128]{2,1,0:T(8,128)S(1)}, f32[12,16,128]{2,1,0:T(8,128)S(1)}, u32[]{:S(2)}, u32[]{:S(2)}) %collective-permute-start.7) | collective-permute-done | bytes 98336 | tf_op jit(solution)/shard_map/ppermute | solution.py:429
  40.8 0.0 collective-permute-done.8
  40.8 0.1 collective-permute-start.10
  40.9 3.5 %collective-permute-start.9 = (f32[48,16,128]{2,1,0:T(8,128)S(1)}, f32[48,16,128]{2,1,0:T(8,128)S(1)}, u32[]{:S(2)}, u32[]{:S(2)}) collective-permute-start(f32[48,16,128]{2,1,0:T(8,128)S(1)} %constant_dynamic-update-slice_fusion.own), channel_id=1, source_target_pairs={{0,8},{8,16},{16,24},{24,32},{32,40},{40,48},{48,56},{56,0},{1,9},... | collective-permute-start | bytes 1179656 | tf_op jit(solution)/shard_map/ppermute | solution.py:424
  44.4 7.4 %collective-permute-done.10.yr = f32[48,16,128]{2,1,0:T(8,128)S(1)} collective-permute-done((f32[48,16,128]{2,1,0:T(8,128)S(1)}, f32[48,16,128]{2,1,0:T(8,128)S(1)}, u32[]{:S(2)}, u32[]{:S(2)}) %collective-permute-start.10) | collective-permute-done | bytes 393248 | tf_op jit(solution)/shard_map/ppermute | solution.py:424
  51.8 0.0 collective-permute-done.9.yl
  51.8 0.5 pack_z1_kernel.1
  52.3 0.0 collective-permute-start.11
  52.3 3.0 %collective-permute-start.12 = (f32[12,48,128]{2,1,0:T(8,128)S(1)}, f32[12,48,128]{2,1,0:T(8,128)S(1)}, u32[]{:S(2)}, u32[]{:S(2)}) collective-permute-start(f32[12,48,128]{2,1,0:T(8,128)S(1)} %get-tuple-element.43), channel_id=1, source_target_pairs={{0,7},{1,0},{2,1},{3,2},{4,3},{5,4},{6,5},{7,6},{8,15},{9,8},{10,9... | collective-permute-start | bytes 884744 | tf_op jit(solution)/shard_map/ppermute | solution.py:424
  55.3 4.4 %collective-permute-done.11.zl = f32[12,48,128]{2,1,0:T(8,128)S(1)} collective-permute-done((f32[12,48,128]{2,1,0:T(8,128)S(1)}, f32[12,48,128]{2,1,0:T(8,128)S(1)}, u32[]{:S(2)}, u32[]{:S(2)}) %collective-permute-start.11) | collective-permute-done | bytes 294944 | tf_op jit(solution)/shard_map/ppermute | solution.py:424
  59.7 11.3 %middle_kernel.1 = (f32[3,8,128]{2,1,0:T(8,128)S(1)}, f32[34,48,128]{2,1,0:T(8,128)S(1)}, f32[34,48,128]{2,1,0:T(8,128)S(1)}, f32[34,48,128]{2,1,0:T(8,128)S(1)}...) custom-call(s32[3]{0:T(128)S(1)} %pad_add_fusion.pos, ...), custom_call_target="tpu_custom_call" | custom-call | tf_op jit(solution)/shard_map/middle_kernel/pallas_call | solution.py:411
  71.0 3.0 %collective-permute-start.14 = (f32[3,8,128]{2,1,0:T(8,128)S(1)}, f32[3,8,128]{2,1,0:T(8,128)S(1)}, u32[]{:S(2)}, u32[]{:S(2)}) collective-permute-start(f32[3,8,128]{2,1,0:T(8,128)S(1)} %get-tuple-element.44), channel_id=1, source_target_pairs={{0,7},{1,0},{2,1},{3,2},{4,3},{5,4},{6,5},{7,6},{8,15},{9,8},{10,9... | collective-permute-start | bytes 36872 | tf_op jit(solution)/shard_map/ppermute | solution.py:424
  74.0 4.3 %collective-permute-done.13 = f32[3,8,128]{2,1,0:T(8,128)S(1)} collective-permute-done((f32[3,8,128]{2,1,0:T(8,128)S(1)}, f32[3,8,128]{2,1,0:T(8,128)S(1)}, u32[]{:S(2)}, u32[]{:S(2)}) %collective-permute-start.13) | collective-permute-done | bytes 12320 | tf_op jit(solution)/shard_map/ppermute | solution.py:424
  78.3 0.0 collective-permute-done.14
  78.3 3.3 %collective-permute-start.16 = (f32[9,8,128]{2,1,0:T(8,128)S(1)}, f32[9,8,128]{2,1,0:T(8,128)S(1)}, u32[]{:S(2)}, u32[]{:S(2)}) collective-permute-start(f32[9,8,128]{2,1,0:T(8,128)S(1)} %constant_dynamic-update-slice_fusion.4.own), channel_id=1, source_target_pairs={{0,16},{8,56},{16,0},{24,8},{32,48},{40,24},{48,32},{56,40},{1,17}... | collective-permute-start | bytes 110600 | tf_op jit(solution)/shard_map/ppermute | solution.py:465
  81.6 2.2 %collective-permute-start.15 = (f32[9,8,128]{2,1,0:T(8,128)S(1)}, f32[9,8,128]{2,1,0:T(8,128)S(1)}, u32[]{:S(2)}, u32[]{:S(2)}) collective-permute-start(f32[9,8,128]{2,1,0:T(8,128)S(1)} %constant_dynamic-update-slice_fusion.4.own), channel_id=1, source_target_pairs={{0,8},{8,24},{16,32},{24,40},{32,16},{40,56},{48,0},{56,48},{1,9},... | collective-permute-start | bytes 110600 | tf_op jit(solution)/shard_map/ppermute | solution.py:465
  83.8 0.0 collective-permute-done.16.second
  83.8 3.8 %collective-permute-done.15.first = f32[9,8,128]{2,1,0:T(8,128)S(1)} collective-permute-done((f32[9,8,128]{2,1,0:T(8,128)S(1)}, f32[9,8,128]{2,1,0:T(8,128)S(1)}, u32[]{:S(2)}, u32[]{:S(2)}) %collective-permute-start.15) | collective-permute-done | bytes 36896 | tf_op jit(solution)/shard_map/ppermute | solution.py:465
  87.6 1.1 %copy-done.7 = f32[34,48,128]{2,1,0:T(8,128)S(1)} copy-done((f32[34,48,128]{2,1,0:T(8,128)S(1)}, f32[34,48,128]{2,1,0:T(8,128)}, u32[]{:S(2)}) %copy-start.7) | copy-done | bytes 835608
  88.8 1.1 %copy-done.8 = f32[34,48,128]{2,1,0:T(8,128)S(1)} copy-done((f32[34,48,128]{2,1,0:T(8,128)S(1)}, f32[34,48,128]{2,1,0:T(8,128)}, u32[]{:S(2)}) %copy-start.8) | copy-done | bytes 835608
  89.9 15.1 %last_kernel.1 = f32[16,32,128]{2,1,0:T(8,128)} custom-call(s32[3]{0:T(128)S(1)} %pad_add_fusion.pos, f32[9,8,128]{2,1,0:T(8,128)S(1)} %constant_dynamic-update-slice_fusion.4.own, f32[9,8,128]{2,1,0:T(8,128)S(1)} %collective-permute-done.15.first, f32[9,8,128]{2,1,0:T(8,128)S(1)} %collective-permute-done.16.second, f32[24,40,256]{2,1,0:T(8,128)} %copy-done.3, ...), custom_call_target="tpu_custom_call" | custom-call | tf_op jit(solution)/shard_map/last_kernel/pallas_call | solution.py:411
  (22 shorter events, 0.1 us)
Async XLA Ops:
  0.0 1.0 copy-start.1
  1.9 7.5 %copy-start = (f32[16,32,128]{2,1,0:T(8,128)S(1)}, f32[16,32,128]{2,1,0:T(8,128)}, u32[]{:S(2)}) copy-start(f32[16,32,128]{2,1,0:T(8,128)} %k.3) | copy-start | bytes 786436
  1.9 7.4 %copy-start.2 = (f32[16,32,128]{2,1,0:T(8,128)S(1)}, f32[16,32,128]{2,1,0:T(8,128)}, u32[]{:S(2)}) copy-start(f32[16,32,128]{2,1,0:T(8,128)} %m.3) | copy-start | bytes 786436
  1.9 7.3 %collective-permute-start = (f32[10,32,128]{2,1,0:T(8,128)S(1)}, f32[10,32,128]{2,1,0:T(8,128)S(1)}, u32[]{:S(2)}, u32[]{:S(2)}) collective-permute-start(f32[10,32,128]{2,1,0:T(8,128)S(1)} %pad_maximum_fusion), channel_id=1, source_target_pairs={{0,64},{64,128},{128,192},{192,0},{1,65},{65,129},{129,193},{193,1... | collective-permute-start | bytes 491528 | tf_op jit(solution)/shard_map/ppermute | solution.py:424
  3.6 5.7 %collective-permute-start.1 = (f32[10,32,128]{2,1,0:T(8,128)S(1)}, f32[10,32,128]{2,1,0:T(8,128)S(1)}, u32[]{:S(2)}, u32[]{:S(2)}) collective-permute-start(f32[10,32,128]{2,1,0:T(8,128)S(1)} %pad_maximum_fusion.1), channel_id=1, source_target_pairs={{0,192},{64,0},{128,64},{192,128},{1,193},{65,1},{129,65},{193,129... | collective-permute-start | bytes 491528 | tf_op jit(solution)/shard_map/ppermute | solution.py:424
  9.4 5.0 %collective-permute-start.2 = (f32[240,128]{1,0:T(8,128)S(1)}, f32[240,128]{1,0:T(8,128)S(1)}, u32[]{:S(2)}, u32[]{:S(2)}) collective-permute-start(f32[240,128]{1,0:T(8,128)S(1)} %get-tuple-element.34), channel_id=1, source_target_pairs={{0,8},{8,16},{16,24},{24,32},{32,40},{40,48},{48,56},{56,0},{1,9},... | collective-permute-start | bytes 368648 | tf_op jit(solution)/shard_map/ppermute | solution.py:424
  11.4 6.0 %collective-permute-start.3 = (f32[240,128]{1,0:T(8,128)S(1)}, f32[240,128]{1,0:T(8,128)S(1)}, u32[]{:S(2)}, u32[]{:S(2)}) collective-permute-start(f32[240,128]{1,0:T(8,128)S(1)} %get-tuple-element.35), channel_id=1, source_target_pairs={{0,56},{8,0},{16,8},{24,16},{32,24},{40,32},{48,40},{56,48},{1,57}... | collective-permute-start | bytes 368648 | tf_op jit(solution)/shard_map/ppermute | solution.py:424
  18.2 4.6 %collective-permute-start.4 = (f32[2,40,128]{2,1,0:T(8,128)S(1)}, f32[2,40,128]{2,1,0:T(8,128)S(1)}, u32[]{:S(2)}, u32[]{:S(2)}) collective-permute-start(f32[2,40,128]{2,1,0:T(8,128)S(1)} %get-tuple-element.39), channel_id=1, source_target_pairs={{0,1},{1,2},{2,3},{3,4},{4,5},{5,6},{6,7},{7,0},{8,9},{9,10},{10,1... | collective-permute-start | bytes 122888 | tf_op jit(solution)/shard_map/ppermute | solution.py:424
  18.2 4.6 %collective-permute-start.5 = (f32[2,40,128]{2,1,0:T(8,128)S(1)}, f32[2,40,128]{2,1,0:T(8,128)S(1)}, u32[]{:S(2)}, u32[]{:S(2)}) collective-permute-start(f32[2,40,128]{2,1,0:T(8,128)S(1)} %get-tuple-element.40), channel_id=1, source_target_pairs={{0,7},{1,0},{2,1},{3,2},{4,3},{5,4},{6,5},{7,6},{8,15},{9,8},{10,9... | collective-permute-start | bytes 122888 | tf_op jit(solution)/shard_map/ppermute | solution.py:424
  28.7 1.0 copy-start.3
  29.6 1.0 copy-start.6
  30.6 21.7 %copy-start.4 = (f32[24,40,256]{2,1,0:T(8,128)}, f32[24,40,256]{2,1,0:T(8,128)S(1)}, u32[]{:S(2)}) copy-start(f32[24,40,256]{2,1,0:T(8,128)S(1)} %get-tuple-element.46.w0) | copy-start | bytes 2949124
  30.6 21.7 %copy-start.5 = (f32[24,40,256]{2,1,0:T(8,128)}, f32[24,40,256]{2,1,0:T(8,128)S(1)}, u32[]{:S(2)}) copy-start(f32[24,40,256]{2,1,0:T(8,128)S(1)} %get-tuple-element.47.g0) | copy-start | bytes 2949124
  30.6 10.1 %collective-permute-start.8 = (f32[12,16,128]{2,1,0:T(8,128)S(1)}, f32[12,16,128]{2,1,0:T(8,128)S(1)}, u32[]{:S(2)}, u32[]{:S(2)}) collective-permute-start(f32[12,16,128]{2,1,0:T(8,128)S(1)} %get-tuple-element.41), channel_id=1, source_target_pairs={{0,192},{64,128},{128,64},{192,0},{1,193},{65,129},{129,65},{193,1... | collective-permute-start | bytes 294920 | tf_op jit(solution)/shard_map/ppermute | solution.py:429
  33.6 7.2 %collective-permute-start.7 = (f32[12,16,128]{2,1,0:T(8,128)S(1)}, f32[12,16,128]{2,1,0:T(8,128)S(1)}, u32[]{:S(2)}, u32[]{:S(2)}) collective-permute-start(f32[12,16,128]{2,1,0:T(8,128)S(1)} %get-tuple-element.41), channel_id=1, source_target_pairs={{0,128},{64,192},{128,0},{192,64},{1,129},{65,193},{129,1},{193,65... | collective-permute-start | bytes 294920 | tf_op jit(solution)/shard_map/ppermute | solution.py:429
  34.3 5.4 %collective-permute-start.6 = (f32[12,16,128]{2,1,0:T(8,128)S(1)}, f32[12,16,128]{2,1,0:T(8,128)S(1)}, u32[]{:S(2)}, u32[]{:S(2)}) collective-permute-start(f32[12,16,128]{2,1,0:T(8,128)S(1)} %get-tuple-element.41), channel_id=1, source_target_pairs={{0,64},{64,0},{128,192},{192,128},{1,65},{65,1},{129,193},{193,129... | collective-permute-start | bytes 294920 | tf_op jit(solution)/shard_map/ppermute | solution.py:429
  40.8 11.0 %collective-permute-start.10 = (f32[48,16,128]{2,1,0:T(8,128)S(1)}, f32[48,16,128]{2,1,0:T(8,128)S(1)}, u32[]{:S(2)}, u32[]{:S(2)}) collective-permute-start(f32[48,16,128]{2,1,0:T(8,128)S(1)} %constant_dynamic-update-slice_fusion.own), channel_id=1, source_target_pairs={{0,56},{8,0},{16,8},{24,16},{32,24},{40,32},{48,40},{56,48},{1,57}... | collective-permute-start | bytes 1179656 | tf_op jit(solution)/shard_map/ppermute | solution.py:424
  40.9 10.9 %collective-permute-start.9 = (f32[48,16,128]{2,1,0:T(8,128)S(1)}, f32[48,16,128]{2,1,0:T(8,128)S(1)}, u32[]{:S(2)}, u32[]{:S(2)}) collective-permute-start(f32[48,16,128]{2,1,0:T(8,128)S(1)} %constant_dynamic-update-slice_fusion.own), channel_id=1, source_target_pairs={{0,8},{8,16},{16,24},{24,32},{32,40},{40,48},{48,56},{56,0},{1,9},... | collective-permute-start | bytes 1179656 | tf_op jit(solution)/shard_map/ppermute | solution.py:424
  52.3 7.4 %collective-permute-start.11 = (f32[12,48,128]{2,1,0:T(8,128)S(1)}, f32[12,48,128]{2,1,0:T(8,128)S(1)}, u32[]{:S(2)}, u32[]{:S(2)}) collective-permute-start(f32[12,48,128]{2,1,0:T(8,128)S(1)} %get-tuple-element.42), channel_id=1, source_target_pairs={{0,1},{1,2},{2,3},{3,4},{4,5},{5,6},{6,7},{7,0},{8,9},{9,10},{10,1... | collective-permute-start | bytes 884744 | tf_op jit(solution)/shard_map/ppermute | solution.py:424
  52.3 7.4 %collective-permute-start.12 = (f32[12,48,128]{2,1,0:T(8,128)S(1)}, f32[12,48,128]{2,1,0:T(8,128)S(1)}, u32[]{:S(2)}, u32[]{:S(2)}) collective-permute-start(f32[12,48,128]{2,1,0:T(8,128)S(1)} %get-tuple-element.43), channel_id=1, source_target_pairs={{0,7},{1,0},{2,1},{3,2},{4,3},{5,4},{6,5},{7,6},{8,15},{9,8},{10,9... | collective-permute-start | bytes 884744 | tf_op jit(solution)/shard_map/ppermute | solution.py:424
  71.0 7.3 %collective-permute-start.14 = (f32[3,8,128]{2,1,0:T(8,128)S(1)}, f32[3,8,128]{2,1,0:T(8,128)S(1)}, u32[]{:S(2)}, u32[]{:S(2)}) collective-permute-start(f32[3,8,128]{2,1,0:T(8,128)S(1)} %get-tuple-element.44), channel_id=1, source_target_pairs={{0,7},{1,0},{2,1},{3,2},{4,3},{5,4},{6,5},{7,6},{8,15},{9,8},{10,9... | collective-permute-start | bytes 36872 | tf_op jit(solution)/shard_map/ppermute | solution.py:424
  74.0 4.3 %collective-permute-start.13 = (f32[3,8,128]{2,1,0:T(8,128)S(1)}, f32[3,8,128]{2,1,0:T(8,128)S(1)}, u32[]{:S(2)}, u32[]{:S(2)}) collective-permute-start(f32[3,8,128]{2,1,0:T(8,128)S(1)} %get-tuple-element.44), channel_id=1, source_target_pairs={{0,1},{1,2},{2,3},{3,4},{4,5},{5,6},{6,7},{7,0},{8,9},{9,10},{10,1... | collective-permute-start | bytes 36872 | tf_op jit(solution)/shard_map/ppermute | solution.py:424
  78.3 5.5 %collective-permute-start.16 = (f32[9,8,128]{2,1,0:T(8,128)S(1)}, f32[9,8,128]{2,1,0:T(8,128)S(1)}, u32[]{:S(2)}, u32[]{:S(2)}) collective-permute-start(f32[9,8,128]{2,1,0:T(8,128)S(1)} %constant_dynamic-update-slice_fusion.4.own), channel_id=1, source_target_pairs={{0,16},{8,56},{16,0},{24,8},{32,48},{40,24},{48,32},{56,40},{1,17}... | collective-permute-start | bytes 110600 | tf_op jit(solution)/shard_map/ppermute | solution.py:465
  81.6 6.1 %collective-permute-start.15 = (f32[9,8,128]{2,1,0:T(8,128)S(1)}, f32[9,8,128]{2,1,0:T(8,128)S(1)}, u32[]{:S(2)}, u32[]{:S(2)}) collective-permute-start(f32[9,8,128]{2,1,0:T(8,128)S(1)} %constant_dynamic-update-slice_fusion.4.own), channel_id=1, source_target_pairs={{0,8},{8,24},{16,32},{24,40},{32,16},{40,56},{48,0},{56,48},{1,9},... | collective-permute-start | bytes 110600 | tf_op jit(solution)/shard_map/ppermute | solution.py:465
  87.6 1.2 %copy-start.7 = (f32[34,48,128]{2,1,0:T(8,128)S(1)}, f32[34,48,128]{2,1,0:T(8,128)}, u32[]{:S(2)}) copy-start(f32[34,48,128]{2,1,0:T(8,128)} %get-tuple-element.54.k1) | copy-start | bytes 2506756
  88.8 1.1 %copy-start.8 = (f32[34,48,128]{2,1,0:T(8,128)S(1)}, f32[34,48,128]{2,1,0:T(8,128)}, u32[]{:S(2)}) copy-start(f32[34,48,128]{2,1,0:T(8,128)} %get-tuple-element.55.cy1) | copy-start | bytes 2506756

commit v2 on v1

v2 whole, which is shorter than its diff:
```python
import functools

import jax
import jax.numpy as jnp
from jax import lax
from jax.experimental import pallas as pl
from jax.experimental.pallas import tpu as pltpu
from jax.sharding import PartitionSpec as P

SWEEPS = 2
COARSE_SWEEPS = 8
OMEGA = 2.0 / 3.0
KEEP = 1.0 - OMEGA
OUTSIDE = 1e30
LIMIT = 1e29
F32 = jnp.float32
BF16 = jnp.bfloat16


def dot(a, b):
    high = a.astype(BF16)
    rest = a - high.astype(F32)
    middle = rest.astype(BF16)
    low = (rest - middle.astype(F32)).astype(BF16)
    terms = jnp.concatenate([high, middle, low], axis=1)
    matrix = b.astype(BF16)
    return jnp.dot(terms, jnp.concatenate([matrix] * 3, axis=0), preferred_element_type=F32)


def iota(shape, dim):
    return lax.broadcasted_iota(jnp.int32, shape, dim)


def roll(x, shift, axis):
    size = x.shape[axis]
    shift = shift % size
    return x if shift == 0 else pltpu.roll(x, shift, axis)


def after(x, axis):
    return roll(x, -1, axis)


def before(x, axis):
    return roll(x, 1, axis)


def planes(low, high, values, store, group):
    def run(first, count):
        found = [values(first + i) for i in range(count)]
        for i, value in enumerate(found):
            store(first + i, value)

    whole = (high - low) // group
    if whole == 1:
        run(low, group)
    elif whole:

        def step(index, carry):
            run(low + index * group, group)
            return carry

        lax.fori_loop(0, whole, step, 0)
    if (high - low) % group:
        run(low + whole * group, (high - low) % group)


def coefficients(low, high, group, k, f, m, d, w, g, cy, cz):
    def values(p):
        here = k[p]
        y = here + after(here, 0)
        z = here + after(here, 1)
        diagonal = m[p] + (k[p - 1] + here) + (here + k[p + 1])
        diagonal = diagonal + y + before(y, 0) + z + before(z, 1)
        weight = jnp.where(m[p] < LIMIT, OMEGA / diagonal, 0.0)
        return y, z, weight, diagonal, None if f is None else weight * f[p]

    def store(p, found):
        cy[p], cz[p], w[p] = found[:3]
        if d is not None:
            d[p] = found[3]
        if f is not None:
            g[p] = found[4]

    planes(low, high, values, store, group)


def neighbours(p, k, cy, cz, v):
    here, centre, y, z = k[p], v[p], cy[p], cz[p]
    total = (k[p - 1] + here) * v[p - 1] + (here + k[p + 1]) * v[p + 1]
    total = total + y * after(centre, 0) + before(y * centre, 0)
    total = total + z * after(centre, 1) + before(z * centre, 1)
    return total, centre


def sweep(low, high, group, k, w, g, cy, cz, v, out):
    def values(p):
        total, centre = neighbours(p, k, cy, cz, v)
        return KEEP * centre + g[p] + w[p] * total

    def store(p, value):
        out[p] = value

    planes(low, high, values, store, group)


def pack_y_kernel(f, k, m, xl, xr, up, down):
    for p in range(24):
        for out, lo3, lo4 in ((up, 29, 28), (down, 0, 0)):
            base = 10 * p
            if p < 4:
                kk = xl[6 + p, lo4 : lo4 + 4]
            elif p < 20:
                kk = k[p - 4, lo4 : lo4 + 4]
            else:
                kk = xr[6 + p - 20, lo4 : lo4 + 4]
            if 1 <= p < 4:
                ff, mm = xl[p - 1, lo3 : lo3 + 3], xl[2 + p, lo3 : lo3 + 3]
            elif 4 <= p < 20:
                ff, mm = f[p - 4, lo3 : lo3 + 3], m[p - 4, lo3 : lo3 + 3]
            elif 20 <= p < 23:
                ff, mm = xr[p - 20, lo3 : lo3 + 3], xr[p - 17, lo3 : lo3 + 3]
            else:
                ff = mm = jnp.zeros((3, 128), F32)
            out[base : base + 3] = ff
            out[base + 3 : base + 6] = mm
            out[base + 6 : base + 10] = kk


def pack_z_kernel(f, k, m, xl, xr, yl, yr, fa, ka, ma, up, down):
    lane = iota((40, 128), 1)
    zero = jnp.zeros((32, 128), F32)
    for g in range(2):
        acc_up = jnp.zeros((40, 128), F32)
        acc_down = jnp.zeros((40, 128), F32)
        for i in range(12):
            p = 12 * g + i
            base = 10 * p
            if p < 4:
                own = (xl[p - 1] if p else zero, xl[2 + p] if p else zero, xl[6 + p])
            elif p < 20:
                own = (f[p - 4], m[p - 4], k[p - 4])
            else:
                own = (xr[p - 20] if p < 23 else zero, xr[p - 17] if p < 23 else zero, xr[p - 14])
            for a, out in enumerate((fa, ma, ka)):
                width = 4 if a == 2 else 3
                out[p, 0:32] = own[a]
                out[p, 32:40] = jnp.zeros((8, 128), F32)
                out[p, 32 : 32 + width] = yr[base + 3 * a : base + 3 * a + width]
                out[p, 40 - width : 40] = yl[base + 3 * a : base + 3 * a + width]
                whole = out[p]
                first = 10 * i + 3 * a
                mask = (lane >= first) & (lane < first + width)
                acc_up = jnp.where(mask, roll(whole, first - (128 - width), 1), acc_up)
                acc_down = jnp.where(mask, roll(whole, first, 1), acc_down)
        up[g] = acc_up
        down[g] = acc_down


def pair_matrix(columns):
    return jnp.where(iota((128, columns), 0) // 2 == iota((128, columns), 1) % 64, 0.125, 0.0)


def coarse_kernel(k, m, message, tall):
    pairs = pair_matrix(128)
    for slot, ref in enumerate((m, k)):
        for i in range(8):
            tall[32 * i : 32 * i + 32] = ref[2 * i] + ref[2 * i + 1]
        halve_and_pack(tall, pairs, message, 4 * slot)


def halve_and_pack(tall, pairs, message, first):
    lane16 = iota((16, 128), 1)
    halves = tall[pl.ds(0, 128, stride=2), :] + tall[pl.ds(1, 128, stride=2), :]
    coarse = dot(halves, pairs)
    for i in range(4):
        message[first + i] = jnp.where(
            lane16 < 64, coarse[16 * i : 16 * i + 16], coarse[16 * i + 64 : 16 * i + 80]
        )


def fine_kernel(pos, fa, ka, ma, zl, zr, message, v_out, w, g, k, cy, cz, f, m, d, tall):
    ix, iy, iz = pos[0], pos[1], pos[2]
    row = iota((40, 128), 0)
    lane = iota((40, 128), 1)
    far = ((row >= 32) & (row < 36) & (iy == 7)) | ((row >= 36) & (iy == 0))
    beside = ((lane < 4) & (iz < 7)) | ((lane >= 124) & (iz > 0))
    row_inner = (row < 35) | (row > 36)
    inner = (lane < 3) | (lane > 124)
    for p in range(24):
        group, i = p // 12, p % 12
        absent = False
        if p < 4:
            absent = ix == 0
        elif p >= 20:
            absent = ix == 3
        gone = far | absent
        for a, (src, out) in enumerate(((fa, f), (ma, m), (ka, k))):
            width = 4 if a == 2 else 3
            first = 10 * i + 3 * a
            if a == 1 and p in (0, 23):
                out[p] = jnp.full((40, 256), OUTSIDE, F32)
                continue
            right = roll(zr[group], -first, 1)
            left = roll(zl[group], 128 - width - first, 1)
            side = jnp.where(lane < 64, right, left)
            own = src[p]
            fill = OUTSIDE if a == 1 else 0.0
            if a == 2:
                here, there = gone, gone | ~beside
                own, side = 0.5 * own, 0.5 * side
            else:
                here = gone | ~row_inner
                there = here | ~(beside & inner)
            out[p, :, 0:128] = jnp.where(here, fill, own)
            out[p, :, 128:256] = jnp.where(there, fill, side)
    coefficients(1, 23, 4, k, f, m, d, w, g, cy, cz)
    sweep(2, 22, 4, k, w, g, cy, cz, g, v_out)

    def residual(p):
        total, centre = neighbours(p, k, cy, cz, v_out)
        return (f[p] + total - d[p] * centre)[0:32, 0:128]

    def values(i):
        return residual(2 * i + 4) + residual(2 * i + 5)

    def store(i, value):
        tall[pl.ds(pl.multiple_of(32 * i, 32), 32), :] = value

    planes(0, 8, values, store, 2)
    halve_and_pack(tall, pair_matrix(128), message, 0)


def pack_z1_kernel(count, own, yl, yr, up, down):
    lane = iota((16, 128), 1) % 64
    for b in range(4 * count):
        for part, src in enumerate((own, yr, yl)):
            acc_up = jnp.zeros((16, 128), F32)
            acc_down = jnp.zeros((16, 128), F32)
            for q in range(4):
                pair = src[4 * b + q]
                mask = (lane >= 16 * q) & (lane < 16 * q + 16)
                acc_up = jnp.where(mask, roll(pair, 16 * q - 48, 1), acc_up)
                acc_down = jnp.where(mask, roll(pair, 16 * q, 1), acc_down)
            up[b, 16 * part : 16 * part + 16] = acc_up
            down[b, 16 * part : 16 * part + 16] = acc_down


def clear(refs, low, high):
    for ref in refs:
        for p in (*range(low), *range(high, ref.shape[0])):
            ref[p] = jnp.zeros(ref.shape[1:], F32)


def outside1(iy, iz):
    row, lane = iota((48, 128), 0), iota((48, 128), 1)
    gone = ((row >= 16) & (row < 32) & (iy == 7)) | ((row >= 32) & (iy == 0))
    gone = gone | ((lane >= 64) & (lane < 80) & (iz == 7)) | ((lane >= 112) & (iz == 0))
    return gone | ((lane >= 80) & (lane < 112))


def spread1(ix, gone, own, yl, yr, zl, zr, count, a, out, fill, scale):
    lane = iota((48, 128), 1)
    for b in range(4):
        block = 8 * jnp.bitwise_xor(ix, b) + 4
        left, right = zl[count * b + a], zr[count * b + a]
        for q in range(4):
            s = 4 * (count * b + a) + q
            pair = jnp.concatenate([own[s], yr[s], yl[s]], axis=0)
            for h in range(2):
                at = 16 * (q + 4 * h)
                side = jnp.where(lane < 96, roll(right, 64 - at, 1), roll(left, 112 - at, 1))
                value = jnp.where(lane < 64, roll(pair, 64 * h, 1), side)
                value = value if scale == 1.0 else scale * value
                out[block + q + 4 * h] = jnp.where(gone, fill, value)


def known2(shape):
    lane = iota(shape, 1)
    return (lane < 40) | (lane >= 120)


def to_second(tall, out, values, fill):
    def store(i, value):
        tall[pl.ds(pl.multiple_of(48 * i, 48), 48), :] = value

    planes(0, 16, lambda i: values(2 * i + 4) + values(2 * i + 5), store, 4)
    halves = tall[pl.ds(0, 384, stride=2), :] + tall[pl.ds(1, 384, stride=2), :]
    coarse = dot(halves, jnp.where(known2((128, 128)), pair_matrix(128), 0.0))
    for i in range(16):
        out[i + 4] = jnp.where(known2((24, 128)), coarse[24 * i : 24 * i + 24], fill)


def to_third(tall, small, write, values):
    for i in range(8):
        tall[24 * i : 24 * i + 24] = values(2 * i + 4) + values(2 * i + 5)
    halves = tall[pl.ds(0, 96, stride=2), :] + tall[pl.ds(1, 96, stride=2), :]
    spread = jnp.where(iota((128, 128), 0) // 2 == iota((128, 128), 1) % 16, 0.125, 0.0)
    small[0:96] = dot(halves, spread)
    group = iota((12, 128), 1) // 16
    packed = jnp.zeros((12, 128), F32)
    for i in range(8):
        packed = jnp.where(group == i, small[12 * i : 12 * i + 12], packed)
    small[0:12] = packed
    write(slice(0, 2), small[10:12])
    write(slice(2, 8), small[0:6])


def cut1(ix, src, out):
    for p in range(16):
        out[p, 0:20] = src[8 * ix + p, 0:20]
        out[p, 20:24] = src[8 * ix + p, 44:48]


def cut2(ix, src, out):
    for p in range(12):
        out[p, 0:12] = src[4 * ix + p, 0:12]
        out[p, 12:16] = src[4 * ix + p, 20:24]


def static_kernel(
    pos, own, yl, yr, zl, zr,
    coarsest, k1, w1, cy1, cz1, d1, k2, w2, cy2, cz2, d2,
    k1n, w1n, cy1n, cz1n, k2n, w2n, cy2n, cz2n,
    m1, m2, tall, small,
):
    ix, iy, iz = pos[0], pos[1], pos[2]
    gone = outside1(iy, iz)
    clear((k1, w1, cy1, cz1), 4, 36)
    clear((k2, w2, cy2, cz2), 4, 20)
    spread1(ix, gone, own, yl, yr, zl, zr, 2, 0, m1, OUTSIDE, 1.0)
    spread1(ix, gone, own, yl, yr, zl, zr, 2, 1, k1, 0.0, 0.125)
    coefficients(4, 36, 8, k1, None, m1, d1, w1, None, cy1, cz1)
    to_second(tall, m2, lambda p: m1[p], OUTSIDE)
    to_second(tall, k2, lambda p: 0.25 * k1[p], 0.0)
    coefficients(4, 20, 8, k2, None, m2, d2, w2, None, cy2, cz2)

    def write(slot):
        def put(where, value):
            coarsest[slot, where] = value

        return put

    to_third(tall, small, write(0), lambda p: m2[p])
    to_third(tall, small, write(1), lambda p: 0.25 * k2[p])
    for src, out in ((k1, k1n), (w1, w1n), (cy1, cy1n), (cz1, cz1n)):
        cut1(ix, src, out)
    for src, out in ((k2, k2n), (w2, w2n), (cy2, cy2n), (cz2, cz2n)):
        cut2(ix, src, out)


def middle_kernel(
    pos, own, yl, yr, zl, zr, coarsest, k1, w1, cy1, cz1, d1, k2, w2, cy2, cz2, d2,
    message, v1n, g1n, v2n, g2n,
    f1, g1, v1, f2, g2, v2, tall, small,
):
    ix, iy, iz = pos[0], pos[1], pos[2]
    gone = outside1(iy, iz)
    clear((g1, v1), 4, 36)
    clear((g2, v2), 4, 20)
    spread1(ix, gone, own, yl, yr, zl, zr, 1, 0, f1, 0.0, 1.0)

    def weigh(low, high, w, f, g):
        def store(p, value):
            g[p] = value

        planes(low, high, lambda p: w[p] * f[p], store, 8)

    weigh(4, 36, w1, f1, g1)
    sweep(4, 36, 8, k1, w1, g1, cy1, cz1, g1, v1)

    def residual1(p):
        total, centre = neighbours(p, k1, cy1, cz1, v1)
        return jnp.where(gone, 0.0, f1[p] + total - d1[p] * centre)

    to_second(tall, f2, residual1, 0.0)
    weigh(4, 20, w2, f2, g2)
    sweep(4, 20, 8, k2, w2, g2, cy2, cz2, g2, v2)
    row24 = iota((24, 128), 0)
    gone2 = ((row24 >= 8) & (row24 < 16) & (iy == 7)) | ((row24 >= 16) & (iy == 0))

    def residual2(p):
        total, centre = neighbours(p, k2, cy2, cz2, v2)
        return jnp.where(gone2, 0.0, f2[p] + total - d2[p] * centre)

    def put(where, value):
        message[0, where] = value

    to_third(tall, small, put, residual2)
    message[1] = coarsest[0]
    message[2] = coarsest[1]
    cut1(ix, v1, v1n)
    cut1(ix, g1, g1n)
    cut2(ix, v2, v2n)
    cut2(ix, g2, g2n)


def duplicate(out, base, rows, first, count):
    value = rows[first : first + count]
    out[pl.ds(base, count, stride=2), :] = value
    out[pl.ds(base + 1, count, stride=2), :] = value


def last_kernel(
    pos, own, first, second, v0, w0, g0, k0, cy0, cz0, v1, g1, v2, g2, k1, w1, cy1, cz1, k2, w2, cy2, cz2,
    out,
    k3, f3, m3, w3, g3, cy3, cz3, a3, b3, rows, dup, a2, b2, a1, b1, wide, low, high, a0, b0,
):
    ix, iy, iz = pos[0], pos[1], pos[2]
    row = iota((24, 128), 0) + 4 * iy - 10
    lane = iota((24, 128), 1)
    gone = (row < 0) | (row >= 32) | ((lane >= 32) & (lane < 112))
    gone = gone | ((lane >= 16) & (lane < 32) & (iz == 7)) | ((lane >= 112) & (iz == 0))
    clear((k3, g3, a3, b3), 2, 10)
    crossed = (iy == 2) | (iy == 6)

    def stack(index):
        one, two = first[index], second[index]
        ahead, behind = jnp.where(crossed, two, one), jnp.where(crossed, one, two)
        ahead = jnp.where(iy == 1, roll(ahead, 4, 0), ahead)
        behind = jnp.where(iy == 6, roll(behind, 4, 0), behind)
        return jnp.concatenate([ahead, own[index], behind], axis=0)

    for a, (ref, fill) in enumerate(((f3, 0.0), (m3, OUTSIDE), (k3, 0.0))):
        here, left, right = (stack(3 * z + a) for z in range(3))
        for x in range(8):
            value = jnp.where(
                lane < 16,
                roll(here, -16 * x, 1),
                jnp.where(lane < 64, roll(right, 16 - 16 * x, 1), roll(left, 112 - 16 * x, 1)),
            )
            ref[x + 2] = jnp.where(gone, fill, value)
    coefficients(2, 10, 8, k3, f3, m3, None, w3, g3, cy3, cz3)
    source = g3
    for index in range(COARSE_SWEEPS - 1):
        target = (a3, b3)[index % 2]
        sweep(2, 10, 8, k3, w3, g3, cy3, cz3, source, target)
        source = target

    src, column = iota((128, 128), 0), iota((128, 128), 1)
    to2 = jnp.where(
        ((column < 40) & (src == column // 2)) | ((column >= 120) & (src == 64 + column // 2)), 1.0, 0.0
    )
    for x in range(6):
        rows[24 * x : 24 * x + 24] = source[2 * ix + x]
    rows[0:144] = dot(rows[0:144], to2)
    for x in range(6):
        duplicate(dup, 16 * x, rows, 24 * x + 10, 6)
        duplicate(dup, 16 * x + 12, rows, 24 * x + 8, 2)
        both = dup[16 * x : 16 * x + 16]
        a2[2 * x] = v2[2 * x] + both
        a2[2 * x + 1] = v2[2 * x + 1] + both
    sweep(1, 11, 10, k2, w2, g2, cy2, cz2, a2, b2)
    sweep(2, 10, 8, k2, w2, g2, cy2, cz2, b2, a2)

    to1 = jnp.where(
        ((column < 80) & (src == column // 2)) | ((column >= 112) & (src == 64 + column // 2)), 1.0, 0.0
    )
    for x in range(8):
        rows[16 * x : 16 * x + 16] = a2[x + 2]
    rows[0:128] = dot(rows[0:128], to1)
    for x in range(8):
        duplicate(dup, 24 * x, rows, 16 * x, 10)
        duplicate(dup, 24 * x + 20, rows, 16 * x + 14, 2)
        both = dup[24 * x : 24 * x + 24]
        a1[2 * x] = v1[2 * x] + both
        a1[2 * x + 1] = v1[2 * x + 1] + both
    sweep(2, 14, 12, k1, w1, g1, cy1, cz1, a1, b1)
    sweep(3, 13, 10, k1, w1, g1, cy1, cz1, b1, a1)

    to0 = jnp.where(iota((128, 256), 0) == iota((128, 256), 1) // 2, 1.0, 0.0)
    for x in range(10):
        rows[24 * x : 24 * x + 24] = a1[x + 3]
    wide[...] = dot(rows[0:240], to0)
    for x in range(10):
        for half, lanes in ((low, slice(0, 128)), (high, slice(128, 256))):
            mid = wide[24 * x : 24 * x + 18, lanes]
            half[pl.ds(0, 18, stride=2), :] = mid
            half[pl.ds(1, 18, stride=2), :] = mid
            ahead = wide[24 * x + 22 : 24 * x + 24, lanes]
            half[pl.ds(36, 2, stride=2), :] = ahead
            half[pl.ds(37, 2, stride=2), :] = ahead
            for p in (2 * x + 2, 2 * x + 3):
                a0[p, :, lanes] = v0[p, :, lanes] + half[...]
    sweep(3, 21, 3, k0, w0, g0, cy0, cz0, a0, b0)

    def values(p):
        total, centre = neighbours(p, k0, cy0, cz0, b0)
        return (KEEP * centre + g0[p] + w0[p] * total)[0:32, 0:128]

    def store(p, value):
        out[p - 4] = value

    planes(4, 20, values, store, 4)


VMEM = pl.BlockSpec(memory_space=pltpu.VMEM)
SMEM = pl.BlockSpec(memory_space=pltpu.SMEM)


COARSE_TARGETS = ((1, 3, 4, 5, 2, 7, 0, 6), (2, 7, 0, 1, 6, 3, 4, 5))


def call(kernel, outs, scratch, *args, pos=None):
    specs = [VMEM] * len(args)
    if pos is not None:
        args = (pos,) + args
        specs = [SMEM] + specs
    return pl.pallas_call(
        kernel,
        out_shape=[jax.ShapeDtypeStruct(s, F32) for s in outs],
        in_specs=specs,
        out_specs=[VMEM] * len(outs),
        scratch_shapes=[pltpu.VMEM(s, F32) for s in scratch],
        compiler_params=pltpu.CompilerParams(vmem_limit_bytes=16 * 1024 * 1024),
        name=getattr(kernel, "__name__", "pack_z1_kernel"),
    )(*args)


def shift(x, axis, step):
    size = lax.axis_size(axis)
    return lax.ppermute(x, axis, [(i, (i + step) % size) for i in range(size)])


def swap(x, axis, bits):
    size = lax.axis_size(axis)
    return lax.ppermute(x, axis, [(i, i ^ bits) for i in range(size)])


FULL, SIDES = (24, 40, 256), (2, 40, 128)
ONE, TWO, THREE = (40, 48, 128), (24, 24, 128), (12, 24, 128)
NEAR1, NEAR2 = (16, 24, 128), (12, 16, 128)
TALL = (768, 128)


def gather_x(x):
    return jnp.concatenate([x] + [swap(x, "gx", bits) for bits in (1, 2, 3)])


def both_sides(up, down, axis):
    return shift(up, axis, 1), shift(down, axis, -1)


def pack_z1(count, own, yl, yr):
    kernel = functools.partial(pack_z1_kernel, count)
    return call(kernel, [(4 * count, 48, 128)] * 2, [], own, yl, yr)


def per_device(f, k, m):
    pos = jnp.stack([lax.axis_index("gx"), lax.axis_index("gy"), lax.axis_index("gz")])
    pos = pos.astype(jnp.int32)
    xl = shift(jnp.concatenate([f[13:], m[13:], k[12:]]), "gx", 1)
    xr = shift(jnp.concatenate([f[:3], m[:3], k[:4]]), "gx", -1)

    (brick,) = call(coarse_kernel, [(8, 16, 128)], [(256, 128)], k, m)
    own = gather_x(brick)
    yl, yr = both_sides(own, own, "gy")
    zl, zr = both_sides(*pack_z1(2, own, yl, yr), "gz")
    coarsest, *static = call(
        static_kernel,
        [(2, 8, 128)] + [ONE] * 5 + [TWO] * 5 + [NEAR1] * 4 + [NEAR2] * 4,
        [ONE, TWO, TALL, (96, 128)],
        own, yl, yr, zl, zr,
        pos=pos,
    )
    whole, near = static[:10], static[10:]

    yl, yr = both_sides(*call(pack_y_kernel, [(240, 128)] * 2, [], f, k, m, xl, xr), "gy")
    fa, ka, ma, up, down = call(
        pack_z_kernel, [(24, 40, 128)] * 3 + [SIDES] * 2, [], f, k, m, xl, xr, yl, yr
    )
    zl, zr = both_sides(up, down, "gz")
    brick, *level0 = call(
        fine_kernel,
        [(4, 16, 128)] + [FULL] * 6,
        [FULL] * 3 + [(256, 128)],
        fa, ka, ma, zl, zr,
        pos=pos,
    )

    own = gather_x(brick)
    yl, yr = both_sides(own, own, "gy")
    zl, zr = both_sides(*pack_z1(1, own, yl, yr), "gz")
    message, *vary = call(
        middle_kernel,
        [(3, 8, 128)] + [NEAR1] * 2 + [NEAR2] * 2,
        [ONE] * 3 + [TWO] * 3 + [TALL, (96, 128)],
        own, yl, yr, zl, zr, coarsest, *whole,
        pos=pos,
    )

    own = jnp.concatenate([message, *both_sides(message, message, "gz")])
    first, second = (lax.ppermute(own, "gy", list(enumerate(t))) for t in COARSE_TARGETS)
    return call(
        last_kernel,
        [(16, 32, 128)],
        [THREE] * 9 + [(240, 128), (192, 128)] + [NEAR2] * 2 + [NEAR1] * 2
        + [(240, 256), (40, 128), (40, 128)] + [FULL] * 2,
        own, first, second, *level0, *vary, *near,
        pos=pos,
    )[0]


def solution(mesh):
    placed = (P("gx", "gy", "gz"), P("gx", "gy", "gz"), P("gx", "gy", "gz"))
    return jax.shard_map(
        per_device, mesh=mesh, in_specs=placed, out_specs=P("gx", "gy", "gz"), check_vma=False
    )
```

time: 107 us -> 74.6 us (0.70); the launches traced: 105 us -> 74.2 us
  waiting for transfers between devices: 37.4 us -> 16.6 us
  Pallas kernels: 33.6 us -> 17.9 us
  starting transfers between devices: 27.6 us -> 37.6 us
  local copies, waits for them, and re-layouts: 6.14 us -> 1.8 us
    ppermute x12 -> x16, waiting for transfers between devices: 27.6 us -> 6.66 us  [shift(): return lax.ppermute(x, axis, [(i, (i + step) % size) for i in range(size)])]
    pallas_call x6 -> x9, Pallas kernels: 33.6 us -> 17.9 us  [call(): pl.pallas_call(kernel, out_shape=[jax.ShapeDtypeStruct(s, F32) for s in o...]
    ppermute x3 -> x6, starting transfers between devices: 4.12 us -> 9.57 us  [swap(): return lax.ppermute(x, axis, [(i, i ^ bits) for i in range(size)])]
    ppermute x12 -> x16, starting transfers between devices: 18 us -> 22.9 us  [shift(): return lax.ppermute(x, axis, [(i, (i + step) % size) for i in range(size)])]
    unnamed x23 -> x11, local copies, waits for them, and re-layouts: 4.37 us -> 0.03 us
    ppermute x3 -> x6, waiting for transfers between devices: 5.99 us -> 5.05 us  [swap(): return lax.ppermute(x, axis, [(i, i ^ bits) for i in range(size)])]
  transfers between devices with their start and end apart: 17 -> 24, of which waited for: 11 -> 10; matrix products, arithmetic and copies ran while one was open for 0% -> 0% of each run, Pallas kernels for 0% -> 13%
where the time goes in v2:
time: 74.6 us; the launch traced here: 74.2 us
  starting transfers between devices  37.6 us (50%)
  Pallas kernels  17.9 us (24%)
  waiting for transfers between devices  16.6 us (22%)
  local copies, waits for them, and re-layouts  1.8 us (2%)
    ppermute x16, starting transfers between devices, shift(): return lax.ppermute(x, axis, [(i, (i + step) % size) for i in range(size)])  22.9 us
    pallas_call x9, Pallas kernels, call(): pl.pallas_call(kernel, out_shape=[jax.ShapeDtypeStruct(s, F32) for s in o...  17.9 us
    ppermute x6, starting transfers between devices, swap(): return lax.ppermute(x, axis, [(i, i ^ bits) for i in range(size)])  9.57 us
    ppermute x16, waiting for transfers between devices, shift(): return lax.ppermute(x, axis, [(i, (i + step) % size) for i in range(size)])  6.66 us
    ppermute x2, starting transfers between devices, per_device(): lax.ppermute(own, 'gy', list(enumerate(t)))  5.11 us
    ppermute x6, waiting for transfers between devices, swap(): return lax.ppermute(x, axis, [(i, i ^ bits) for i in range(size)])  5.05 us
    ppermute x2, waiting for transfers between devices, per_device(): lax.ppermute(own, 'gy', list(enumerate(t)))  4.85 us
    slice x3, local copies, waits for them, and re-layouts, per_device(): xr = shift(jnp.concatenate([f[:3], m[:3], k[:4]]), 'gx', -1)  1.76 us
  transfers between devices with their start and end apart: 24, of which 10 were waited for; matrix products, arithmetic and copies ran while one was open for 0% of the time, Pallas kernels for 13%

profile of v2, /device:TPU:64, one launch (start us, length us, event | category | flops | bytes accessed | tf_op | source)
XLA Modules:
  0.0 74.2 jit_solution(3363554948824004536)
XLA Ops:
  0.0 0.9 %fusion.2 = (f32[4,32,128]{2,1,0:T(8,128)S(1)}, f32[4,32,128]{2,1,0:T(8,128)S(1)}) fusion(f32[16,32,128]{2,1,0:T(8,128)} %k.5), kind=kLoop, calls=%fused_computation.13 | loop fusion | bytes 262144 | tf_op jit(solution)/shard_map/slice | solution.py:553
  0.9 0.8 %fusion = (f32[3,32,128]{2,1,0:T(8,128)S(1)}, f32[3,32,128]{2,1,0:T(8,128)S(1)}) fusion(f32[16,32,128]{2,1,0:T(8,128)} %f.3), kind=kLoop, calls=%fused_computation.11 | loop fusion | bytes 196608 | tf_op jit(solution)/shard_map/slice | solution.py:553
  1.8 0.0 copy-start
  1.8 0.0 copy-start.2
  1.8 1.7 %collective-permute-start = (f32[10,32,128]{2,1,0:T(8,128)S(1)}, f32[10,32,128]{2,1,0:T(8,128)S(1)}, u32[]{:S(2)}, u32[]{:S(2)}) collective-permute-start(f32[10,32,128]{2,1,0:T(8,128)S(1)} %pad_maximum_fusion.1), channel_id=1, source_target_pairs={{0,64},{64,128},{128,192},{192,0},{1,65},{65,129},{129,193},{193,1... | collective-permute-start | bytes 491528 | tf_op jit(solution)/shard_map/ppermute | solution.py:522
  3.5 1.7 %collective-permute-start.1 = (f32[10,32,128]{2,1,0:T(8,128)S(1)}, f32[10,32,128]{2,1,0:T(8,128)S(1)}, u32[]{:S(2)}, u32[]{:S(2)}) collective-permute-start(f32[10,32,128]{2,1,0:T(8,128)S(1)} %pad_maximum_fusion.2), channel_id=1, source_target_pairs={{0,192},{64,0},{128,64},{192,128},{1,193},{65,1},{129,65},{193,129... | collective-permute-start | bytes 491528 | tf_op jit(solution)/shard_map/ppermute | solution.py:522
  5.2 3.9 %collective-permute-done.xl = f32[10,32,128]{2,1,0:T(8,128)S(1)} collective-permute-done((f32[10,32,128]{2,1,0:T(8,128)S(1)}, f32[10,32,128]{2,1,0:T(8,128)S(1)}, u32[]{:S(2)}, u32[]{:S(2)}) %collective-permute-start) | collective-permute-done | bytes 163872 | tf_op jit(solution)/shard_map/ppermute | solution.py:522
  9.1 0.1 collective-permute-done.1.xr
  9.2 0.1 pack_y_kernel.1
  9.3 2.0 %collective-permute-start.2 = (f32[240,128]{1,0:T(8,128)S(1)}, f32[240,128]{1,0:T(8,128)S(1)}, u32[]{:S(2)}, u32[]{:S(2)}) collective-permute-start(f32[240,128]{1,0:T(8,128)S(1)} %get-tuple-element.47), channel_id=1, source_target_pairs={{0,8},{8,16},{16,24},{24,32},{32,40},{40,48},{48,56},{56,0},{1,9},... | collective-permute-start | bytes 368648 | tf_op jit(solution)/shard_map/ppermute | solution.py:522
  11.3 0.1 collective-permute-start.3
  11.4 0.2 coarse_kernel.1
  11.6 1.7 %collective-permute-start.13 = (f32[8,16,128]{2,1,0:T(8,128)S(1)}, f32[8,16,128]{2,1,0:T(8,128)S(1)}, u32[]{:S(2)}, u32[]{:S(2)}) collective-permute-start(f32[8,16,128]{2,1,0:T(8,128)S(1)} %coarse_kernel.1), channel_id=1, source_target_pairs={{0,64},{64,0},{128,192},{192,128},{1,65},{65,1},{129,193},{193,129... | collective-permute-start | bytes 196616 | tf_op jit(solution)/shard_map/ppermute | solution.py:527
  13.3 2.8 %collective-permute-start.14 = (f32[8,16,128]{2,1,0:T(8,128)S(1)}, f32[8,16,128]{2,1,0:T(8,128)S(1)}, u32[]{:S(2)}, u32[]{:S(2)}) collective-permute-start(f32[8,16,128]{2,1,0:T(8,128)S(1)} %coarse_kernel.1), channel_id=1, source_target_pairs={{0,128},{64,192},{128,0},{192,64},{1,129},{65,193},{129,1},{193,65... | collective-permute-start | bytes 196616 | tf_op jit(solution)/shard_map/ppermute | solution.py:527
  16.1 0.3 collective-permute-start.15
  16.4 0.1 pad_add_fusion.pos
  16.5 0.8 %collective-permute-done.3.yr = f32[240,128]{1,0:T(8,128)S(1)} collective-permute-done((f32[240,128]{1,0:T(8,128)S(1)}, f32[240,128]{1,0:T(8,128)S(1)}, u32[]{:S(2)}, u32[]{:S(2)}) %collective-permute-start.3) | collective-permute-done | bytes 122912 | tf_op jit(solution)/shard_map/ppermute | solution.py:522
  17.3 0.9 %pack_z_kernel.1 = (f32[24,40,128]{2,1,0:T(8,128)S(1)}, f32[24,40,128]{2,1,0:T(8,128)S(1)}, f32[24,40,128]{2,1,0:T(8,128)S(1)}, f32[2,40,128]{2,1,0:T(8,128)S(1)}, f32[2,40,128]{2,1,0:T(8,128)S(1)}) custom-call(f32[16,32,128]{2,1,0:T(8,128)S(1)} %copy-done.2, f32[16,32,128]{2,1,0:T(8,128)S(1)} %copy-done, f32[16,32,128]{2,1,0:T(8,128)S(1)} %copy-done.1, ...), custom_call_target="tpu_custom_call" | custom-call | tf_op jit(solution)/shard_map/pack_z_kernel/pallas_call | solution.py:509
  18.1 0.0 collective-permute-start.4
  18.2 2.9 %collective-permute-start.5 = (f32[2,40,128]{2,1,0:T(8,128)S(1)}, f32[2,40,128]{2,1,0:T(8,128)S(1)}, u32[]{:S(2)}, u32[]{:S(2)}) collective-permute-start(f32[2,40,128]{2,1,0:T(8,128)S(1)} %get-tuple-element.53), channel_id=1, source_target_pairs={{0,7},{1,0},{2,1},{3,2},{4,3},{5,4},{6,5},{7,6},{8,15},{9,8},{10,9... | collective-permute-start | bytes 122888 | tf_op jit(solution)/shard_map/ppermute | solution.py:522
  21.1 0.5 collective-permute-done.15
  21.6 3.1 %collective-permute-start.16 = (f32[32,16,128]{2,1,0:T(8,128)S(1)}, f32[32,16,128]{2,1,0:T(8,128)S(1)}, u32[]{:S(2)}, u32[]{:S(2)}) collective-permute-start(f32[32,16,128]{2,1,0:T(8,128)S(1)} %pad_maximum_fusion.own), channel_id=1, source_target_pairs={{0,8},{8,16},{16,24},{24,32},{32,40},{40,48},{48,56},{56,0},{1,9},... | collective-permute-start | bytes 786440 | tf_op jit(solution)/shard_map/ppermute | solution.py:522
  24.7 0.0 collective-permute-start.17
  24.7 4.2 %fine_kernel.1 = (f32[4,16,128]{2,1,0:T(8,128)S(1)}, f32[24,40,256]{2,1,0:T(8,128)S(1)}, f32[24,40,256]{2,1,0:T(8,128)S(1)}, f32[24,40,256]{2,1,0:T(8,128)S(1)},...) custom-call(s32[3]{0:T(128)S(1)} %pad_add_fusion.pos, ...), custom_call_target="tpu_custom_call" | custom-call | tf_op jit(solution)/shard_map/fine_kernel/pallas_call | solution.py:509
  28.9 1.4 %collective-permute-start.6 = (f32[4,16,128]{2,1,0:T(8,128)S(1)}, f32[4,16,128]{2,1,0:T(8,128)S(1)}, u32[]{:S(2)}, u32[]{:S(2)}) collective-permute-start(f32[4,16,128]{2,1,0:T(8,128)S(1)} %get-tuple-element.54), channel_id=1, source_target_pairs={{0,64},{64,0},{128,192},{192,128},{1,65},{65,1},{129,193},{193,129... | collective-permute-start | bytes 98312 | tf_op jit(solution)/shard_map/ppermute | solution.py:527
  30.4 2.8 %collective-permute-start.7 = (f32[4,16,128]{2,1,0:T(8,128)S(1)}, f32[4,16,128]{2,1,0:T(8,128)S(1)}, u32[]{:S(2)}, u32[]{:S(2)}) collective-permute-start(f32[4,16,128]{2,1,0:T(8,128)S(1)} %get-tuple-element.54), channel_id=1, source_target_pairs={{0,128},{64,192},{128,0},{192,64},{1,129},{65,193},{129,1},{193,65... | collective-permute-start | bytes 98312 | tf_op jit(solution)/shard_map/ppermute | solution.py:527
  33.2 0.5 collective-permute-start.8
  33.7 2.1 %collective-permute-done.7 = f32[4,16,128]{2,1,0:T(8,128)S(1)} collective-permute-done((f32[4,16,128]{2,1,0:T(8,128)S(1)}, f32[4,16,128]{2,1,0:T(8,128)S(1)}, u32[]{:S(2)}, u32[]{:S(2)}) %collective-permute-start.7) | collective-permute-done | bytes 32800 | tf_op jit(solution)/shard_map/ppermute | solution.py:527
  35.8 2.5 %collective-permute-done.8 = f32[4,16,128]{2,1,0:T(8,128)S(1)} collective-permute-done((f32[4,16,128]{2,1,0:T(8,128)S(1)}, f32[4,16,128]{2,1,0:T(8,128)S(1)}, u32[]{:S(2)}, u32[]{:S(2)}) %collective-permute-start.8) | collective-permute-done | bytes 32800 | tf_op jit(solution)/shard_map/ppermute | solution.py:527
  38.3 0.2 collective-permute-start.10
  38.5 2.3 %collective-permute-start.9 = (f32[16,16,128]{2,1,0:T(8,128)S(1)}, f32[16,16,128]{2,1,0:T(8,128)S(1)}, u32[]{:S(2)}, u32[]{:S(2)}) collective-permute-start(f32[16,16,128]{2,1,0:T(8,128)S(1)} %constant_dynamic-update-slice_fusion.own), channel_id=1, source_target_pairs={{0,8},{8,16},{16,24},{24,32},{32,40},{40,48},{48,56},{56,0},{1,9},... | collective-permute-start | bytes 393224 | tf_op jit(solution)/shard_map/ppermute | solution.py:522
  40.8 0.4 pack_z1_kernel.3
  41.2 0.0 collective-permute-start.18
  41.2 2.9 %collective-permute-start.19 = (f32[8,48,128]{2,1,0:T(8,128)S(1)}, f32[8,48,128]{2,1,0:T(8,128)S(1)}, u32[]{:S(2)}, u32[]{:S(2)}) collective-permute-start(f32[8,48,128]{2,1,0:T(8,128)S(1)} %get-tuple-element.58), channel_id=1, source_target_pairs={{0,7},{1,0},{2,1},{3,2},{4,3},{5,4},{6,5},{7,6},{8,15},{9,8},{10,9... | collective-permute-start | bytes 589832 | tf_op jit(solution)/shard_map/ppermute | solution.py:522
  44.2 0.4 collective-permute-done.9.yl
  44.6 0.2 pack_z1_kernel.2
  44.8 0.0 collective-permute-start.11
  44.8 2.9 %collective-permute-start.12 = (f32[4,48,128]{2,1,0:T(8,128)S(1)}, f32[4,48,128]{2,1,0:T(8,128)S(1)}, u32[]{:S(2)}, u32[]{:S(2)}) collective-permute-start(f32[4,48,128]{2,1,0:T(8,128)S(1)} %get-tuple-element.56), channel_id=1, source_target_pairs={{0,7},{1,0},{2,1},{3,2},{4,3},{5,4},{6,5},{7,6},{8,15},{9,8},{10,9... | collective-permute-start | bytes 294920 | tf_op jit(solution)/shard_map/ppermute | solution.py:522
  47.8 3.6 %static_kernel.1 = (f32[2,8,128]{2,1,0:T(8,128)S(1)}, f32[40,48,128]{2,1,0:T(8,128)S(1)}, f32[40,48,128]{2,1,0:T(8,128)S(1)}, f32[40,48,128]{2,1,0:T(8,128)S(1)}...) custom-call(s32[3]{0:T(128)S(1)} %pad_add_fusion.pos, ...), custom_call_target="tpu_custom_call" | custom-call | tf_op jit(solution)/shard_map/static_kernel/pallas_call | solution.py:509
  51.4 3.7 %middle_kernel.1 = (f32[3,8,128]{2,1,0:T(8,128)S(1)}, f32[16,24,128]{2,1,0:T(8,128)S(1)}, f32[16,24,128]{2,1,0:T(8,128)S(1)}, f32[12,16,128]{2,1,0:T(8,128)S(1)}, f32[12,16,128]{2,1,0:T(8,128)S(1)}) custom-call(s32[3]{0:T(128)S(1)} %pad_add_fusion.pos, f32[16,16,128]{2,1,0:T(8,128)S(1)} %constant_dynamic-update-slice_fusion.own, ...), custom_call_target="tpu_custom_call" | custom-call | tf_op jit(solution)/shard_map/middle_kernel/pallas_call | solution.py:509
  55.1 0.0 collective-permute-start.20
  55.1 2.9 %collective-permute-start.21 = (f32[3,8,128]{2,1,0:T(8,128)S(1)}, f32[3,8,128]{2,1,0:T(8,128)S(1)}, u32[]{:S(2)}, u32[]{:S(2)}) collective-permute-start(f32[3,8,128]{2,1,0:T(8,128)S(1)} %get-tuple-element.70), channel_id=1, source_target_pairs={{0,7},{1,0},{2,1},{3,2},{4,3},{5,4},{6,5},{7,6},{8,15},{9,8},{10,9... | collective-permute-start | bytes 36872 | tf_op jit(solution)/shard_map/ppermute | solution.py:522
  58.1 1.4 %collective-permute-done.20 = f32[3,8,128]{2,1,0:T(8,128)S(1)} collective-permute-done((f32[3,8,128]{2,1,0:T(8,128)S(1)}, f32[3,8,128]{2,1,0:T(8,128)S(1)}, u32[]{:S(2)}, u32[]{:S(2)}) %collective-permute-start.20) | collective-permute-done | bytes 12320 | tf_op jit(solution)/shard_map/ppermute | solution.py:522
  59.4 0.0 collective-permute-done.21
  59.5 5.1 %collective-permute-start.22 = (f32[9,8,128]{2,1,0:T(8,128)S(1)}, f32[9,8,128]{2,1,0:T(8,128)S(1)}, u32[]{:S(2)}, u32[]{:S(2)}) collective-permute-start(f32[9,8,128]{2,1,0:T(8,128)S(1)} %constant_dynamic-update-slice_fusion.4.own), channel_id=1, source_target_pairs={{0,8},{8,24},{16,32},{24,40},{32,16},{40,56},{48,0},{56,48},{1,9},... | collective-permute-start | bytes 110600 | tf_op jit(solution)/shard_map/ppermute | solution.py:593
  64.6 1.9 %collective-permute-done.22.first = f32[9,8,128]{2,1,0:T(8,128)S(1)} collective-permute-done((f32[9,8,128]{2,1,0:T(8,128)S(1)}, f32[9,8,128]{2,1,0:T(8,128)S(1)}, u32[]{:S(2)}, u32[]{:S(2)}) %collective-permute-start.22) | collective-permute-done | bytes 36896 | tf_op jit(solution)/shard_map/ppermute | solution.py:593
  66.5 2.9 %collective-permute-done.23.second = f32[9,8,128]{2,1,0:T(8,128)S(1)} collective-permute-done((f32[9,8,128]{2,1,0:T(8,128)S(1)}, f32[9,8,128]{2,1,0:T(8,128)S(1)}, u32[]{:S(2)}, u32[]{:S(2)}) %collective-permute-start.23) | collective-permute-done | bytes 36896 | tf_op jit(solution)/shard_map/ppermute | solution.py:593
  69.4 4.8 %last_kernel.1 = f32[16,32,128]{2,1,0:T(8,128)} custom-call(s32[3]{0:T(128)S(1)} %pad_add_fusion.pos, f32[9,8,128]{2,1,0:T(8,128)S(1)} %constant_dynamic-update-slice_fusion.4.own, f32[9,8,128]{2,1,0:T(8,128)S(1)} %collective-permute-done.22.first, f32[9,8,128]{2,1,0:T(8,128)S(1)} %collective-permute-done.23.second, ...), custom_call_target="tpu_custom_call" | custom-call | tf_op jit(solution)/shard_map/last_kernel/pallas_call | solution.py:509
  (29 shorter events, 0.1 us)
Async XLA Ops:
  0.0 1.8 %copy-start.1 = (f32[16,32,128]{2,1,0:T(8,128)S(1)}, f32[16,32,128]{2,1,0:T(8,128)}, u32[]{:S(2)}) copy-start(f32[16,32,128]{2,1,0:T(8,128)} %m.5) | copy-start | bytes 786436
  1.8 7.5 %copy-start = (f32[16,32,128]{2,1,0:T(8,128)S(1)}, f32[16,32,128]{2,1,0:T(8,128)}, u32[]{:S(2)}) copy-start(f32[16,32,128]{2,1,0:T(8,128)} %k.5) | copy-start | bytes 786436
  1.8 7.4 %copy-start.2 = (f32[16,32,128]{2,1,0:T(8,128)S(1)}, f32[16,32,128]{2,1,0:T(8,128)}, u32[]{:S(2)}) copy-start(f32[16,32,128]{2,1,0:T(8,128)} %f.3) | copy-start | bytes 786436
  1.8 7.3 %collective-permute-start = (f32[10,32,128]{2,1,0:T(8,128)S(1)}, f32[10,32,128]{2,1,0:T(8,128)S(1)}, u32[]{:S(2)}, u32[]{:S(2)}) collective-permute-start(f32[10,32,128]{2,1,0:T(8,128)S(1)} %pad_maximum_fusion.1), channel_id=1, source_target_pairs={{0,64},{64,128},{128,192},{192,0},{1,65},{65,129},{129,193},{193,1... | collective-permute-start | bytes 491528 | tf_op jit(solution)/shard_map/ppermute | solution.py:522
  3.5 5.7 %collective-permute-start.1 = (f32[10,32,128]{2,1,0:T(8,128)S(1)}, f32[10,32,128]{2,1,0:T(8,128)S(1)}, u32[]{:S(2)}, u32[]{:S(2)}) collective-permute-start(f32[10,32,128]{2,1,0:T(8,128)S(1)} %pad_maximum_fusion.2), channel_id=1, source_target_pairs={{0,192},{64,0},{128,64},{192,128},{1,193},{65,1},{129,65},{193,129... | collective-permute-start | bytes 491528 | tf_op jit(solution)/shard_map/ppermute | solution.py:522
  9.3 7.2 %collective-permute-start.2 = (f32[240,128]{1,0:T(8,128)S(1)}, f32[240,128]{1,0:T(8,128)S(1)}, u32[]{:S(2)}, u32[]{:S(2)}) collective-permute-start(f32[240,128]{1,0:T(8,128)S(1)} %get-tuple-element.47), channel_id=1, source_target_pairs={{0,8},{8,16},{16,24},{24,32},{32,40},{40,48},{48,56},{56,0},{1,9},... | collective-permute-start | bytes 368648 | tf_op jit(solution)/shard_map/ppermute | solution.py:522
  11.3 6.0 %collective-permute-start.3 = (f32[240,128]{1,0:T(8,128)S(1)}, f32[240,128]{1,0:T(8,128)S(1)}, u32[]{:S(2)}, u32[]{:S(2)}) collective-permute-start(f32[240,128]{1,0:T(8,128)S(1)} %get-tuple-element.48), channel_id=1, source_target_pairs={{0,56},{8,0},{16,8},{24,16},{32,24},{40,32},{48,40},{56,48},{1,57}... | collective-permute-start | bytes 368648 | tf_op jit(solution)/shard_map/ppermute | solution.py:522
  11.6 9.5 %collective-permute-start.13 = (f32[8,16,128]{2,1,0:T(8,128)S(1)}, f32[8,16,128]{2,1,0:T(8,128)S(1)}, u32[]{:S(2)}, u32[]{:S(2)}) collective-permute-start(f32[8,16,128]{2,1,0:T(8,128)S(1)} %coarse_kernel.1), channel_id=1, source_target_pairs={{0,64},{64,0},{128,192},{192,128},{1,65},{65,1},{129,193},{193,129... | collective-permute-start | bytes 196616 | tf_op jit(solution)/shard_map/ppermute | solution.py:527
  13.3 7.8 %collective-permute-start.14 = (f32[8,16,128]{2,1,0:T(8,128)S(1)}, f32[8,16,128]{2,1,0:T(8,128)S(1)}, u32[]{:S(2)}, u32[]{:S(2)}) collective-permute-start(f32[8,16,128]{2,1,0:T(8,128)S(1)} %coarse_kernel.1), channel_id=1, source_target_pairs={{0,128},{64,192},{128,0},{192,64},{1,129},{65,193},{129,1},{193,65... | collective-permute-start | bytes 196616 | tf_op jit(solution)/shard_map/ppermute | solution.py:527
  16.1 5.5 %collective-permute-start.15 = (f32[8,16,128]{2,1,0:T(8,128)S(1)}, f32[8,16,128]{2,1,0:T(8,128)S(1)}, u32[]{:S(2)}, u32[]{:S(2)}) collective-permute-start(f32[8,16,128]{2,1,0:T(8,128)S(1)} %coarse_kernel.1), channel_id=1, source_target_pairs={{0,192},{64,128},{128,64},{192,0},{1,193},{65,129},{129,65},{193,1... | collective-permute-start | bytes 196616 | tf_op jit(solution)/shard_map/ppermute | solution.py:527
  18.1 6.6 %collective-permute-start.4 = (f32[2,40,128]{2,1,0:T(8,128)S(1)}, f32[2,40,128]{2,1,0:T(8,128)S(1)}, u32[]{:S(2)}, u32[]{:S(2)}) collective-permute-start(f32[2,40,128]{2,1,0:T(8,128)S(1)} %get-tuple-element.52), channel_id=1, source_target_pairs={{0,1},{1,2},{2,3},{3,4},{4,5},{5,6},{6,7},{7,0},{8,9},{9,10},{10,1... | collective-permute-start | bytes 122888 | tf_op jit(solution)/shard_map/ppermute | solution.py:522
  18.2 6.6 %collective-permute-start.5 = (f32[2,40,128]{2,1,0:T(8,128)S(1)}, f32[2,40,128]{2,1,0:T(8,128)S(1)}, u32[]{:S(2)}, u32[]{:S(2)}) collective-permute-start(f32[2,40,128]{2,1,0:T(8,128)S(1)} %get-tuple-element.53), channel_id=1, source_target_pairs={{0,7},{1,0},{2,1},{3,2},{4,3},{5,4},{6,5},{7,6},{8,15},{9,8},{10,9... | collective-permute-start | bytes 122888 | tf_op jit(solution)/shard_map/ppermute | solution.py:522
  21.6 19.2 %collective-permute-start.16 = (f32[32,16,128]{2,1,0:T(8,128)S(1)}, f32[32,16,128]{2,1,0:T(8,128)S(1)}, u32[]{:S(2)}, u32[]{:S(2)}) collective-permute-start(f32[32,16,128]{2,1,0:T(8,128)S(1)} %pad_maximum_fusion.own), channel_id=1, source_target_pairs={{0,8},{8,16},{16,24},{24,32},{32,40},{40,48},{48,56},{56,0},{1,9},... | collective-permute-start | bytes 786440 | tf_op jit(solution)/shard_map/ppermute | solution.py:522
  24.7 16.1 %collective-permute-start.17 = (f32[32,16,128]{2,1,0:T(8,128)S(1)}, f32[32,16,128]{2,1,0:T(8,128)S(1)}, u32[]{:S(2)}, u32[]{:S(2)}) collective-permute-start(f32[32,16,128]{2,1,0:T(8,128)S(1)} %pad_maximum_fusion.own), channel_id=1, source_target_pairs={{0,56},{8,0},{16,8},{24,16},{32,24},{40,32},{48,40},{56,48},{1,57}... | collective-permute-start | bytes 786440 | tf_op jit(solution)/shard_map/ppermute | solution.py:522
  28.9 4.8 %collective-permute-start.6 = (f32[4,16,128]{2,1,0:T(8,128)S(1)}, f32[4,16,128]{2,1,0:T(8,128)S(1)}, u32[]{:S(2)}, u32[]{:S(2)}) collective-permute-start(f32[4,16,128]{2,1,0:T(8,128)S(1)} %get-tuple-element.54), channel_id=1, source_target_pairs={{0,64},{64,0},{128,192},{192,128},{1,65},{65,1},{129,193},{193,129... | collective-permute-start | bytes 98312 | tf_op jit(solution)/shard_map/ppermute | solution.py:527
  30.4 5.5 %collective-permute-start.7 = (f32[4,16,128]{2,1,0:T(8,128)S(1)}, f32[4,16,128]{2,1,0:T(8,128)S(1)}, u32[]{:S(2)}, u32[]{:S(2)}) collective-permute-start(f32[4,16,128]{2,1,0:T(8,128)S(1)} %get-tuple-element.54), channel_id=1, source_target_pairs={{0,128},{64,192},{128,0},{192,64},{1,129},{65,193},{129,1},{193,65... | collective-permute-start | bytes 98312 | tf_op jit(solution)/shard_map/ppermute | solution.py:527
  33.2 5.1 %collective-permute-start.8 = (f32[4,16,128]{2,1,0:T(8,128)S(1)}, f32[4,16,128]{2,1,0:T(8,128)S(1)}, u32[]{:S(2)}, u32[]{:S(2)}) collective-permute-start(f32[4,16,128]{2,1,0:T(8,128)S(1)} %get-tuple-element.54), channel_id=1, source_target_pairs={{0,192},{64,128},{128,64},{192,0},{1,193},{65,129},{129,65},{193,1... | collective-permute-start | bytes 98312 | tf_op jit(solution)/shard_map/ppermute | solution.py:527
  38.3 5.8 %collective-permute-start.10 = (f32[16,16,128]{2,1,0:T(8,128)S(1)}, f32[16,16,128]{2,1,0:T(8,128)S(1)}, u32[]{:S(2)}, u32[]{:S(2)}) collective-permute-start(f32[16,16,128]{2,1,0:T(8,128)S(1)} %constant_dynamic-update-slice_fusion.own), channel_id=1, source_target_pairs={{0,56},{8,0},{16,8},{24,16},{32,24},{40,32},{48,40},{56,48},{1,57}... | collective-permute-start | bytes 393224 | tf_op jit(solution)/shard_map/ppermute | solution.py:522
  38.5 6.1 %collective-permute-start.9 = (f32[16,16,128]{2,1,0:T(8,128)S(1)}, f32[16,16,128]{2,1,0:T(8,128)S(1)}, u32[]{:S(2)}, u32[]{:S(2)}) collective-permute-start(f32[16,16,128]{2,1,0:T(8,128)S(1)} %constant_dynamic-update-slice_fusion.own), channel_id=1, source_target_pairs={{0,8},{8,16},{16,24},{24,32},{32,40},{40,48},{48,56},{56,0},{1,9},... | collective-permute-start | bytes 393224 | tf_op jit(solution)/shard_map/ppermute | solution.py:522
  41.2 6.6 %collective-permute-start.18 = (f32[8,48,128]{2,1,0:T(8,128)S(1)}, f32[8,48,128]{2,1,0:T(8,128)S(1)}, u32[]{:S(2)}, u32[]{:S(2)}) collective-permute-start(f32[8,48,128]{2,1,0:T(8,128)S(1)} %get-tuple-element.57), channel_id=1, source_target_pairs={{0,1},{1,2},{2,3},{3,4},{4,5},{5,6},{6,7},{7,0},{8,9},{9,10},{10,1... | collective-permute-start | bytes 589832 | tf_op jit(solution)/shard_map/ppermute | solution.py:522
  41.2 6.6 %collective-permute-start.19 = (f32[8,48,128]{2,1,0:T(8,128)S(1)}, f32[8,48,128]{2,1,0:T(8,128)S(1)}, u32[]{:S(2)}, u32[]{:S(2)}) collective-permute-start(f32[8,48,128]{2,1,0:T(8,128)S(1)} %get-tuple-element.58), channel_id=1, source_target_pairs={{0,7},{1,0},{2,1},{3,2},{4,3},{5,4},{6,5},{7,6},{8,15},{9,8},{10,9... | collective-permute-start | bytes 589832 | tf_op jit(solution)/shard_map/ppermute | solution.py:522
  44.8 6.6 %collective-permute-start.11 = (f32[4,48,128]{2,1,0:T(8,128)S(1)}, f32[4,48,128]{2,1,0:T(8,128)S(1)}, u32[]{:S(2)}, u32[]{:S(2)}) collective-permute-start(f32[4,48,128]{2,1,0:T(8,128)S(1)} %get-tuple-element.55), channel_id=1, source_target_pairs={{0,1},{1,2},{2,3},{3,4},{4,5},{5,6},{6,7},{7,0},{8,9},{9,10},{10,1... | collective-permute-start | bytes 294920 | tf_op jit(solution)/shard_map/ppermute | solution.py:522
  44.8 6.6 %collective-permute-start.12 = (f32[4,48,128]{2,1,0:T(8,128)S(1)}, f32[4,48,128]{2,1,0:T(8,128)S(1)}, u32[]{:S(2)}, u32[]{:S(2)}) collective-permute-start(f32[4,48,128]{2,1,0:T(8,128)S(1)} %get-tuple-element.56), channel_id=1, source_target_pairs={{0,7},{1,0},{2,1},{3,2},{4,3},{5,4},{6,5},{7,6},{8,15},{9,8},{10,9... | collective-permute-start | bytes 294920 | tf_op jit(solution)/shard_map/ppermute | solution.py:522
  55.1 4.3 %collective-permute-start.20 = (f32[3,8,128]{2,1,0:T(8,128)S(1)}, f32[3,8,128]{2,1,0:T(8,128)S(1)}, u32[]{:S(2)}, u32[]{:S(2)}) collective-permute-start(f32[3,8,128]{2,1,0:T(8,128)S(1)} %get-tuple-element.70), channel_id=1, source_target_pairs={{0,1},{1,2},{2,3},{3,4},{4,5},{5,6},{6,7},{7,0},{8,9},{9,10},{10,1... | collective-permute-start | bytes 36872 | tf_op jit(solution)/shard_map/ppermute | solution.py:522
  55.1 4.3 %collective-permute-start.21 = (f32[3,8,128]{2,1,0:T(8,128)S(1)}, f32[3,8,128]{2,1,0:T(8,128)S(1)}, u32[]{:S(2)}, u32[]{:S(2)}) collective-permute-start(f32[3,8,128]{2,1,0:T(8,128)S(1)} %get-tuple-element.70), channel_id=1, source_target_pairs={{0,7},{1,0},{2,1},{3,2},{4,3},{5,4},{6,5},{7,6},{8,15},{9,8},{10,9... | collective-permute-start | bytes 36872 | tf_op jit(solution)/shard_map/ppermute | solution.py:522
  59.5 7.0 %collective-permute-start.22 = (f32[9,8,128]{2,1,0:T(8,128)S(1)}, f32[9,8,128]{2,1,0:T(8,128)S(1)}, u32[]{:S(2)}, u32[]{:S(2)}) collective-permute-start(f32[9,8,128]{2,1,0:T(8,128)S(1)} %constant_dynamic-update-slice_fusion.4.own), channel_id=1, source_target_pairs={{0,8},{8,24},{16,32},{24,40},{32,16},{40,56},{48,0},{56,48},{1,9},... | collective-permute-start | bytes 110600 | tf_op jit(solution)/shard_map/ppermute | solution.py:593
  64.6 4.9 %collective-permute-start.23 = (f32[9,8,128]{2,1,0:T(8,128)S(1)}, f32[9,8,128]{2,1,0:T(8,128)S(1)}, u32[]{:S(2)}, u32[]{:S(2)}) collective-permute-start(f32[9,8,128]{2,1,0:T(8,128)S(1)} %constant_dynamic-update-slice_fusion.4.own), channel_id=1, source_target_pairs={{0,16},{8,56},{16,0},{24,8},{32,48},{40,24},{48,32},{56,40},{1,17}... | collective-permute-start | bytes 110600 | tf_op jit(solution)/shard_map/ppermute | solution.py:593

commit v3 on v2

--- a/solution.py
+++ b/solution.py
@@ -104,27 +104,36 @@
     planes(low, high, values, store, group)
 
 
+def reach(p):
+    away = max(0, 4 - p, p - 19)
+    return max(0, 3 - away), 4 - away
+
+
+def row_table():
+    table, base = [], 0
+    for p in range(24):
+        three, four = reach(p)
+        table.append((base, base + three, base + 2 * three))
+        base += 2 * three + four
+    return table, base
+
+
+ROWS, ROW_COUNT = row_table()
+
+
 def pack_y_kernel(f, k, m, xl, xr, up, down):
     for p in range(24):
-        for out, lo3, lo4 in ((up, 29, 28), (down, 0, 0)):
-            base = 10 * p
-            if p < 4:
-                kk = xl[6 + p, lo4 : lo4 + 4]
-            elif p < 20:
-                kk = k[p - 4, lo4 : lo4 + 4]
-            else:
-                kk = xr[6 + p - 20, lo4 : lo4 + 4]
-            if 1 <= p < 4:
-                ff, mm = xl[p - 1, lo3 : lo3 + 3], xl[2 + p, lo3 : lo3 + 3]
-            elif 4 <= p < 20:
-                ff, mm = f[p - 4, lo3 : lo3 + 3], m[p - 4, lo3 : lo3 + 3]
-            elif 20 <= p < 23:
-                ff, mm = xr[p - 20, lo3 : lo3 + 3], xr[p - 17, lo3 : lo3 + 3]
-            else:
-                ff = mm = jnp.zeros((3, 128), F32)
-            out[base : base + 3] = ff
-            out[base + 3 : base + 6] = mm
-            out[base + 6 : base + 10] = kk
+        if p < 4:
+            refs = ((xl, p - 1), (xl, 2 + p), (xl, 6 + p))
+        elif p < 20:
+            refs = ((f, p - 4), (m, p - 4), (k, p - 4))
+        else:
+            refs = ((xr, p - 20), (xr, p - 17), (xr, p - 14))
+        for a, (ref, plane) in enumerate(refs):
+            count, base = reach(p)[a // 2], ROWS[p][a]
+            if count:
+                up[base : base + count] = ref[plane, 32 - count : 32]
+                down[base : base + count] = ref[plane, 0:count]
 
 
 def pack_z_kernel(f, k, m, xl, xr, yl, yr, fa, ka, ma, up, down):
@@ -135,7 +144,6 @@
         acc_down = jnp.zeros((40, 128), F32)
         for i in range(12):
             p = 12 * g + i
-            base = 10 * p
             if p < 4:
                 own = (xl[p - 1] if p else zero, xl[2 + p] if p else zero, xl[6 + p])
             elif p < 20:
@@ -143,12 +151,14 @@
             else:
                 own = (xr[p - 20] if p < 23 else zero, xr[p - 17] if p < 23 else zero, xr[p - 14])
             for a, out in enumerate((fa, ma, ka)):
-                width = 4 if a == 2 else 3
+                count, base = reach(p)[a // 2], ROWS[p][a]
                 out[p, 0:32] = own[a]
                 out[p, 32:40] = jnp.zeros((8, 128), F32)
-                out[p, 32 : 32 + width] = yr[base + 3 * a : base + 3 * a + width]
-                out[p, 40 - width : 40] = yl[base + 3 * a : base + 3 * a + width]
+                if count:
+                    out[p, 32 : 32 + count] = yr[base : base + count]
+                    out[p, 40 - count : 40] = yl[base : base + count]
                 whole = out[p]
+                width = 4 if a == 2 else 3
                 first = 10 * i + 3 * a
                 mask = (lane >= first) & (lane < first + width)
                 acc_up = jnp.where(mask, roll(whole, first - (128 - width), 1), acc_up)
@@ -185,7 +195,6 @@
     lane = iota((40, 128), 1)
     far = ((row >= 32) & (row < 36) & (iy == 7)) | ((row >= 36) & (iy == 0))
     beside = ((lane < 4) & (iz < 7)) | ((lane >= 124) & (iz > 0))
-    row_inner = (row < 35) | (row > 36)
     inner = (lane < 3) | (lane > 124)
     for p in range(24):
         group, i = p // 12, p % 12
@@ -195,6 +204,8 @@
         elif p >= 20:
             absent = ix == 3
         gone = far | absent
+        three = reach(p)[0]
+        unknown = (row >= 32 + three) & (row < 40 - three)
         for a, (src, out) in enumerate(((fa, f), (ma, m), (ka, k))):
             width = 4 if a == 2 else 3
             first = 10 * i + 3 * a
@@ -210,7 +221,7 @@
                 here, there = gone, gone | ~beside
                 own, side = 0.5 * own, 0.5 * side
             else:
-                here = gone | ~row_inner
+                here = gone | unknown
                 there = here | ~(beside & inner)
             out[p, :, 0:128] = jnp.where(here, fill, own)
             out[p, :, 128:256] = jnp.where(there, fill, side)
@@ -259,10 +270,10 @@
     return gone | ((lane >= 80) & (lane < 112))
 
 
-def spread1(ix, gone, own, yl, yr, zl, zr, count, a, out, fill, scale):
+def spread1(ix, gone, own, yl, yr, zl, zr, order, count, a, out, fill, scale):
     lane = iota((48, 128), 1)
     for b in range(4):
-        block = 8 * jnp.bitwise_xor(ix, b) + 4
+        block = 8 * jnp.bitwise_xor(ix, order[b]) + 4
         left, right = zl[count * b + a], zr[count * b + a]
         for q in range(4):
             s = 4 * (count * b + a) + q
@@ -328,8 +339,8 @@
     gone = outside1(iy, iz)
     clear((k1, w1, cy1, cz1), 4, 36)
     clear((k2, w2, cy2, cz2), 4, 20)
-    spread1(ix, gone, own, yl, yr, zl, zr, 2, 0, m1, OUTSIDE, 1.0)
-    spread1(ix, gone, own, yl, yr, zl, zr, 2, 1, k1, 0.0, 0.125)
+    spread1(ix, gone, own, yl, yr, zl, zr, (0, 1, 2, 3), 2, 0, m1, OUTSIDE, 1.0)
+    spread1(ix, gone, own, yl, yr, zl, zr, (0, 1, 2, 3), 2, 1, k1, 0.0, 0.125)
     coefficients(4, 36, 8, k1, None, m1, d1, w1, None, cy1, cz1)
     to_second(tall, m2, lambda p: m1[p], OUTSIDE)
     to_second(tall, k2, lambda p: 0.25 * k1[p], 0.0)
@@ -358,7 +369,7 @@
     gone = outside1(iy, iz)
     clear((g1, v1), 4, 36)
     clear((g2, v2), 4, 20)
-    spread1(ix, gone, own, yl, yr, zl, zr, 1, 0, f1, 0.0, 1.0)
+    spread1(ix, gone, own, yl, yr, zl, zr, (0, 1, 2, 3), 1, 0, f1, 0.0, 1.0)
 
     def weigh(low, high, w, f, g):
         def store(p, value):
@@ -412,7 +423,7 @@
     gone = (row < 0) | (row >= 32) | ((lane >= 32) & (lane < 112))
     gone = gone | ((lane >= 16) & (lane < 32) & (iz == 7)) | ((lane >= 112) & (iz == 0))
     clear((k3, g3, a3, b3), 2, 10)
-    crossed = (iy == 2) | (iy == 6)
+    crossed = (iy // 2) % 2 == 0
 
     def stack(index):
         one, two = first[index], second[index]
@@ -498,7 +509,7 @@
 SMEM = pl.BlockSpec(memory_space=pltpu.SMEM)
 
 
-COARSE_TARGETS = ((1, 3, 4, 5, 2, 7, 0, 6), (2, 7, 0, 1, 6, 3, 4, 5))
+COARSE_TARGETS = ((2, 3, 0, 1, 6, 7, 4, 5), (1, 0, 4, 5, 2, 3, 7, 6))
 
 
 def call(kernel, outs, scratch, *args, pos=None):
@@ -537,6 +548,11 @@
     return jnp.concatenate([x] + [swap(x, "gx", bits) for bits in (1, 2, 3)])
 
 
+def gather_x_pairs(x):
+    pair = jnp.concatenate([x, swap(x, "gx", 1)])
+    return jnp.concatenate([pair, swap(pair, "gx", 3)])
+
+
 def both_sides(up, down, axis):
     return shift(up, axis, 1), shift(down, axis, -1)
 
@@ -546,30 +562,28 @@
     return call(kernel, [(4 * count, 48, 128)] * 2, [], own, yl, yr)
 
 
+def ordered(x, *others):
+    return lax.optimization_barrier((x, *others))[0]
+
+
 def per_device(f, k, m):
     pos = jnp.stack([lax.axis_index("gx"), lax.axis_index("gy"), lax.axis_index("gz")])
     pos = pos.astype(jnp.int32)
-    xl = shift(jnp.concatenate([f[13:], m[13:], k[12:]]), "gx", 1)
-    xr = shift(jnp.concatenate([f[:3], m[:3], k[:4]]), "gx", -1)
-
-    (brick,) = call(coarse_kernel, [(8, 16, 128)], [(256, 128)], k, m)
-    own = gather_x(brick)
-    yl, yr = both_sides(own, own, "gy")
-    zl, zr = both_sides(*pack_z1(2, own, yl, yr), "gz")
-    coarsest, *static = call(
-        static_kernel,
-        [(2, 8, 128)] + [ONE] * 5 + [TWO] * 5 + [NEAR1] * 4 + [NEAR2] * 4,
-        [ONE, TWO, TALL, (96, 128)],
-        own, yl, yr, zl, zr,
-        pos=pos,
-    )
-    whole, near = static[:10], static[10:]
-
-    yl, yr = both_sides(*call(pack_y_kernel, [(240, 128)] * 2, [], f, k, m, xl, xr), "gy")
+
+    up = jnp.concatenate([f[13:], m[13:], k[12:]])
+    down = jnp.concatenate([f[:3], m[:3], k[:4]])
+    xl, xr = both_sides(up, down, "gx")
+    (brick,) = call(
+        coarse_kernel, [(8, 16, 128)], [(256, 128)], k, m
+    )
+    static = gather_x(brick)
+
+    yl, yr = both_sides(*call(pack_y_kernel, [(ROW_COUNT, 128)] * 2, [], f, k, m, xl, xr), "gy")
     fa, ka, ma, up, down = call(
         pack_z_kernel, [(24, 40, 128)] * 3 + [SIDES] * 2, [], f, k, m, xl, xr, yl, yr
     )
     zl, zr = both_sides(up, down, "gz")
+    static_yl, static_yr = both_sides(static, static, "gy")
     brick, *level0 = call(
         fine_kernel,
         [(4, 16, 128)] + [FULL] * 6,
@@ -577,10 +591,21 @@
         fa, ka, ma, zl, zr,
         pos=pos,
     )
+    static_up, static_down = pack_z1(2, static, static_yl, static_yr)
 
     own = gather_x(brick)
+    static_zl, static_zr = both_sides(static_up, static_down, "gz")
+    coarsest, *static = call(
+        static_kernel,
+        [(2, 8, 128)] + [ONE] * 5 + [TWO] * 5 + [NEAR1] * 4 + [NEAR2] * 4,
+        [ONE, TWO, TALL, (96, 128)],
+        static, static_yl, static_yr, static_zl, static_zr,
+        pos=pos,
+    )
+    whole, near = static[:10], static[10:]
     yl, yr = both_sides(own, own, "gy")
-    zl, zr = both_sides(*pack_z1(1, own, yl, yr), "gz")
+    up, down = pack_z1(1, own, yl, yr)
+    zl, zr = both_sides(up, down, "gz")
     message, *vary = call(
         middle_kernel,
         [(3, 8, 128)] + [NEAR1] * 2 + [NEAR2] * 2,

time: 74.6 us -> 73.3 us (0.983)
  waiting for transfers between devices: 16.6 us -> 15.4 us
    ppermute x6, waiting for transfers between devices: 5.05 us -> 3.76 us  [swap(): return lax.ppermute(x, axis, [(i, i ^ bits) for i in range(size)])]
    ppermute x16, waiting for transfers between devices: 6.66 us -> 7.46 us  [shift(): return lax.ppermute(x, axis, [(i, (i + step) % size) for i in range(size)])]
where the time goes in v3:
time: 73.3 us; the launch traced here: 73.1 us
  starting transfers between devices  37.7 us (51%)
  Pallas kernels  17.9 us (24%)
  waiting for transfers between devices  15.4 us (21%)
  local copies, waits for them, and re-layouts  1.8 us (2%)
    ppermute x16, starting transfers between devices, shift(): return lax.ppermute(x, axis, [(i, (i + step) % size) for i in range(size)])  22.9 us
    pallas_call x9, Pallas kernels, call(): pl.pallas_call(kernel, out_shape=[jax.ShapeDtypeStruct(s, F32) for s in o...  17.9 us
    ppermute x6, starting transfers between devices, swap(): return lax.ppermute(x, axis, [(i, i ^ bits) for i in range(size)])  9.57 us
    ppermute x16, waiting for transfers between devices, shift(): return lax.ppermute(x, axis, [(i, (i + step) % size) for i in range(size)])  7.46 us
    ppermute x2, starting transfers between devices, per_device(): lax.ppermute(own, 'gy', list(enumerate(t)))  5.23 us
    ppermute x2, waiting for transfers between devices, per_device(): lax.ppermute(own, 'gy', list(enumerate(t)))  4.19 us
    ppermute x6, waiting for transfers between devices, swap(): return lax.ppermute(x, axis, [(i, i ^ bits) for i in range(size)])  3.76 us
    slice x3, local copies, waits for them, and re-layouts, per_device(): down = jnp.concatenate([f[:3], m[:3], k[:4]])  1.76 us
  transfers between devices with their start and end apart: 24, of which 10 were waited for; matrix products, arithmetic and copies ran while one was open for 0% of the time, Pallas kernels for 13%

profile of v3, /device:TPU:64, one launch (start us, length us, event | category | flops | bytes accessed | tf_op | source)
XLA Modules:
  0.0 73.1 jit_solution(722380724624334826)
XLA Ops:
  0.0 0.9 %fusion.2 = (f32[4,32,128]{2,1,0:T(8,128)S(1)}, f32[4,32,128]{2,1,0:T(8,128)S(1)}) fusion(f32[16,32,128]{2,1,0:T(8,128)} %k.5), kind=kLoop, calls=%fused_computation.13 | loop fusion | bytes 262144 | tf_op jit(solution)/shard_map/slice | solution.py:574
  0.9 0.8 %fusion = (f32[3,32,128]{2,1,0:T(8,128)S(1)}, f32[3,32,128]{2,1,0:T(8,128)S(1)}) fusion(f32[16,32,128]{2,1,0:T(8,128)} %f.3), kind=kLoop, calls=%fused_computation.11 | loop fusion | bytes 196608 | tf_op jit(solution)/shard_map/slice | solution.py:574
  1.8 0.0 copy-start
  1.8 1.7 %collective-permute-start = (f32[10,32,128]{2,1,0:T(8,128)S(1)}, f32[10,32,128]{2,1,0:T(8,128)S(1)}, u32[]{:S(2)}, u32[]{:S(2)}) collective-permute-start(f32[10,32,128]{2,1,0:T(8,128)S(1)} %pad_maximum_fusion.1), channel_id=1, source_target_pairs={{0,64},{64,128},{128,192},{192,0},{1,65},{65,129},{129,193},{193,1... | collective-permute-start | bytes 491528 | tf_op jit(solution)/shard_map/ppermute | solution.py:533
  3.5 0.0 copy-start.2
  3.5 1.7 %collective-permute-start.1 = (f32[10,32,128]{2,1,0:T(8,128)S(1)}, f32[10,32,128]{2,1,0:T(8,128)S(1)}, u32[]{:S(2)}, u32[]{:S(2)}) collective-permute-start(f32[10,32,128]{2,1,0:T(8,128)S(1)} %pad_maximum_fusion.2), channel_id=1, source_target_pairs={{0,192},{64,0},{128,64},{192,128},{1,193},{65,1},{129,65},{193,129... | collective-permute-start | bytes 491528 | tf_op jit(solution)/shard_map/ppermute | solution.py:533
  5.2 0.2 coarse_kernel.1
  5.5 0.5 collective-permute-start.13
  5.9 2.9 %collective-permute-start.14 = (f32[8,16,128]{2,1,0:T(8,128)S(1)}, f32[8,16,128]{2,1,0:T(8,128)S(1)}, u32[]{:S(2)}, u32[]{:S(2)}) collective-permute-start(f32[8,16,128]{2,1,0:T(8,128)S(1)} %coarse_kernel.1), channel_id=1, source_target_pairs={{0,128},{64,192},{128,0},{192,64},{1,129},{65,193},{129,1},{193,65... | collective-permute-start | bytes 196616 | tf_op jit(solution)/shard_map/ppermute | solution.py:538
  8.8 1.4 %collective-permute-start.15 = (f32[8,16,128]{2,1,0:T(8,128)S(1)}, f32[8,16,128]{2,1,0:T(8,128)S(1)}, u32[]{:S(2)}, u32[]{:S(2)}) collective-permute-start(f32[8,16,128]{2,1,0:T(8,128)S(1)} %coarse_kernel.1), channel_id=1, source_target_pairs={{0,192},{64,128},{128,64},{192,0},{1,193},{65,129},{129,65},{193,1... | collective-permute-start | bytes 196616 | tf_op jit(solution)/shard_map/ppermute | solution.py:538
  10.3 0.4 collective-permute-done.1.xr
  10.7 2.0 %collective-permute-start.2 = (f32[184,128]{1,0:T(8,128)S(1)}, f32[184,128]{1,0:T(8,128)S(1)}, u32[]{:S(2)}, u32[]{:S(2)}) collective-permute-start(f32[184,128]{1,0:T(8,128)S(1)} %get-tuple-element.47), channel_id=1, source_target_pairs={{0,8},{8,16},{16,24},{24,32},{32,40},{40,48},{48,56},{56,0},{1,9},... | collective-permute-start | bytes 282632 | tf_op jit(solution)/shard_map/ppermute | solution.py:533
  12.7 0.1 collective-permute-start.3
  12.8 0.1 pad_add_fusion.pos
  12.9 2.5 %collective-permute-done.2.yl = f32[184,128]{1,0:T(8,128)S(1)} collective-permute-done((f32[184,128]{1,0:T(8,128)S(1)}, f32[184,128]{1,0:T(8,128)S(1)}, u32[]{:S(2)}, u32[]{:S(2)}) %collective-permute-start.2) | collective-permute-done | bytes 94240 | tf_op jit(solution)/shard_map/ppermute | solution.py:533
  15.3 3.0 %collective-permute-done.3.yr = f32[184,128]{1,0:T(8,128)S(1)} collective-permute-done((f32[184,128]{1,0:T(8,128)S(1)}, f32[184,128]{1,0:T(8,128)S(1)}, u32[]{:S(2)}, u32[]{:S(2)}) %collective-permute-start.3) | collective-permute-done | bytes 94240 | tf_op jit(solution)/shard_map/ppermute | solution.py:533
  18.4 0.8 %pack_z_kernel.1 = (f32[24,40,128]{2,1,0:T(8,128)S(1)}, f32[24,40,128]{2,1,0:T(8,128)S(1)}, f32[24,40,128]{2,1,0:T(8,128)S(1)}, f32[2,40,128]{2,1,0:T(8,128)S(1)}, f32[2,40,128]{2,1,0:T(8,128)S(1)}) custom-call(f32[16,32,128]{2,1,0:T(8,128)S(1)} %copy-done.2, f32[16,32,128]{2,1,0:T(8,128)S(1)} %copy-done, f32[16,32,128]{2,1,0:T(8,128)S(1)} %copy-done.1, ...), custom_call_target="tpu_custom_call" | custom-call | tf_op jit(solution)/shard_map/pack_z_kernel/pallas_call | solution.py:520
  19.2 0.0 collective-permute-start.4
  19.2 2.9 %collective-permute-start.5 = (f32[2,40,128]{2,1,0:T(8,128)S(1)}, f32[2,40,128]{2,1,0:T(8,128)S(1)}, u32[]{:S(2)}, u32[]{:S(2)}) collective-permute-start(f32[2,40,128]{2,1,0:T(8,128)S(1)} %get-tuple-element.53), channel_id=1, source_target_pairs={{0,7},{1,0},{2,1},{3,2},{4,3},{5,4},{6,5},{7,6},{8,15},{9,8},{10,9... | collective-permute-start | bytes 122888 | tf_op jit(solution)/shard_map/ppermute | solution.py:533
  22.2 0.0 collective-permute-done.13
  22.2 0.0 collective-permute-done.14
  22.2 0.0 collective-permute-done.15
  22.2 3.3 %collective-permute-start.16 = (f32[32,16,128]{2,1,0:T(8,128)S(1)}, f32[32,16,128]{2,1,0:T(8,128)S(1)}, u32[]{:S(2)}, u32[]{:S(2)}) collective-permute-start(f32[32,16,128]{2,1,0:T(8,128)S(1)} %pad_maximum_fusion.own), channel_id=1, source_target_pairs={{0,8},{8,16},{16,24},{24,32},{32,40},{40,48},{48,56},{56,0},{1,9},... | collective-permute-start | bytes 786440 | tf_op jit(solution)/shard_map/ppermute | solution.py:533
  25.5 4.2 %fine_kernel.1 = (f32[4,16,128]{2,1,0:T(8,128)S(1)}, f32[24,40,256]{2,1,0:T(8,128)S(1)}, f32[24,40,256]{2,1,0:T(8,128)S(1)}, f32[24,40,256]{2,1,0:T(8,128)S(1)},...) custom-call(s32[3]{0:T(128)S(1)} %pad_add_fusion.pos, ...), custom_call_target="tpu_custom_call" | custom-call | tf_op jit(solution)/shard_map/fine_kernel/pallas_call | solution.py:520
  29.7 0.7 %collective-permute-start.6 = (f32[4,16,128]{2,1,0:T(8,128)S(1)}, f32[4,16,128]{2,1,0:T(8,128)S(1)}, u32[]{:S(2)}, u32[]{:S(2)}) collective-permute-start(f32[4,16,128]{2,1,0:T(8,128)S(1)} %get-tuple-element.54), channel_id=1, source_target_pairs={{0,64},{64,0},{128,192},{192,128},{1,65},{65,1},{129,193},{193,129... | collective-permute-start | bytes 98312 | tf_op jit(solution)/shard_map/ppermute | solution.py:538
  30.5 2.7 %collective-permute-start.7 = (f32[4,16,128]{2,1,0:T(8,128)S(1)}, f32[4,16,128]{2,1,0:T(8,128)S(1)}, u32[]{:S(2)}, u32[]{:S(2)}) collective-permute-start(f32[4,16,128]{2,1,0:T(8,128)S(1)} %get-tuple-element.54), channel_id=1, source_target_pairs={{0,128},{64,192},{128,0},{192,64},{1,129},{65,193},{129,1},{193,65... | collective-permute-start | bytes 98312 | tf_op jit(solution)/shard_map/ppermute | solution.py:538
  33.2 1.4 %collective-permute-start.8 = (f32[4,16,128]{2,1,0:T(8,128)S(1)}, f32[4,16,128]{2,1,0:T(8,128)S(1)}, u32[]{:S(2)}, u32[]{:S(2)}) collective-permute-start(f32[4,16,128]{2,1,0:T(8,128)S(1)} %get-tuple-element.54), channel_id=1, source_target_pairs={{0,192},{64,128},{128,64},{192,0},{1,193},{65,129},{129,65},{193,1... | collective-permute-start | bytes 98312 | tf_op jit(solution)/shard_map/ppermute | solution.py:538
  34.5 1.4 %collective-permute-done.7 = f32[4,16,128]{2,1,0:T(8,128)S(1)} collective-permute-done((f32[4,16,128]{2,1,0:T(8,128)S(1)}, f32[4,16,128]{2,1,0:T(8,128)S(1)}, u32[]{:S(2)}, u32[]{:S(2)}) %collective-permute-start.7) | collective-permute-done | bytes 32800 | tf_op jit(solution)/shard_map/ppermute | solution.py:538
  35.9 2.4 %collective-permute-done.8 = f32[4,16,128]{2,1,0:T(8,128)S(1)} collective-permute-done((f32[4,16,128]{2,1,0:T(8,128)S(1)}, f32[4,16,128]{2,1,0:T(8,128)S(1)}, u32[]{:S(2)}, u32[]{:S(2)}) %collective-permute-start.8) | collective-permute-done | bytes 32800 | tf_op jit(solution)/shard_map/ppermute | solution.py:538
  38.3 2.3 %collective-permute-start.9 = (f32[16,16,128]{2,1,0:T(8,128)S(1)}, f32[16,16,128]{2,1,0:T(8,128)S(1)}, u32[]{:S(2)}, u32[]{:S(2)}) collective-permute-start(f32[16,16,128]{2,1,0:T(8,128)S(1)} %constant_dynamic-update-slice_fusion.own), channel_id=1, source_target_pairs={{0,8},{8,16},{16,24},{24,32},{32,40},{40,48},{48,56},{56,0},{1,9},... | collective-permute-start | bytes 393224 | tf_op jit(solution)/shard_map/ppermute | solution.py:533
  40.6 0.4 pack_z1_kernel.3
  40.9 0.0 collective-permute-start.18
  41.0 2.9 %collective-permute-start.19 = (f32[8,48,128]{2,1,0:T(8,128)S(1)}, f32[8,48,128]{2,1,0:T(8,128)S(1)}, u32[]{:S(2)}, u32[]{:S(2)}) collective-permute-start(f32[8,48,128]{2,1,0:T(8,128)S(1)} %get-tuple-element.58), channel_id=1, source_target_pairs={{0,7},{1,0},{2,1},{3,2},{4,3},{5,4},{6,5},{7,6},{8,15},{9,8},{10,9... | collective-permute-start | bytes 589832 | tf_op jit(solution)/shard_map/ppermute | solution.py:533
  43.9 0.2 pack_z1_kernel.2
  44.1 0.0 collective-permute-start.11
  44.2 2.9 %collective-permute-start.12 = (f32[4,48,128]{2,1,0:T(8,128)S(1)}, f32[4,48,128]{2,1,0:T(8,128)S(1)}, u32[]{:S(2)}, u32[]{:S(2)}) collective-permute-start(f32[4,48,128]{2,1,0:T(8,128)S(1)} %get-tuple-element.56), channel_id=1, source_target_pairs={{0,7},{1,0},{2,1},{3,2},{4,3},{5,4},{6,5},{7,6},{8,15},{9,8},{10,9... | collective-permute-start | bytes 294920 | tf_op jit(solution)/shard_map/ppermute | solution.py:533
  47.1 0.2 collective-permute-done.18.zl
  47.3 3.6 %static_kernel.1 = (f32[2,8,128]{2,1,0:T(8,128)S(1)}, f32[40,48,128]{2,1,0:T(8,128)S(1)}, f32[40,48,128]{2,1,0:T(8,128)S(1)}, f32[40,48,128]{2,1,0:T(8,128)S(1)}...) custom-call(s32[3]{0:T(128)S(1)} %pad_add_fusion.pos, ...), custom_call_target="tpu_custom_call" | custom-call | tf_op jit(solution)/shard_map/static_kernel/pallas_call | solution.py:520
  50.9 3.7 %middle_kernel.1 = (f32[3,8,128]{2,1,0:T(8,128)S(1)}, f32[16,24,128]{2,1,0:T(8,128)S(1)}, f32[16,24,128]{2,1,0:T(8,128)S(1)}, f32[12,16,128]{2,1,0:T(8,128)S(1)}, f32[12,16,128]{2,1,0:T(8,128)S(1)}) custom-call(s32[3]{0:T(128)S(1)} %pad_add_fusion.pos, f32[16,16,128]{2,1,0:T(8,128)S(1)} %constant_dynamic-update-slice_fusion.own, ...), custom_call_target="tpu_custom_call" | custom-call | tf_op jit(solution)/shard_map/middle_kernel/pallas_call | solution.py:520
  54.6 0.0 collective-permute-start.20
  54.6 3.0 %collective-permute-start.21 = (f32[3,8,128]{2,1,0:T(8,128)S(1)}, f32[3,8,128]{2,1,0:T(8,128)S(1)}, u32[]{:S(2)}, u32[]{:S(2)}) collective-permute-start(f32[3,8,128]{2,1,0:T(8,128)S(1)} %get-tuple-element.70), channel_id=1, source_target_pairs={{0,7},{1,0},{2,1},{3,2},{4,3},{5,4},{6,5},{7,6},{8,15},{9,8},{10,9... | collective-permute-start | bytes 36872 | tf_op jit(solution)/shard_map/ppermute | solution.py:533
  57.5 1.3 %collective-permute-done.20 = f32[3,8,128]{2,1,0:T(8,128)S(1)} collective-permute-done((f32[3,8,128]{2,1,0:T(8,128)S(1)}, f32[3,8,128]{2,1,0:T(8,128)S(1)}, u32[]{:S(2)}, u32[]{:S(2)}) %collective-permute-start.20) | collective-permute-done | bytes 12320 | tf_op jit(solution)/shard_map/ppermute | solution.py:533
  58.9 0.1 collective-permute-done.21
  59.0 3.3 %collective-permute-start.22 = (f32[9,8,128]{2,1,0:T(8,128)S(1)}, f32[9,8,128]{2,1,0:T(8,128)S(1)}, u32[]{:S(2)}, u32[]{:S(2)}) collective-permute-start(f32[9,8,128]{2,1,0:T(8,128)S(1)} %constant_dynamic-update-slice_fusion.4.own), channel_id=1, source_target_pairs={{0,16},{8,24},{16,0},{24,8},{32,48},{40,56},{48,32},{56,40},{1,17}... | collective-permute-start | bytes 110600 | tf_op jit(solution)/shard_map/ppermute | solution.py:618
  62.3 1.9 %collective-permute-start.23 = (f32[9,8,128]{2,1,0:T(8,128)S(1)}, f32[9,8,128]{2,1,0:T(8,128)S(1)}, u32[]{:S(2)}, u32[]{:S(2)}) collective-permute-start(f32[9,8,128]{2,1,0:T(8,128)S(1)} %constant_dynamic-update-slice_fusion.4.own), channel_id=1, source_target_pairs={{0,8},{8,0},{16,32},{24,40},{32,16},{40,24},{48,56},{56,48},{1,9},... | collective-permute-start | bytes 110600 | tf_op jit(solution)/shard_map/ppermute | solution.py:618
  64.2 0.1 collective-permute-done.22.first
  64.2 4.1 %collective-permute-done.23.second = f32[9,8,128]{2,1,0:T(8,128)S(1)} collective-permute-done((f32[9,8,128]{2,1,0:T(8,128)S(1)}, f32[9,8,128]{2,1,0:T(8,128)S(1)}, u32[]{:S(2)}, u32[]{:S(2)}) %collective-permute-start.23) | collective-permute-done | bytes 36896 | tf_op jit(solution)/shard_map/ppermute | solution.py:618
  68.4 4.8 %last_kernel.1 = f32[16,32,128]{2,1,0:T(8,128)} custom-call(s32[3]{0:T(128)S(1)} %pad_add_fusion.pos, f32[9,8,128]{2,1,0:T(8,128)S(1)} %constant_dynamic-update-slice_fusion.4.own, f32[9,8,128]{2,1,0:T(8,128)S(1)} %collective-permute-done.22.first, f32[9,8,128]{2,1,0:T(8,128)S(1)} %collective-permute-done.23.second, ...), custom_call_target="tpu_custom_call" | custom-call | tf_op jit(solution)/shard_map/last_kernel/pallas_call | solution.py:520
  (29 shorter events, 0.2 us)
Async XLA Ops:
  0.0 1.8 %copy-start.1 = (f32[16,32,128]{2,1,0:T(8,128)S(1)}, f32[16,32,128]{2,1,0:T(8,128)}, u32[]{:S(2)}) copy-start(f32[16,32,128]{2,1,0:T(8,128)} %m.5) | copy-start | bytes 786436
  1.8 3.5 %copy-start = (f32[16,32,128]{2,1,0:T(8,128)S(1)}, f32[16,32,128]{2,1,0:T(8,128)}, u32[]{:S(2)}) copy-start(f32[16,32,128]{2,1,0:T(8,128)} %k.5) | copy-start | bytes 786436
  1.8 8.4 %collective-permute-start = (f32[10,32,128]{2,1,0:T(8,128)S(1)}, f32[10,32,128]{2,1,0:T(8,128)S(1)}, u32[]{:S(2)}, u32[]{:S(2)}) collective-permute-start(f32[10,32,128]{2,1,0:T(8,128)S(1)} %pad_maximum_fusion.1), channel_id=1, source_target_pairs={{0,64},{64,128},{128,192},{192,0},{1,65},{65,129},{129,193},{193,1... | collective-permute-start | bytes 491528 | tf_op jit(solution)/shard_map/ppermute | solution.py:533
  3.5 7.2 %copy-start.2 = (f32[16,32,128]{2,1,0:T(8,128)S(1)}, f32[16,32,128]{2,1,0:T(8,128)}, u32[]{:S(2)}) copy-start(f32[16,32,128]{2,1,0:T(8,128)} %f.3) | copy-start | bytes 786436
  3.5 7.1 %collective-permute-start.1 = (f32[10,32,128]{2,1,0:T(8,128)S(1)}, f32[10,32,128]{2,1,0:T(8,128)S(1)}, u32[]{:S(2)}, u32[]{:S(2)}) collective-permute-start(f32[10,32,128]{2,1,0:T(8,128)S(1)} %pad_maximum_fusion.2), channel_id=1, source_target_pairs={{0,192},{64,0},{128,64},{192,128},{1,193},{65,1},{129,65},{193,129... | collective-permute-start | bytes 491528 | tf_op jit(solution)/shard_map/ppermute | solution.py:533
  5.5 16.7 %collective-permute-start.13 = (f32[8,16,128]{2,1,0:T(8,128)S(1)}, f32[8,16,128]{2,1,0:T(8,128)S(1)}, u32[]{:S(2)}, u32[]{:S(2)}) collective-permute-start(f32[8,16,128]{2,1,0:T(8,128)S(1)} %coarse_kernel.1), channel_id=1, source_target_pairs={{0,64},{64,0},{128,192},{192,128},{1,65},{65,1},{129,193},{193,129... | collective-permute-start | bytes 196616 | tf_op jit(solution)/shard_map/ppermute | solution.py:538
  5.9 16.3 %collective-permute-start.14 = (f32[8,16,128]{2,1,0:T(8,128)S(1)}, f32[8,16,128]{2,1,0:T(8,128)S(1)}, u32[]{:S(2)}, u32[]{:S(2)}) collective-permute-start(f32[8,16,128]{2,1,0:T(8,128)S(1)} %coarse_kernel.1), channel_id=1, source_target_pairs={{0,128},{64,192},{128,0},{192,64},{1,129},{65,193},{129,1},{193,65... | collective-permute-start | bytes 196616 | tf_op jit(solution)/shard_map/ppermute | solution.py:538
  8.8 13.4 %collective-permute-start.15 = (f32[8,16,128]{2,1,0:T(8,128)S(1)}, f32[8,16,128]{2,1,0:T(8,128)S(1)}, u32[]{:S(2)}, u32[]{:S(2)}) collective-permute-start(f32[8,16,128]{2,1,0:T(8,128)S(1)} %coarse_kernel.1), channel_id=1, source_target_pairs={{0,192},{64,128},{128,64},{192,0},{1,193},{65,129},{129,65},{193,1... | collective-permute-start | bytes 196616 | tf_op jit(solution)/shard_map/ppermute | solution.py:538
  10.7 4.7 %collective-permute-start.2 = (f32[184,128]{1,0:T(8,128)S(1)}, f32[184,128]{1,0:T(8,128)S(1)}, u32[]{:S(2)}, u32[]{:S(2)}) collective-permute-start(f32[184,128]{1,0:T(8,128)S(1)} %get-tuple-element.47), channel_id=1, source_target_pairs={{0,8},{8,16},{16,24},{24,32},{32,40},{40,48},{48,56},{56,0},{1,9},... | collective-permute-start | bytes 282632 | tf_op jit(solution)/shard_map/ppermute | solution.py:533
  12.7 5.7 %collective-permute-start.3 = (f32[184,128]{1,0:T(8,128)S(1)}, f32[184,128]{1,0:T(8,128)S(1)}, u32[]{:S(2)}, u32[]{:S(2)}) collective-permute-start(f32[184,128]{1,0:T(8,128)S(1)} %get-tuple-element.48), channel_id=1, source_target_pairs={{0,56},{8,0},{16,8},{24,16},{32,24},{40,32},{48,40},{56,48},{1,57}... | collective-permute-start | bytes 282632 | tf_op jit(solution)/shard_map/ppermute | solution.py:533
  19.2 6.3 %collective-permute-start.4 = (f32[2,40,128]{2,1,0:T(8,128)S(1)}, f32[2,40,128]{2,1,0:T(8,128)S(1)}, u32[]{:S(2)}, u32[]{:S(2)}) collective-permute-start(f32[2,40,128]{2,1,0:T(8,128)S(1)} %get-tuple-element.52), channel_id=1, source_target_pairs={{0,1},{1,2},{2,3},{3,4},{4,5},{5,6},{6,7},{7,0},{8,9},{9,10},{10,1... | collective-permute-start | bytes 122888 | tf_op jit(solution)/shard_map/ppermute | solution.py:533
  19.2 6.3 %collective-permute-start.5 = (f32[2,40,128]{2,1,0:T(8,128)S(1)}, f32[2,40,128]{2,1,0:T(8,128)S(1)}, u32[]{:S(2)}, u32[]{:S(2)}) collective-permute-start(f32[2,40,128]{2,1,0:T(8,128)S(1)} %get-tuple-element.53), channel_id=1, source_target_pairs={{0,7},{1,0},{2,1},{3,2},{4,3},{5,4},{6,5},{7,6},{8,15},{9,8},{10,9... | collective-permute-start | bytes 122888 | tf_op jit(solution)/shard_map/ppermute | solution.py:533
  22.2 18.4 %collective-permute-start.16 = (f32[32,16,128]{2,1,0:T(8,128)S(1)}, f32[32,16,128]{2,1,0:T(8,128)S(1)}, u32[]{:S(2)}, u32[]{:S(2)}) collective-permute-start(f32[32,16,128]{2,1,0:T(8,128)S(1)} %pad_maximum_fusion.own), channel_id=1, source_target_pairs={{0,8},{8,16},{16,24},{24,32},{32,40},{40,48},{48,56},{56,0},{1,9},... | collective-permute-start | bytes 786440 | tf_op jit(solution)/shard_map/ppermute | solution.py:533
  25.5 15.0 %collective-permute-start.17 = (f32[32,16,128]{2,1,0:T(8,128)S(1)}, f32[32,16,128]{2,1,0:T(8,128)S(1)}, u32[]{:S(2)}, u32[]{:S(2)}) collective-permute-start(f32[32,16,128]{2,1,0:T(8,128)S(1)} %pad_maximum_fusion.own), channel_id=1, source_target_pairs={{0,56},{8,0},{16,8},{24,16},{32,24},{40,32},{48,40},{56,48},{1,57}... | collective-permute-start | bytes 786440 | tf_op jit(solution)/shard_map/ppermute | solution.py:533
  29.7 4.8 %collective-permute-start.6 = (f32[4,16,128]{2,1,0:T(8,128)S(1)}, f32[4,16,128]{2,1,0:T(8,128)S(1)}, u32[]{:S(2)}, u32[]{:S(2)}) collective-permute-start(f32[4,16,128]{2,1,0:T(8,128)S(1)} %get-tuple-element.54), channel_id=1, source_target_pairs={{0,64},{64,0},{128,192},{192,128},{1,65},{65,1},{129,193},{193,129... | collective-permute-start | bytes 98312 | tf_op jit(solution)/shard_map/ppermute | solution.py:538
  30.5 5.4 %collective-permute-start.7 = (f32[4,16,128]{2,1,0:T(8,128)S(1)}, f32[4,16,128]{2,1,0:T(8,128)S(1)}, u32[]{:S(2)}, u32[]{:S(2)}) collective-permute-start(f32[4,16,128]{2,1,0:T(8,128)S(1)} %get-tuple-element.54), channel_id=1, source_target_pairs={{0,128},{64,192},{128,0},{192,64},{1,129},{65,193},{129,1},{193,65... | collective-permute-start | bytes 98312 | tf_op jit(solution)/shard_map/ppermute | solution.py:538
  33.2 5.1 %collective-permute-start.8 = (f32[4,16,128]{2,1,0:T(8,128)S(1)}, f32[4,16,128]{2,1,0:T(8,128)S(1)}, u32[]{:S(2)}, u32[]{:S(2)}) collective-permute-start(f32[4,16,128]{2,1,0:T(8,128)S(1)} %get-tuple-element.54), channel_id=1, source_target_pairs={{0,192},{64,128},{128,64},{192,0},{1,193},{65,129},{129,65},{193,1... | collective-permute-start | bytes 98312 | tf_op jit(solution)/shard_map/ppermute | solution.py:538
  38.3 5.6 %collective-permute-start.10 = (f32[16,16,128]{2,1,0:T(8,128)S(1)}, f32[16,16,128]{2,1,0:T(8,128)S(1)}, u32[]{:S(2)}, u32[]{:S(2)}) collective-permute-start(f32[16,16,128]{2,1,0:T(8,128)S(1)} %constant_dynamic-update-slice_fusion.own), channel_id=1, source_target_pairs={{0,56},{8,0},{16,8},{24,16},{32,24},{40,32},{48,40},{56,48},{1,57}... | collective-permute-start | bytes 393224 | tf_op jit(solution)/shard_map/ppermute | solution.py:533
  38.3 5.6 %collective-permute-start.9 = (f32[16,16,128]{2,1,0:T(8,128)S(1)}, f32[16,16,128]{2,1,0:T(8,128)S(1)}, u32[]{:S(2)}, u32[]{:S(2)}) collective-permute-start(f32[16,16,128]{2,1,0:T(8,128)S(1)} %constant_dynamic-update-slice_fusion.own), channel_id=1, source_target_pairs={{0,8},{8,16},{16,24},{24,32},{32,40},{40,48},{48,56},{56,0},{1,9},... | collective-permute-start | bytes 393224 | tf_op jit(solution)/shard_map/ppermute | solution.py:533
  40.9 6.3 %collective-permute-start.18 = (f32[8,48,128]{2,1,0:T(8,128)S(1)}, f32[8,48,128]{2,1,0:T(8,128)S(1)}, u32[]{:S(2)}, u32[]{:S(2)}) collective-permute-start(f32[8,48,128]{2,1,0:T(8,128)S(1)} %get-tuple-element.57), channel_id=1, source_target_pairs={{0,1},{1,2},{2,3},{3,4},{4,5},{5,6},{6,7},{7,0},{8,9},{9,10},{10,1... | collective-permute-start | bytes 589832 | tf_op jit(solution)/shard_map/ppermute | solution.py:533
  41.0 6.3 %collective-permute-start.19 = (f32[8,48,128]{2,1,0:T(8,128)S(1)}, f32[8,48,128]{2,1,0:T(8,128)S(1)}, u32[]{:S(2)}, u32[]{:S(2)}) collective-permute-start(f32[8,48,128]{2,1,0:T(8,128)S(1)} %get-tuple-element.58), channel_id=1, source_target_pairs={{0,7},{1,0},{2,1},{3,2},{4,3},{5,4},{6,5},{7,6},{8,15},{9,8},{10,9... | collective-permute-start | bytes 589832 | tf_op jit(solution)/shard_map/ppermute | solution.py:533
  44.1 6.7 %collective-permute-start.11 = (f32[4,48,128]{2,1,0:T(8,128)S(1)}, f32[4,48,128]{2,1,0:T(8,128)S(1)}, u32[]{:S(2)}, u32[]{:S(2)}) collective-permute-start(f32[4,48,128]{2,1,0:T(8,128)S(1)} %get-tuple-element.55), channel_id=1, source_target_pairs={{0,1},{1,2},{2,3},{3,4},{4,5},{5,6},{6,7},{7,0},{8,9},{9,10},{10,1... | collective-permute-start | bytes 294920 | tf_op jit(solution)/shard_map/ppermute | solution.py:533
  44.2 6.7 %collective-permute-start.12 = (f32[4,48,128]{2,1,0:T(8,128)S(1)}, f32[4,48,128]{2,1,0:T(8,128)S(1)}, u32[]{:S(2)}, u32[]{:S(2)}) collective-permute-start(f32[4,48,128]{2,1,0:T(8,128)S(1)} %get-tuple-element.56), channel_id=1, source_target_pairs={{0,7},{1,0},{2,1},{3,2},{4,3},{5,4},{6,5},{7,6},{8,15},{9,8},{10,9... | collective-permute-start | bytes 294920 | tf_op jit(solution)/shard_map/ppermute | solution.py:533
  54.6 4.3 %collective-permute-start.20 = (f32[3,8,128]{2,1,0:T(8,128)S(1)}, f32[3,8,128]{2,1,0:T(8,128)S(1)}, u32[]{:S(2)}, u32[]{:S(2)}) collective-permute-start(f32[3,8,128]{2,1,0:T(8,128)S(1)} %get-tuple-element.70), channel_id=1, source_target_pairs={{0,1},{1,2},{2,3},{3,4},{4,5},{5,6},{6,7},{7,0},{8,9},{9,10},{10,1... | collective-permute-start | bytes 36872 | tf_op jit(solution)/shard_map/ppermute | solution.py:533
  54.6 4.4 %collective-permute-start.21 = (f32[3,8,128]{2,1,0:T(8,128)S(1)}, f32[3,8,128]{2,1,0:T(8,128)S(1)}, u32[]{:S(2)}, u32[]{:S(2)}) collective-permute-start(f32[3,8,128]{2,1,0:T(8,128)S(1)} %get-tuple-element.70), channel_id=1, source_target_pairs={{0,7},{1,0},{2,1},{3,2},{4,3},{5,4},{6,5},{7,6},{8,15},{9,8},{10,9... | collective-permute-start | bytes 36872 | tf_op jit(solution)/shard_map/ppermute | solution.py:533
  59.0 5.3 %collective-permute-start.22 = (f32[9,8,128]{2,1,0:T(8,128)S(1)}, f32[9,8,128]{2,1,0:T(8,128)S(1)}, u32[]{:S(2)}, u32[]{:S(2)}) collective-permute-start(f32[9,8,128]{2,1,0:T(8,128)S(1)} %constant_dynamic-update-slice_fusion.4.own), channel_id=1, source_target_pairs={{0,16},{8,24},{16,0},{24,8},{32,48},{40,56},{48,32},{56,40},{1,17}... | collective-permute-start | bytes 110600 | tf_op jit(solution)/shard_map/ppermute | solution.py:618
  62.3 6.1 %collective-permute-start.23 = (f32[9,8,128]{2,1,0:T(8,128)S(1)}, f32[9,8,128]{2,1,0:T(8,128)S(1)}, u32[]{:S(2)}, u32[]{:S(2)}) collective-permute-start(f32[9,8,128]{2,1,0:T(8,128)S(1)} %constant_dynamic-update-slice_fusion.4.own), channel_id=1, source_target_pairs={{0,8},{8,0},{16,32},{24,40},{32,16},{40,24},{48,56},{56,48},{1,9},... | collective-permute-start | bytes 110600 | tf_op jit(solution)/shard_map/ppermute | solution.py:618

commit v4 on v3

--- a/solution.py
+++ b/solution.py
@@ -139,32 +139,30 @@
 def pack_z_kernel(f, k, m, xl, xr, yl, yr, fa, ka, ma, up, down):
     lane = iota((40, 128), 1)
     zero = jnp.zeros((32, 128), F32)
-    for g in range(2):
-        acc_up = jnp.zeros((40, 128), F32)
-        acc_down = jnp.zeros((40, 128), F32)
-        for i in range(12):
-            p = 12 * g + i
-            if p < 4:
-                own = (xl[p - 1] if p else zero, xl[2 + p] if p else zero, xl[6 + p])
-            elif p < 20:
-                own = (f[p - 4], m[p - 4], k[p - 4])
-            else:
-                own = (xr[p - 20] if p < 23 else zero, xr[p - 17] if p < 23 else zero, xr[p - 14])
-            for a, out in enumerate((fa, ma, ka)):
-                count, base = reach(p)[a // 2], ROWS[p][a]
-                out[p, 0:32] = own[a]
-                out[p, 32:40] = jnp.zeros((8, 128), F32)
-                if count:
-                    out[p, 32 : 32 + count] = yr[base : base + count]
-                    out[p, 40 - count : 40] = yl[base : base + count]
-                whole = out[p]
-                width = 4 if a == 2 else 3
-                first = 10 * i + 3 * a
-                mask = (lane >= first) & (lane < first + width)
-                acc_up = jnp.where(mask, roll(whole, first - (128 - width), 1), acc_up)
-                acc_down = jnp.where(mask, roll(whole, first, 1), acc_down)
-        up[g] = acc_up
-        down[g] = acc_down
+    faces = [[None, None] for _ in range(3)]
+    for p in range(24):
+        g, i = p // 16, p % 16
+        if p < 4:
+            own = (xl[p - 1] if p else zero, xl[2 + p] if p else zero, xl[6 + p])
+        elif p < 20:
+            own = (f[p - 4], m[p - 4], k[p - 4])
+        else:
+            own = (xr[p - 20] if p < 23 else zero, xr[p - 17] if p < 23 else zero, xr[p - 14])
+        for a, out in enumerate((fa, ma, ka)):
+            count, base = reach(p)[a // 2], ROWS[p][a]
+            out[p, 0:32] = own[a]
+            out[p, 32:40] = jnp.zeros((8, 128), F32)
+            if count:
+                out[p, 32 : 32 + count] = yr[base : base + count]
+                out[p, 40 - count : 40] = yl[base : base + count]
+            moved = roll(out[p], 8 * i + 4, 1)
+            faces[a][g] = moved if i == 0 else jnp.where(lane // 8 == i, moved, faces[a][g])
+    front = lane % 8 < 4
+    source, screening, conductivity = faces
+    pairs = ((source[0], screening[0]), (source[1], screening[1]), conductivity)
+    for g, (one, two) in enumerate(pairs):
+        up[g] = jnp.where(front, one, roll(two, 4, 1))
+        down[g] = jnp.where(front, roll(one, -4, 1), two)
 
 
 def pair_matrix(columns):
@@ -196,8 +194,12 @@
     far = ((row >= 32) & (row < 36) & (iy == 7)) | ((row >= 36) & (iy == 0))
     beside = ((lane < 4) & (iz < 7)) | ((lane >= 124) & (iz > 0))
     inner = (lane < 3) | (lane > 124)
+    front = lane % 8 < 4
+    ones = [jnp.where(front, zl[g], roll(zr[g], 4, 1)) for g in range(3)]
+    twos = [jnp.where(front, roll(zl[g], -4, 1), zr[g]) for g in range(3)]
+    faces = (ones[:2], twos[:2], (ones[2], twos[2]))
     for p in range(24):
-        group, i = p // 12, p % 12
+        group, i = p // 16, p % 16
         absent = False
         if p < 4:
             absent = ix == 0
@@ -207,14 +209,10 @@
         three = reach(p)[0]
         unknown = (row >= 32 + three) & (row < 40 - three)
         for a, (src, out) in enumerate(((fa, f), (ma, m), (ka, k))):
-            width = 4 if a == 2 else 3
-            first = 10 * i + 3 * a
             if a == 1 and p in (0, 23):
                 out[p] = jnp.full((40, 256), OUTSIDE, F32)
                 continue
-            right = roll(zr[group], -first, 1)
-            left = roll(zl[group], 128 - width - first, 1)
-            side = jnp.where(lane < 64, right, left)
+            side = roll(faces[a][group], -8 * i - 4, 1)
             own = src[p]
             fill = OUTSIDE if a == 1 else 0.0
             if a == 2:
@@ -225,8 +223,8 @@
                 there = here | ~(beside & inner)
             out[p, :, 0:128] = jnp.where(here, fill, own)
             out[p, :, 128:256] = jnp.where(there, fill, side)
-    coefficients(1, 23, 4, k, f, m, d, w, g, cy, cz)
-    sweep(2, 22, 4, k, w, g, cy, cz, g, v_out)
+    coefficients(1, 23, 11, k, f, m, d, w, g, cy, cz)
+    sweep(2, 22, 10, k, w, g, cy, cz, g, v_out)
 
     def residual(p):
         total, centre = neighbours(p, k, cy, cz, v_out)
@@ -238,7 +236,7 @@
     def store(i, value):
         tall[pl.ds(pl.multiple_of(32 * i, 32), 32), :] = value
 
-    planes(0, 8, values, store, 2)
+    planes(0, 8, values, store, 8)
     halve_and_pack(tall, pair_matrix(128), message, 0)
 
 
@@ -272,15 +270,17 @@
 
 def spread1(ix, gone, own, yl, yr, zl, zr, order, count, a, out, fill, scale):
     lane = iota((48, 128), 1)
+    even = lane // 16 % 2 == 0
     for b in range(4):
         block = 8 * jnp.bitwise_xor(ix, order[b]) + 4
-        left, right = zl[count * b + a], zr[count * b + a]
+        left, right = roll(zl[count * b + a], 48, 1), zr[count * b + a]
+        sides = (jnp.where(even, right, left), jnp.where(even, left, right))
         for q in range(4):
             s = 4 * (count * b + a) + q
             pair = jnp.concatenate([own[s], yr[s], yl[s]], axis=0)
             for h in range(2):
                 at = 16 * (q + 4 * h)
-                side = jnp.where(lane < 96, roll(right, 64 - at, 1), roll(left, 112 - at, 1))
+                side = roll(sides[q % 2], 64 - at, 1)
                 value = jnp.where(lane < 64, roll(pair, 64 * h, 1), side)
                 value = value if scale == 1.0 else scale * value
                 out[block + q + 4 * h] = jnp.where(gone, fill, value)
@@ -344,7 +344,7 @@
     coefficients(4, 36, 8, k1, None, m1, d1, w1, None, cy1, cz1)
     to_second(tall, m2, lambda p: m1[p], OUTSIDE)
     to_second(tall, k2, lambda p: 0.25 * k1[p], 0.0)
-    coefficients(4, 20, 8, k2, None, m2, d2, w2, None, cy2, cz2)
+    coefficients(4, 20, 16, k2, None, m2, d2, w2, None, cy2, cz2)
 
     def write(slot):
         def put(where, value):
@@ -378,7 +378,7 @@
         planes(low, high, lambda p: w[p] * f[p], store, 8)
 
     weigh(4, 36, w1, f1, g1)
-    sweep(4, 36, 8, k1, w1, g1, cy1, cz1, g1, v1)
+    sweep(4, 36, 16, k1, w1, g1, cy1, cz1, g1, v1)
 
     def residual1(p):
         total, centre = neighbours(p, k1, cy1, cz1, v1)
@@ -386,7 +386,7 @@
 
     to_second(tall, f2, residual1, 0.0)
     weigh(4, 20, w2, f2, g2)
-    sweep(4, 20, 8, k2, w2, g2, cy2, cz2, g2, v2)
+    sweep(4, 20, 16, k2, w2, g2, cy2, cz2, g2, v2)
     row24 = iota((24, 128), 0)
     gone2 = ((row24 >= 8) & (row24 < 16) & (iy == 7)) | ((row24 >= 16) & (iy == 0))
 
@@ -493,7 +493,7 @@
             half[pl.ds(37, 2, stride=2), :] = ahead
             for p in (2 * x + 2, 2 * x + 3):
                 a0[p, :, lanes] = v0[p, :, lanes] + half[...]
-    sweep(3, 21, 3, k0, w0, g0, cy0, cz0, a0, b0)
+    sweep(3, 21, 9, k0, w0, g0, cy0, cz0, a0, b0)
 
     def values(p):
         total, centre = neighbours(p, k0, cy0, cz0, b0)
@@ -502,7 +502,7 @@
     def store(p, value):
         out[p - 4] = value
 
-    planes(4, 20, values, store, 4)
+    planes(4, 20, values, store, 8)
 
 
 VMEM = pl.BlockSpec(memory_space=pltpu.VMEM)
@@ -538,7 +538,7 @@
     return lax.ppermute(x, axis, [(i, i ^ bits) for i in range(size)])
 
 
-FULL, SIDES = (24, 40, 256), (2, 40, 128)
+FULL, SIDES = (24, 40, 256), (3, 40, 128)
 ONE, TWO, THREE = (40, 48, 128), (24, 24, 128), (12, 24, 128)
 NEAR1, NEAR2 = (16, 24, 128), (12, 16, 128)
 TALL = (768, 128)

time: 73.3 us -> 71.6 us (0.977)
  Pallas kernels: 17.9 us -> 16.3 us
    pallas_call x9, Pallas kernels: 17.9 us -> 16.3 us  [call(): pl.pallas_call(kernel, out_shape=[jax.ShapeDtypeStruct(s, F32) for s in o...]
  transfers between devices with their start and end apart: 24 -> 24, of which waited for: 10 -> 10; matrix products, arithmetic and copies ran while one was open for 0% -> 0% of each run, Pallas kernels for 13% -> 12%
where the time goes in v4:
time: 71.6 us; the launch traced here: 71.5 us
  starting transfers between devices  37.7 us (53%)
  Pallas kernels  16.3 us (23%)
  waiting for transfers between devices  15.4 us (22%)
  local copies, waits for them, and re-layouts  1.8 us (3%)
    ppermute x16, starting transfers between devices, shift(): return lax.ppermute(x, axis, [(i, (i + step) % size) for i in range(size)])  22.9 us
    pallas_call x9, Pallas kernels, call(): pl.pallas_call(kernel, out_shape=[jax.ShapeDtypeStruct(s, F32) for s in o...  16.3 us
    ppermute x6, starting transfers between devices, swap(): return lax.ppermute(x, axis, [(i, i ^ bits) for i in range(size)])  9.55 us
    ppermute x16, waiting for transfers between devices, shift(): return lax.ppermute(x, axis, [(i, (i + step) % size) for i in range(size)])  7.46 us
    ppermute x2, starting transfers between devices, per_device(): lax.ppermute(own, 'gy', list(enumerate(t)))  5.23 us
    ppermute x2, waiting for transfers between devices, per_device(): lax.ppermute(own, 'gy', list(enumerate(t)))  4.19 us
    ppermute x6, waiting for transfers between devices, swap(): return lax.ppermute(x, axis, [(i, i ^ bits) for i in range(size)])  3.76 us
    slice x3, local copies, waits for them, and re-layouts, per_device(): down = jnp.concatenate([f[:3], m[:3], k[:4]])  1.76 us
  transfers between devices with their start and end apart: 24, of which 10 were waited for; matrix products, arithmetic and copies ran while one was open for 0% of the time, Pallas kernels for 12%

profile of v4, /device:TPU:64, one launch (start us, length us, event | category | flops | bytes accessed | tf_op | source)
XLA Modules:
  0.0 71.5 jit_solution(12707709311382651357)
XLA Ops:
  0.0 0.9 %fusion.2 = (f32[4,32,128]{2,1,0:T(8,128)S(1)}, f32[4,32,128]{2,1,0:T(8,128)S(1)}) fusion(f32[16,32,128]{2,1,0:T(8,128)} %k.5), kind=kLoop, calls=%fused_computation.13 | loop fusion | bytes 262144 | tf_op jit(solution)/shard_map/slice | solution.py:574
  0.9 0.8 %fusion = (f32[3,32,128]{2,1,0:T(8,128)S(1)}, f32[3,32,128]{2,1,0:T(8,128)S(1)}) fusion(f32[16,32,128]{2,1,0:T(8,128)} %f.3), kind=kLoop, calls=%fused_computation.11 | loop fusion | bytes 196608 | tf_op jit(solution)/shard_map/slice | solution.py:574
  1.8 0.0 copy-start
  1.8 1.7 %collective-permute-start = (f32[10,32,128]{2,1,0:T(8,128)S(1)}, f32[10,32,128]{2,1,0:T(8,128)S(1)}, u32[]{:S(2)}, u32[]{:S(2)}) collective-permute-start(f32[10,32,128]{2,1,0:T(8,128)S(1)} %pad_maximum_fusion.1), channel_id=1, source_target_pairs={{0,64},{64,128},{128,192},{192,0},{1,65},{65,129},{129,193},{193,1... | collective-permute-start | bytes 491528 | tf_op jit(solution)/shard_map/ppermute | solution.py:533
  3.5 0.0 copy-start.2
  3.5 1.7 %collective-permute-start.1 = (f32[10,32,128]{2,1,0:T(8,128)S(1)}, f32[10,32,128]{2,1,0:T(8,128)S(1)}, u32[]{:S(2)}, u32[]{:S(2)}) collective-permute-start(f32[10,32,128]{2,1,0:T(8,128)S(1)} %pad_maximum_fusion.2), channel_id=1, source_target_pairs={{0,192},{64,0},{128,64},{192,128},{1,193},{65,1},{129,65},{193,129... | collective-permute-start | bytes 491528 | tf_op jit(solution)/shard_map/ppermute | solution.py:533
  5.2 0.2 coarse_kernel.1
  5.5 0.5 collective-permute-start.13
  5.9 2.9 %collective-permute-start.14 = (f32[8,16,128]{2,1,0:T(8,128)S(1)}, f32[8,16,128]{2,1,0:T(8,128)S(1)}, u32[]{:S(2)}, u32[]{:S(2)}) collective-permute-start(f32[8,16,128]{2,1,0:T(8,128)S(1)} %coarse_kernel.1), channel_id=1, source_target_pairs={{0,128},{64,192},{128,0},{192,64},{1,129},{65,193},{129,1},{193,65... | collective-permute-start | bytes 196616 | tf_op jit(solution)/shard_map/ppermute | solution.py:538
  8.8 1.4 %collective-permute-start.15 = (f32[8,16,128]{2,1,0:T(8,128)S(1)}, f32[8,16,128]{2,1,0:T(8,128)S(1)}, u32[]{:S(2)}, u32[]{:S(2)}) collective-permute-start(f32[8,16,128]{2,1,0:T(8,128)S(1)} %coarse_kernel.1), channel_id=1, source_target_pairs={{0,192},{64,128},{128,64},{192,0},{1,193},{65,129},{129,65},{193,1... | collective-permute-start | bytes 196616 | tf_op jit(solution)/shard_map/ppermute | solution.py:538
  10.3 0.4 collective-permute-done.1.xr
  10.7 2.0 %collective-permute-start.2 = (f32[184,128]{1,0:T(8,128)S(1)}, f32[184,128]{1,0:T(8,128)S(1)}, u32[]{:S(2)}, u32[]{:S(2)}) collective-permute-start(f32[184,128]{1,0:T(8,128)S(1)} %get-tuple-element.47), channel_id=1, source_target_pairs={{0,8},{8,16},{16,24},{24,32},{32,40},{40,48},{48,56},{56,0},{1,9},... | collective-permute-start | bytes 282632 | tf_op jit(solution)/shard_map/ppermute | solution.py:533
  12.7 0.1 collective-permute-start.3
  12.8 0.1 pad_add_fusion.pos
  12.9 2.5 %collective-permute-done.2.yl = f32[184,128]{1,0:T(8,128)S(1)} collective-permute-done((f32[184,128]{1,0:T(8,128)S(1)}, f32[184,128]{1,0:T(8,128)S(1)}, u32[]{:S(2)}, u32[]{:S(2)}) %collective-permute-start.2) | collective-permute-done | bytes 94240 | tf_op jit(solution)/shard_map/ppermute | solution.py:533
  15.3 3.0 %collective-permute-done.3.yr = f32[184,128]{1,0:T(8,128)S(1)} collective-permute-done((f32[184,128]{1,0:T(8,128)S(1)}, f32[184,128]{1,0:T(8,128)S(1)}, u32[]{:S(2)}, u32[]{:S(2)}) %collective-permute-start.3) | collective-permute-done | bytes 94240 | tf_op jit(solution)/shard_map/ppermute | solution.py:533
  18.4 0.5 pack_z_kernel.1
  18.9 0.0 collective-permute-start.4
  18.9 2.9 %collective-permute-start.5 = (f32[3,40,128]{2,1,0:T(8,128)S(1)}, f32[3,40,128]{2,1,0:T(8,128)S(1)}, u32[]{:S(2)}, u32[]{:S(2)}) collective-permute-start(f32[3,40,128]{2,1,0:T(8,128)S(1)} %get-tuple-element.53), channel_id=1, source_target_pairs={{0,7},{1,0},{2,1},{3,2},{4,3},{5,4},{6,5},{7,6},{8,15},{9,8},{10,9... | collective-permute-start | bytes 184328 | tf_op jit(solution)/shard_map/ppermute | solution.py:533
  21.9 0.0 collective-permute-done.13
  21.9 3.3 %collective-permute-start.16 = (f32[32,16,128]{2,1,0:T(8,128)S(1)}, f32[32,16,128]{2,1,0:T(8,128)S(1)}, u32[]{:S(2)}, u32[]{:S(2)}) collective-permute-start(f32[32,16,128]{2,1,0:T(8,128)S(1)} %pad_maximum_fusion.own), channel_id=1, source_target_pairs={{0,8},{8,16},{16,24},{24,32},{32,40},{40,48},{48,56},{56,0},{1,9},... | collective-permute-start | bytes 786440 | tf_op jit(solution)/shard_map/ppermute | solution.py:533
  25.2 0.0 collective-permute-done.4.zl
  25.2 0.0 collective-permute-done.5.zr
  25.2 3.5 %fine_kernel.1 = (f32[4,16,128]{2,1,0:T(8,128)S(1)}, f32[24,40,256]{2,1,0:T(8,128)S(1)}, f32[24,40,256]{2,1,0:T(8,128)S(1)}, f32[24,40,256]{2,1,0:T(8,128)S(1)},...) custom-call(s32[3]{0:T(128)S(1)} %pad_add_fusion.pos, ...), custom_call_target="tpu_custom_call" | custom-call | tf_op jit(solution)/shard_map/fine_kernel/pallas_call | solution.py:520
  28.8 0.7 %collective-permute-start.6 = (f32[4,16,128]{2,1,0:T(8,128)S(1)}, f32[4,16,128]{2,1,0:T(8,128)S(1)}, u32[]{:S(2)}, u32[]{:S(2)}) collective-permute-start(f32[4,16,128]{2,1,0:T(8,128)S(1)} %get-tuple-element.54), channel_id=1, source_target_pairs={{0,64},{64,0},{128,192},{192,128},{1,65},{65,1},{129,193},{193,129... | collective-permute-start | bytes 98312 | tf_op jit(solution)/shard_map/ppermute | solution.py:538
  29.5 2.7 %collective-permute-start.7 = (f32[4,16,128]{2,1,0:T(8,128)S(1)}, f32[4,16,128]{2,1,0:T(8,128)S(1)}, u32[]{:S(2)}, u32[]{:S(2)}) collective-permute-start(f32[4,16,128]{2,1,0:T(8,128)S(1)} %get-tuple-element.54), channel_id=1, source_target_pairs={{0,128},{64,192},{128,0},{192,64},{1,129},{65,193},{129,1},{193,65... | collective-permute-start | bytes 98312 | tf_op jit(solution)/shard_map/ppermute | solution.py:538
  32.2 1.4 %collective-permute-start.8 = (f32[4,16,128]{2,1,0:T(8,128)S(1)}, f32[4,16,128]{2,1,0:T(8,128)S(1)}, u32[]{:S(2)}, u32[]{:S(2)}) collective-permute-start(f32[4,16,128]{2,1,0:T(8,128)S(1)} %get-tuple-element.54), channel_id=1, source_target_pairs={{0,192},{64,128},{128,64},{192,0},{1,193},{65,129},{129,65},{193,1... | collective-permute-start | bytes 98312 | tf_op jit(solution)/shard_map/ppermute | solution.py:538
  33.5 1.5 %collective-permute-done.7 = f32[4,16,128]{2,1,0:T(8,128)S(1)} collective-permute-done((f32[4,16,128]{2,1,0:T(8,128)S(1)}, f32[4,16,128]{2,1,0:T(8,128)S(1)}, u32[]{:S(2)}, u32[]{:S(2)}) %collective-permute-start.7) | collective-permute-done | bytes 32800 | tf_op jit(solution)/shard_map/ppermute | solution.py:538
  35.0 2.3 %collective-permute-done.8 = f32[4,16,128]{2,1,0:T(8,128)S(1)} collective-permute-done((f32[4,16,128]{2,1,0:T(8,128)S(1)}, f32[4,16,128]{2,1,0:T(8,128)S(1)}, u32[]{:S(2)}, u32[]{:S(2)}) %collective-permute-start.8) | collective-permute-done | bytes 32800 | tf_op jit(solution)/shard_map/ppermute | solution.py:538
  37.3 2.3 %collective-permute-start.9 = (f32[16,16,128]{2,1,0:T(8,128)S(1)}, f32[16,16,128]{2,1,0:T(8,128)S(1)}, u32[]{:S(2)}, u32[]{:S(2)}) collective-permute-start(f32[16,16,128]{2,1,0:T(8,128)S(1)} %constant_dynamic-update-slice_fusion.own), channel_id=1, source_target_pairs={{0,8},{8,16},{16,24},{24,32},{32,40},{40,48},{48,56},{56,0},{1,9},... | collective-permute-start | bytes 393224 | tf_op jit(solution)/shard_map/ppermute | solution.py:533
  39.6 0.4 pack_z1_kernel.3
  39.9 0.0 collective-permute-start.18
  40.0 2.9 %collective-permute-start.19 = (f32[8,48,128]{2,1,0:T(8,128)S(1)}, f32[8,48,128]{2,1,0:T(8,128)S(1)}, u32[]{:S(2)}, u32[]{:S(2)}) collective-permute-start(f32[8,48,128]{2,1,0:T(8,128)S(1)} %get-tuple-element.58), channel_id=1, source_target_pairs={{0,7},{1,0},{2,1},{3,2},{4,3},{5,4},{6,5},{7,6},{8,15},{9,8},{10,9... | collective-permute-start | bytes 589832 | tf_op jit(solution)/shard_map/ppermute | solution.py:533
  42.9 0.2 pack_z1_kernel.2
  43.1 0.0 collective-permute-start.11
  43.2 2.9 %collective-permute-start.12 = (f32[4,48,128]{2,1,0:T(8,128)S(1)}, f32[4,48,128]{2,1,0:T(8,128)S(1)}, u32[]{:S(2)}, u32[]{:S(2)}) collective-permute-start(f32[4,48,128]{2,1,0:T(8,128)S(1)} %get-tuple-element.56), channel_id=1, source_target_pairs={{0,7},{1,0},{2,1},{3,2},{4,3},{5,4},{6,5},{7,6},{8,15},{9,8},{10,9... | collective-permute-start | bytes 294920 | tf_op jit(solution)/shard_map/ppermute | solution.py:533
  46.1 0.2 collective-permute-done.18.zl
  46.3 3.4 %static_kernel.1 = (f32[2,8,128]{2,1,0:T(8,128)S(1)}, f32[40,48,128]{2,1,0:T(8,128)S(1)}, f32[40,48,128]{2,1,0:T(8,128)S(1)}, f32[40,48,128]{2,1,0:T(8,128)S(1)}...) custom-call(s32[3]{0:T(128)S(1)} %pad_add_fusion.pos, ...), custom_call_target="tpu_custom_call" | custom-call | tf_op jit(solution)/shard_map/static_kernel/pallas_call | solution.py:520
  49.7 3.6 %middle_kernel.1 = (f32[3,8,128]{2,1,0:T(8,128)S(1)}, f32[16,24,128]{2,1,0:T(8,128)S(1)}, f32[16,24,128]{2,1,0:T(8,128)S(1)}, f32[12,16,128]{2,1,0:T(8,128)S(1)}, f32[12,16,128]{2,1,0:T(8,128)S(1)}) custom-call(s32[3]{0:T(128)S(1)} %pad_add_fusion.pos, f32[16,16,128]{2,1,0:T(8,128)S(1)} %constant_dynamic-update-slice_fusion.own, ...), custom_call_target="tpu_custom_call" | custom-call | tf_op jit(solution)/shard_map/middle_kernel/pallas_call | solution.py:520
  53.2 0.0 collective-permute-start.20
  53.3 3.0 %collective-permute-start.21 = (f32[3,8,128]{2,1,0:T(8,128)S(1)}, f32[3,8,128]{2,1,0:T(8,128)S(1)}, u32[]{:S(2)}, u32[]{:S(2)}) collective-permute-start(f32[3,8,128]{2,1,0:T(8,128)S(1)} %get-tuple-element.70), channel_id=1, source_target_pairs={{0,7},{1,0},{2,1},{3,2},{4,3},{5,4},{6,5},{7,6},{8,15},{9,8},{10,9... | collective-permute-start | bytes 36872 | tf_op jit(solution)/shard_map/ppermute | solution.py:533
  56.2 1.3 %collective-permute-done.20 = f32[3,8,128]{2,1,0:T(8,128)S(1)} collective-permute-done((f32[3,8,128]{2,1,0:T(8,128)S(1)}, f32[3,8,128]{2,1,0:T(8,128)S(1)}, u32[]{:S(2)}, u32[]{:S(2)}) %collective-permute-start.20) | collective-permute-done | bytes 12320 | tf_op jit(solution)/shard_map/ppermute | solution.py:533
  57.6 0.1 collective-permute-done.21
  57.6 3.3 %collective-permute-start.22 = (f32[9,8,128]{2,1,0:T(8,128)S(1)}, f32[9,8,128]{2,1,0:T(8,128)S(1)}, u32[]{:S(2)}, u32[]{:S(2)}) collective-permute-start(f32[9,8,128]{2,1,0:T(8,128)S(1)} %constant_dynamic-update-slice_fusion.4.own), channel_id=1, source_target_pairs={{0,16},{8,24},{16,0},{24,8},{32,48},{40,56},{48,32},{56,40},{1,17}... | collective-permute-start | bytes 110600 | tf_op jit(solution)/shard_map/ppermute | solution.py:618
  61.0 1.9 %collective-permute-start.23 = (f32[9,8,128]{2,1,0:T(8,128)S(1)}, f32[9,8,128]{2,1,0:T(8,128)S(1)}, u32[]{:S(2)}, u32[]{:S(2)}) collective-permute-start(f32[9,8,128]{2,1,0:T(8,128)S(1)} %constant_dynamic-update-slice_fusion.4.own), channel_id=1, source_target_pairs={{0,8},{8,0},{16,32},{24,40},{32,16},{40,24},{48,56},{56,48},{1,9},... | collective-permute-start | bytes 110600 | tf_op jit(solution)/shard_map/ppermute | solution.py:618
  62.9 0.2 collective-permute-done.22.first
  63.0 4.0 %collective-permute-done.23.second = f32[9,8,128]{2,1,0:T(8,128)S(1)} collective-permute-done((f32[9,8,128]{2,1,0:T(8,128)S(1)}, f32[9,8,128]{2,1,0:T(8,128)S(1)}, u32[]{:S(2)}, u32[]{:S(2)}) %collective-permute-start.23) | collective-permute-done | bytes 36896 | tf_op jit(solution)/shard_map/ppermute | solution.py:618
  67.0 4.5 %last_kernel.1 = f32[16,32,128]{2,1,0:T(8,128)} custom-call(s32[3]{0:T(128)S(1)} %pad_add_fusion.pos, f32[9,8,128]{2,1,0:T(8,128)S(1)} %constant_dynamic-update-slice_fusion.4.own, f32[9,8,128]{2,1,0:T(8,128)S(1)} %collective-permute-done.22.first, f32[9,8,128]{2,1,0:T(8,128)S(1)} %collective-permute-done.23.second, ...), custom_call_target="tpu_custom_call" | custom-call | tf_op jit(solution)/shard_map/last_kernel/pallas_call | solution.py:520
  (29 shorter events, 0.2 us)
Async XLA Ops:
  0.0 1.8 %copy-start.1 = (f32[16,32,128]{2,1,0:T(8,128)S(1)}, f32[16,32,128]{2,1,0:T(8,128)}, u32[]{:S(2)}) copy-start(f32[16,32,128]{2,1,0:T(8,128)} %m.5) | copy-start | bytes 786436
  1.8 3.5 %copy-start = (f32[16,32,128]{2,1,0:T(8,128)S(1)}, f32[16,32,128]{2,1,0:T(8,128)}, u32[]{:S(2)}) copy-start(f32[16,32,128]{2,1,0:T(8,128)} %k.5) | copy-start | bytes 786436
  1.8 8.4 %collective-permute-start = (f32[10,32,128]{2,1,0:T(8,128)S(1)}, f32[10,32,128]{2,1,0:T(8,128)S(1)}, u32[]{:S(2)}, u32[]{:S(2)}) collective-permute-start(f32[10,32,128]{2,1,0:T(8,128)S(1)} %pad_maximum_fusion.1), channel_id=1, source_target_pairs={{0,64},{64,128},{128,192},{192,0},{1,65},{65,129},{129,193},{193,1... | collective-permute-start | bytes 491528 | tf_op jit(solution)/shard_map/ppermute | solution.py:533
  3.5 7.2 %copy-start.2 = (f32[16,32,128]{2,1,0:T(8,128)S(1)}, f32[16,32,128]{2,1,0:T(8,128)}, u32[]{:S(2)}) copy-start(f32[16,32,128]{2,1,0:T(8,128)} %f.3) | copy-start | bytes 786436
  3.5 7.1 %collective-permute-start.1 = (f32[10,32,128]{2,1,0:T(8,128)S(1)}, f32[10,32,128]{2,1,0:T(8,128)S(1)}, u32[]{:S(2)}, u32[]{:S(2)}) collective-permute-start(f32[10,32,128]{2,1,0:T(8,128)S(1)} %pad_maximum_fusion.2), channel_id=1, source_target_pairs={{0,192},{64,0},{128,64},{192,128},{1,193},{65,1},{129,65},{193,129... | collective-permute-start | bytes 491528 | tf_op jit(solution)/shard_map/ppermute | solution.py:533
  5.5 16.4 %collective-permute-start.13 = (f32[8,16,128]{2,1,0:T(8,128)S(1)}, f32[8,16,128]{2,1,0:T(8,128)S(1)}, u32[]{:S(2)}, u32[]{:S(2)}) collective-permute-start(f32[8,16,128]{2,1,0:T(8,128)S(1)} %coarse_kernel.1), channel_id=1, source_target_pairs={{0,64},{64,0},{128,192},{192,128},{1,65},{65,1},{129,193},{193,129... | collective-permute-start | bytes 196616 | tf_op jit(solution)/shard_map/ppermute | solution.py:538
  5.9 16.0 %collective-permute-start.14 = (f32[8,16,128]{2,1,0:T(8,128)S(1)}, f32[8,16,128]{2,1,0:T(8,128)S(1)}, u32[]{:S(2)}, u32[]{:S(2)}) collective-permute-start(f32[8,16,128]{2,1,0:T(8,128)S(1)} %coarse_kernel.1), channel_id=1, source_target_pairs={{0,128},{64,192},{128,0},{192,64},{1,129},{65,193},{129,1},{193,65... | collective-permute-start | bytes 196616 | tf_op jit(solution)/shard_map/ppermute | solution.py:538
  8.8 13.1 %collective-permute-start.15 = (f32[8,16,128]{2,1,0:T(8,128)S(1)}, f32[8,16,128]{2,1,0:T(8,128)S(1)}, u32[]{:S(2)}, u32[]{:S(2)}) collective-permute-start(f32[8,16,128]{2,1,0:T(8,128)S(1)} %coarse_kernel.1), channel_id=1, source_target_pairs={{0,192},{64,128},{128,64},{192,0},{1,193},{65,129},{129,65},{193,1... | collective-permute-start | bytes 196616 | tf_op jit(solution)/shard_map/ppermute | solution.py:538
  10.7 4.7 %collective-permute-start.2 = (f32[184,128]{1,0:T(8,128)S(1)}, f32[184,128]{1,0:T(8,128)S(1)}, u32[]{:S(2)}, u32[]{:S(2)}) collective-permute-start(f32[184,128]{1,0:T(8,128)S(1)} %get-tuple-element.47), channel_id=1, source_target_pairs={{0,8},{8,16},{16,24},{24,32},{32,40},{40,48},{48,56},{56,0},{1,9},... | collective-permute-start | bytes 282632 | tf_op jit(solution)/shard_map/ppermute | solution.py:533
  12.7 5.7 %collective-permute-start.3 = (f32[184,128]{1,0:T(8,128)S(1)}, f32[184,128]{1,0:T(8,128)S(1)}, u32[]{:S(2)}, u32[]{:S(2)}) collective-permute-start(f32[184,128]{1,0:T(8,128)S(1)} %get-tuple-element.48), channel_id=1, source_target_pairs={{0,56},{8,0},{16,8},{24,16},{32,24},{40,32},{48,40},{56,48},{1,57}... | collective-permute-start | bytes 282632 | tf_op jit(solution)/shard_map/ppermute | solution.py:533
  18.9 6.3 %collective-permute-start.4 = (f32[3,40,128]{2,1,0:T(8,128)S(1)}, f32[3,40,128]{2,1,0:T(8,128)S(1)}, u32[]{:S(2)}, u32[]{:S(2)}) collective-permute-start(f32[3,40,128]{2,1,0:T(8,128)S(1)} %get-tuple-element.52), channel_id=1, source_target_pairs={{0,1},{1,2},{2,3},{3,4},{4,5},{5,6},{6,7},{7,0},{8,9},{9,10},{10,1... | collective-permute-start | bytes 184328 | tf_op jit(solution)/shard_map/ppermute | solution.py:533
  18.9 6.3 %collective-permute-start.5 = (f32[3,40,128]{2,1,0:T(8,128)S(1)}, f32[3,40,128]{2,1,0:T(8,128)S(1)}, u32[]{:S(2)}, u32[]{:S(2)}) collective-permute-start(f32[3,40,128]{2,1,0:T(8,128)S(1)} %get-tuple-element.53), channel_id=1, source_target_pairs={{0,7},{1,0},{2,1},{3,2},{4,3},{5,4},{6,5},{7,6},{8,15},{9,8},{10,9... | collective-permute-start | bytes 184328 | tf_op jit(solution)/shard_map/ppermute | solution.py:533
  21.9 17.6 %collective-permute-start.16 = (f32[32,16,128]{2,1,0:T(8,128)S(1)}, f32[32,16,128]{2,1,0:T(8,128)S(1)}, u32[]{:S(2)}, u32[]{:S(2)}) collective-permute-start(f32[32,16,128]{2,1,0:T(8,128)S(1)} %pad_maximum_fusion.own), channel_id=1, source_target_pairs={{0,8},{8,16},{16,24},{24,32},{32,40},{40,48},{48,56},{56,0},{1,9},... | collective-permute-start | bytes 786440 | tf_op jit(solution)/shard_map/ppermute | solution.py:533
  25.2 14.3 %collective-permute-start.17 = (f32[32,16,128]{2,1,0:T(8,128)S(1)}, f32[32,16,128]{2,1,0:T(8,128)S(1)}, u32[]{:S(2)}, u32[]{:S(2)}) collective-permute-start(f32[32,16,128]{2,1,0:T(8,128)S(1)} %pad_maximum_fusion.own), channel_id=1, source_target_pairs={{0,56},{8,0},{16,8},{24,16},{32,24},{40,32},{48,40},{56,48},{1,57}... | collective-permute-start | bytes 786440 | tf_op jit(solution)/shard_map/ppermute | solution.py:533
  28.8 4.8 %collective-permute-start.6 = (f32[4,16,128]{2,1,0:T(8,128)S(1)}, f32[4,16,128]{2,1,0:T(8,128)S(1)}, u32[]{:S(2)}, u32[]{:S(2)}) collective-permute-start(f32[4,16,128]{2,1,0:T(8,128)S(1)} %get-tuple-element.54), channel_id=1, source_target_pairs={{0,64},{64,0},{128,192},{192,128},{1,65},{65,1},{129,193},{193,129... | collective-permute-start | bytes 98312 | tf_op jit(solution)/shard_map/ppermute | solution.py:538
  29.5 5.5 %collective-permute-start.7 = (f32[4,16,128]{2,1,0:T(8,128)S(1)}, f32[4,16,128]{2,1,0:T(8,128)S(1)}, u32[]{:S(2)}, u32[]{:S(2)}) collective-permute-start(f32[4,16,128]{2,1,0:T(8,128)S(1)} %get-tuple-element.54), channel_id=1, source_target_pairs={{0,128},{64,192},{128,0},{192,64},{1,129},{65,193},{129,1},{193,65... | collective-permute-start | bytes 98312 | tf_op jit(solution)/shard_map/ppermute | solution.py:538
  32.2 5.1 %collective-permute-start.8 = (f32[4,16,128]{2,1,0:T(8,128)S(1)}, f32[4,16,128]{2,1,0:T(8,128)S(1)}, u32[]{:S(2)}, u32[]{:S(2)}) collective-permute-start(f32[4,16,128]{2,1,0:T(8,128)S(1)} %get-tuple-element.54), channel_id=1, source_target_pairs={{0,192},{64,128},{128,64},{192,0},{1,193},{65,129},{129,65},{193,1... | collective-permute-start | bytes 98312 | tf_op jit(solution)/shard_map/ppermute | solution.py:538
  37.3 5.6 %collective-permute-start.10 = (f32[16,16,128]{2,1,0:T(8,128)S(1)}, f32[16,16,128]{2,1,0:T(8,128)S(1)}, u32[]{:S(2)}, u32[]{:S(2)}) collective-permute-start(f32[16,16,128]{2,1,0:T(8,128)S(1)} %constant_dynamic-update-slice_fusion.own), channel_id=1, source_target_pairs={{0,56},{8,0},{16,8},{24,16},{32,24},{40,32},{48,40},{56,48},{1,57}... | collective-permute-start | bytes 393224 | tf_op jit(solution)/shard_map/ppermute | solution.py:533
  37.3 5.6 %collective-permute-start.9 = (f32[16,16,128]{2,1,0:T(8,128)S(1)}, f32[16,16,128]{2,1,0:T(8,128)S(1)}, u32[]{:S(2)}, u32[]{:S(2)}) collective-permute-start(f32[16,16,128]{2,1,0:T(8,128)S(1)} %constant_dynamic-update-slice_fusion.own), channel_id=1, source_target_pairs={{0,8},{8,16},{16,24},{24,32},{32,40},{40,48},{48,56},{56,0},{1,9},... | collective-permute-start | bytes 393224 | tf_op jit(solution)/shard_map/ppermute | solution.py:533
  39.9 6.3 %collective-permute-start.18 = (f32[8,48,128]{2,1,0:T(8,128)S(1)}, f32[8,48,128]{2,1,0:T(8,128)S(1)}, u32[]{:S(2)}, u32[]{:S(2)}) collective-permute-start(f32[8,48,128]{2,1,0:T(8,128)S(1)} %get-tuple-element.57), channel_id=1, source_target_pairs={{0,1},{1,2},{2,3},{3,4},{4,5},{5,6},{6,7},{7,0},{8,9},{9,10},{10,1... | collective-permute-start | bytes 589832 | tf_op jit(solution)/shard_map/ppermute | solution.py:533
  40.0 6.3 %collective-permute-start.19 = (f32[8,48,128]{2,1,0:T(8,128)S(1)}, f32[8,48,128]{2,1,0:T(8,128)S(1)}, u32[]{:S(2)}, u32[]{:S(2)}) collective-permute-start(f32[8,48,128]{2,1,0:T(8,128)S(1)} %get-tuple-element.58), channel_id=1, source_target_pairs={{0,7},{1,0},{2,1},{3,2},{4,3},{5,4},{6,5},{7,6},{8,15},{9,8},{10,9... | collective-permute-start | bytes 589832 | tf_op jit(solution)/shard_map/ppermute | solution.py:533
  43.1 6.5 %collective-permute-start.11 = (f32[4,48,128]{2,1,0:T(8,128)S(1)}, f32[4,48,128]{2,1,0:T(8,128)S(1)}, u32[]{:S(2)}, u32[]{:S(2)}) collective-permute-start(f32[4,48,128]{2,1,0:T(8,128)S(1)} %get-tuple-element.55), channel_id=1, source_target_pairs={{0,1},{1,2},{2,3},{3,4},{4,5},{5,6},{6,7},{7,0},{8,9},{9,10},{10,1... | collective-permute-start | bytes 294920 | tf_op jit(solution)/shard_map/ppermute | solution.py:533
  43.2 6.5 %collective-permute-start.12 = (f32[4,48,128]{2,1,0:T(8,128)S(1)}, f32[4,48,128]{2,1,0:T(8,128)S(1)}, u32[]{:S(2)}, u32[]{:S(2)}) collective-permute-start(f32[4,48,128]{2,1,0:T(8,128)S(1)} %get-tuple-element.56), channel_id=1, source_target_pairs={{0,7},{1,0},{2,1},{3,2},{4,3},{5,4},{6,5},{7,6},{8,15},{9,8},{10,9... | collective-permute-start | bytes 294920 | tf_op jit(solution)/shard_map/ppermute | solution.py:533
  53.2 4.3 %collective-permute-start.20 = (f32[3,8,128]{2,1,0:T(8,128)S(1)}, f32[3,8,128]{2,1,0:T(8,128)S(1)}, u32[]{:S(2)}, u32[]{:S(2)}) collective-permute-start(f32[3,8,128]{2,1,0:T(8,128)S(1)} %get-tuple-element.70), channel_id=1, source_target_pairs={{0,1},{1,2},{2,3},{3,4},{4,5},{5,6},{6,7},{7,0},{8,9},{9,10},{10,1... | collective-permute-start | bytes 36872 | tf_op jit(solution)/shard_map/ppermute | solution.py:533
  53.3 4.4 %collective-permute-start.21 = (f32[3,8,128]{2,1,0:T(8,128)S(1)}, f32[3,8,128]{2,1,0:T(8,128)S(1)}, u32[]{:S(2)}, u32[]{:S(2)}) collective-permute-start(f32[3,8,128]{2,1,0:T(8,128)S(1)} %get-tuple-element.70), channel_id=1, source_target_pairs={{0,7},{1,0},{2,1},{3,2},{4,3},{5,4},{6,5},{7,6},{8,15},{9,8},{10,9... | collective-permute-start | bytes 36872 | tf_op jit(solution)/shard_map/ppermute | solution.py:533
  57.6 5.4 %collective-permute-start.22 = (f32[9,8,128]{2,1,0:T(8,128)S(1)}, f32[9,8,128]{2,1,0:T(8,128)S(1)}, u32[]{:S(2)}, u32[]{:S(2)}) collective-permute-start(f32[9,8,128]{2,1,0:T(8,128)S(1)} %constant_dynamic-update-slice_fusion.4.own), channel_id=1, source_target_pairs={{0,16},{8,24},{16,0},{24,8},{32,48},{40,56},{48,32},{56,40},{1,17}... | collective-permute-start | bytes 110600 | tf_op jit(solution)/shard_map/ppermute | solution.py:618
  61.0 6.1 %collective-permute-start.23 = (f32[9,8,128]{2,1,0:T(8,128)S(1)}, f32[9,8,128]{2,1,0:T(8,128)S(1)}, u32[]{:S(2)}, u32[]{:S(2)}) collective-permute-start(f32[9,8,128]{2,1,0:T(8,128)S(1)} %constant_dynamic-update-slice_fusion.4.own), channel_id=1, source_target_pairs={{0,8},{8,0},{16,32},{24,40},{32,16},{40,24},{48,56},{56,48},{1,9},... | collective-permute-start | bytes 110600 | tf_op jit(solution)/shard_map/ppermute | solution.py:618

commit v5 on v4

--- a/solution.py
+++ b/solution.py
@@ -268,11 +268,11 @@
     return gone | ((lane >= 80) & (lane < 112))
 
 
-def spread1(ix, gone, own, yl, yr, zl, zr, order, count, a, out, fill, scale):
+def spread1(ix, own, yl, yr, zl, zr, count, a, write):
     lane = iota((48, 128), 1)
     even = lane // 16 % 2 == 0
     for b in range(4):
-        block = 8 * jnp.bitwise_xor(ix, order[b]) + 4
+        block = 8 * jnp.bitwise_xor(ix, b) + 4
         left, right = roll(zl[count * b + a], 48, 1), zr[count * b + a]
         sides = (jnp.where(even, right, left), jnp.where(even, left, right))
         for q in range(4):
@@ -282,8 +282,7 @@
                 at = 16 * (q + 4 * h)
                 side = roll(sides[q % 2], 64 - at, 1)
                 value = jnp.where(lane < 64, roll(pair, 64 * h, 1), side)
-                value = value if scale == 1.0 else scale * value
-                out[block + q + 4 * h] = jnp.where(gone, fill, value)
+                write(block + q + 4 * h, value)
 
 
 def known2(shape):
@@ -339,8 +338,15 @@
     gone = outside1(iy, iz)
     clear((k1, w1, cy1, cz1), 4, 36)
     clear((k2, w2, cy2, cz2), 4, 20)
-    spread1(ix, gone, own, yl, yr, zl, zr, (0, 1, 2, 3), 2, 0, m1, OUTSIDE, 1.0)
-    spread1(ix, gone, own, yl, yr, zl, zr, (0, 1, 2, 3), 2, 1, k1, 0.0, 0.125)
+
+    def write_m(p, value):
+        m1[p] = jnp.where(gone, OUTSIDE, value)
+
+    def write_k(p, value):
+        k1[p] = jnp.where(gone, 0.0, 0.125 * value)
+
+    spread1(ix, own, yl, yr, zl, zr, 2, 0, write_m)
+    spread1(ix, own, yl, yr, zl, zr, 2, 1, write_k)
     coefficients(4, 36, 8, k1, None, m1, d1, w1, None, cy1, cz1)
     to_second(tall, m2, lambda p: m1[p], OUTSIDE)
     to_second(tall, k2, lambda p: 0.25 * k1[p], 0.0)
@@ -369,15 +375,13 @@
     gone = outside1(iy, iz)
     clear((g1, v1), 4, 36)
     clear((g2, v2), 4, 20)
-    spread1(ix, gone, own, yl, yr, zl, zr, (0, 1, 2, 3), 1, 0, f1, 0.0, 1.0)
-
-    def weigh(low, high, w, f, g):
-        def store(p, value):
-            g[p] = value
-
-        planes(low, high, lambda p: w[p] * f[p], store, 8)
-
-    weigh(4, 36, w1, f1, g1)
+
+    def write(p, value):
+        value = jnp.where(gone, 0.0, value)
+        f1[p] = value
+        g1[p] = w1[p] * value
+
+    spread1(ix, own, yl, yr, zl, zr, 1, 0, write)
     sweep(4, 36, 16, k1, w1, g1, cy1, cz1, g1, v1)
 
     def residual1(p):
@@ -385,7 +389,8 @@
         return jnp.where(gone, 0.0, f1[p] + total - d1[p] * centre)
 
     to_second(tall, f2, residual1, 0.0)
-    weigh(4, 20, w2, f2, g2)
+    for p in range(4, 20):
+        g2[p] = w2[p] * f2[p]
     sweep(4, 20, 16, k2, w2, g2, cy2, cz2, g2, v2)
     row24 = iota((24, 128), 0)
     gone2 = ((row24 >= 8) & (row24 < 16) & (iy == 7)) | ((row24 >= 16) & (iy == 0))
@@ -415,14 +420,14 @@
 def last_kernel(
     pos, own, first, second, v0, w0, g0, k0, cy0, cz0, v1, g1, v2, g2, k1, w1, cy1, cz1, k2, w2, cy2, cz2,
     out,
-    k3, f3, m3, w3, g3, cy3, cz3, a3, b3, rows, dup, a2, b2, a1, b1, wide, low, high, a0, b0,
+    k3, f3, m3, w3, g3, cy3, cz3, a3, rows, dup, a2, b2, a1, b1, wide, low, high, a0, b0,
 ):
     ix, iy, iz = pos[0], pos[1], pos[2]
     row = iota((24, 128), 0) + 4 * iy - 10
     lane = iota((24, 128), 1)
     gone = (row < 0) | (row >= 32) | ((lane >= 32) & (lane < 112))
     gone = gone | ((lane >= 16) & (lane < 32) & (iz == 7)) | ((lane >= 112) & (iz == 0))
-    clear((k3, g3, a3, b3), 2, 10)
+    clear((k3, g3, a3), 2, 10)
     crossed = (iy // 2) % 2 == 0
 
     def stack(index):
@@ -442,18 +447,23 @@
             )
             ref[x + 2] = jnp.where(gone, fill, value)
     coefficients(2, 10, 8, k3, f3, m3, None, w3, g3, cy3, cz3)
-    source = g3
-    for index in range(COARSE_SWEEPS - 1):
-        target = (a3, b3)[index % 2]
-        sweep(2, 10, 8, k3, w3, g3, cy3, cz3, source, target)
-        source = target
+    field = [g3[p] for p in range(1, 11)]
+    for _ in range(COARSE_SWEEPS - 1):
+        inner = []
+        for p in range(2, 10):
+            behind, here, ahead = field[p - 2 : p + 1]
+            total, _ = neighbours(p, k3, cy3, cz3, {p: here, p - 1: behind, p + 1: ahead})
+            inner.append(KEEP * here + g3[p] + w3[p] * total)
+        field = [field[0], *inner, field[9]]
+    for p in range(8):
+        a3[p + 2] = field[p + 1]
 
     src, column = iota((128, 128), 0), iota((128, 128), 1)
     to2 = jnp.where(
         ((column < 40) & (src == column // 2)) | ((column >= 120) & (src == 64 + column // 2)), 1.0, 0.0
     )
     for x in range(6):
-        rows[24 * x : 24 * x + 24] = source[2 * ix + x]
+        rows[24 * x : 24 * x + 24] = a3[2 * ix + x]
     rows[0:144] = dot(rows[0:144], to2)
     for x in range(6):
         duplicate(dup, 16 * x, rows, 24 * x + 10, 6)
@@ -528,11 +538,6 @@
     )(*args)
 
 
-def shift(x, axis, step):
-    size = lax.axis_size(axis)
-    return lax.ppermute(x, axis, [(i, (i + step) % size) for i in range(size)])
-
-
 def swap(x, axis, bits):
     size = lax.axis_size(axis)
     return lax.ppermute(x, axis, [(i, i ^ bits) for i in range(size)])
@@ -548,13 +553,13 @@
     return jnp.concatenate([x] + [swap(x, "gx", bits) for bits in (1, 2, 3)])
 
 
-def gather_x_pairs(x):
-    pair = jnp.concatenate([x, swap(x, "gx", 1)])
-    return jnp.concatenate([pair, swap(pair, "gx", 3)])
-
-
 def both_sides(up, down, axis):
-    return shift(up, axis, 1), shift(down, axis, -1)
+    size = lax.axis_size(axis)
+    even = lax.axis_index(axis) % 2 == 0
+    far = [(i, (i + 1) % size if i % 2 else (i - 1) % size) for i in range(size)]
+    there = lax.ppermute(jnp.where(even, down, up), axis, far)
+    here = swap(jnp.where(even, up, down), axis, 1)
+    return jnp.where(even, there, here), jnp.where(even, here, there)
 
 
 def pack_z1(count, own, yl, yr):
@@ -619,7 +624,7 @@
     return call(
         last_kernel,
         [(16, 32, 128)],
-        [THREE] * 9 + [(240, 128), (192, 128)] + [NEAR2] * 2 + [NEAR1] * 2
+        [THREE] * 8 + [(240, 128), (192, 128)] + [NEAR2] * 2 + [NEAR1] * 2
         + [(240, 256), (40, 128), (40, 128)] + [FULL] * 2,
         own, first, second, *level0, *vary, *near,
         pos=pos,

time: 71.6 us -> 69.1 us (0.965)
  starting transfers between devices: 37.7 us -> 30.9 us
  waiting for transfers between devices: 15.4 us -> 19.5 us
    ppermute x16 -> x8, starting transfers between devices: 22.9 us -> 6.65 us  [both_sides(): there = lax.ppermute(jnp.where(even, down, up), axis, far)]
    ppermute x6 -> x14, starting transfers between devices: 9.55 us -> 21.1 us  [swap(): return lax.ppermute(x, axis, [(i, i ^ bits) for i in range(size)])]
    ppermute x6 -> x14, waiting for transfers between devices: 3.76 us -> 7.43 us  [swap(): return lax.ppermute(x, axis, [(i, i ^ bits) for i in range(size)])]
    ppermute x2, starting transfers between devices: 5.23 us -> 3.2 us  [per_device(): lax.ppermute(own, 'gy', list(enumerate(t)))]
    ppermute x16 -> x8, waiting for transfers between devices: 7.46 us -> 7.48 us  [both_sides(): there = lax.ppermute(jnp.where(even, down, up), axis, far)]
where the time goes in v5:
time: 69.1 us; the launch traced here: 68.9 us
  starting transfers between devices  30.9 us (45%)
  waiting for transfers between devices  19.5 us (28%)
  Pallas kernels  16.1 us (23%)
  local copies, waits for them, and re-layouts  1.79 us (3%)
    ppermute x14, starting transfers between devices, swap(): return lax.ppermute(x, axis, [(i, i ^ bits) for i in range(size)])  21.1 us
    pallas_call x9, Pallas kernels, call(): pl.pallas_call(kernel, out_shape=[jax.ShapeDtypeStruct(s, F32) for s in o...  16.1 us
    ppermute x8, waiting for transfers between devices, both_sides(): there = lax.ppermute(jnp.where(even, down, up), axis, far)  7.48 us
    ppermute x14, waiting for transfers between devices, swap(): return lax.ppermute(x, axis, [(i, i ^ bits) for i in range(size)])  7.43 us
    ppermute x8, starting transfers between devices, both_sides(): there = lax.ppermute(jnp.where(even, down, up), axis, far)  6.65 us
    ppermute x2, waiting for transfers between devices, per_device(): lax.ppermute(own, 'gy', list(enumerate(t)))  4.54 us
    ppermute x2, starting transfers between devices, per_device(): lax.ppermute(own, 'gy', list(enumerate(t)))  3.2 us
    slice x3, local copies, waits for them, and re-layouts, per_device(): down = jnp.concatenate([f[:3], m[:3], k[:4]])  1.76 us
  transfers between devices with their start and end apart: 24, of which 10 were waited for; matrix products, arithmetic and copies ran while one was open for 0% of the time, Pallas kernels for 12%

profile of v5, /device:TPU:64, one launch (start us, length us, event | category | flops | bytes accessed | tf_op | source)
XLA Modules:
  0.0 68.9 jit_solution(8802790208611653454)
XLA Ops:
  0.0 0.9 %fusion.4 = (f32[4,32,128]{2,1,0:T(8,128)S(1)}, f32[4,32,128]{2,1,0:T(8,128)S(1)}) fusion(f32[16,32,128]{2,1,0:T(8,128)} %k.5), kind=kLoop, calls=%fused_computation.37 | loop fusion | bytes 262144 | tf_op jit(solution)/shard_map/slice | solution.py:579
  0.9 0.8 %fusion.2 = (f32[3,32,128]{2,1,0:T(8,128)S(1)}, f32[3,32,128]{2,1,0:T(8,128)S(1)}) fusion(f32[16,32,128]{2,1,0:T(8,128)} %f.3), kind=kLoop, calls=%fused_computation.35 | loop fusion | bytes 196608 | tf_op jit(solution)/shard_map/slice | solution.py:579
  1.8 0.0 copy-start
  1.8 3.1 %collective-permute-start = (f32[10,32,128]{2,1,0:T(8,128)S(1)}, f32[10,32,128]{2,1,0:T(8,128)S(1)}, u32[]{:S(2)}, u32[]{:S(2)}) collective-permute-start(f32[10,32,128]{2,1,0:T(8,128)S(1)} %get-tuple-element.98), channel_id=1, source_target_pairs={{0,192},{64,128},{128,64},{192,0},{1,193},{65,129},{129,65},{193,1... | collective-permute-start | bytes 491528 | tf_op jit(solution)/shard_map/ppermute | solution.py:560
  4.9 0.1 collective-permute-start.1
  5.1 0.2 coarse_kernel.1
  5.3 2.0 %collective-permute-start.13 = (f32[8,16,128]{2,1,0:T(8,128)S(1)}, f32[8,16,128]{2,1,0:T(8,128)S(1)}, u32[]{:S(2)}, u32[]{:S(2)}) collective-permute-start(f32[8,16,128]{2,1,0:T(8,128)S(1)} %coarse_kernel.1), channel_id=1, source_target_pairs={{0,64},{64,0},{128,192},{192,128},{1,65},{65,1},{129,193},{193,129... | collective-permute-start | bytes 196616 | tf_op jit(solution)/shard_map/ppermute | solution.py:543
  7.3 0.6 collective-permute-start.14
  7.9 2.2 %collective-permute-start.15 = (f32[8,16,128]{2,1,0:T(8,128)S(1)}, f32[8,16,128]{2,1,0:T(8,128)S(1)}, u32[]{:S(2)}, u32[]{:S(2)}) collective-permute-start(f32[8,16,128]{2,1,0:T(8,128)S(1)} %coarse_kernel.1), channel_id=1, source_target_pairs={{0,192},{64,128},{128,64},{192,0},{1,193},{65,129},{129,65},{193,1... | collective-permute-start | bytes 196616 | tf_op jit(solution)/shard_map/ppermute | solution.py:543
  10.1 0.0 collective-permute-done
  10.1 1.9 %collective-permute-done.1 = f32[10,32,128]{2,1,0:T(8,128)S(1)} collective-permute-done((f32[10,32,128]{2,1,0:T(8,128)S(1)}, f32[10,32,128]{2,1,0:T(8,128)S(1)}, u32[]{:S(2)}, u32[]{:S(2)}) %collective-permute-start.1) | collective-permute-done | bytes 163872 | tf_op jit(solution)/shard_map/ppermute | solution.py:543
  12.1 0.2 collective-permute-start.2
  12.3 4.9 %collective-permute-start.3 = (f32[184,128]{1,0:T(8,128)S(1)}, f32[184,128]{1,0:T(8,128)S(1)}, u32[]{:S(2)}, u32[]{:S(2)}) collective-permute-start(f32[184,128]{1,0:T(8,128)S(1)} %get-tuple-element.113), channel_id=1, source_target_pairs={{0,8},{8,0},{16,24},{24,16},{32,40},{40,32},{48,56},{56,48},{1,9},... | collective-permute-start | bytes 282632 | tf_op jit(solution)/shard_map/ppermute | solution.py:543
  17.2 0.1 pad_add_fusion.pos
  17.3 2.5 %collective-permute-done.3 = f32[184,128]{1,0:T(8,128)S(1)} collective-permute-done((f32[184,128]{1,0:T(8,128)S(1)}, f32[184,128]{1,0:T(8,128)S(1)}, u32[]{:S(2)}, u32[]{:S(2)}) %collective-permute-start.3) | collective-permute-done | bytes 94240 | tf_op jit(solution)/shard_map/ppermute | solution.py:543
  19.8 0.5 pack_z_kernel.1
  20.4 0.1 collective-permute-start.4
  20.5 1.6 %collective-permute-start.5 = (f32[3,40,128]{2,1,0:T(8,128)S(1)}, f32[3,40,128]{2,1,0:T(8,128)S(1)}, u32[]{:S(2)}, u32[]{:S(2)}) collective-permute-start(f32[3,40,128]{2,1,0:T(8,128)S(1)} %get-tuple-element.117), channel_id=1, source_target_pairs={{0,1},{1,0},{2,3},{3,2},{4,5},{5,4},{6,7},{7,6},{8,9},{9,8},{10,11... | collective-permute-start | bytes 184328 | tf_op jit(solution)/shard_map/ppermute | solution.py:543
  22.1 0.0 collective-permute-done.13
  22.1 0.0 collective-permute-done.14
  22.1 1.1 %collective-permute-start.16 = (f32[32,16,128]{2,1,0:T(8,128)S(1)}, f32[32,16,128]{2,1,0:T(8,128)S(1)}, u32[]{:S(2)}, u32[]{:S(2)}) collective-permute-start(f32[32,16,128]{2,1,0:T(8,128)S(1)} %pad_maximum_fusion.own), channel_id=1, source_target_pairs={{0,56},{8,16},{16,8},{24,32},{32,24},{40,48},{48,40},{56,0},{1,57}... | collective-permute-start | bytes 786440 | tf_op jit(solution)/shard_map/ppermute | solution.py:560
  23.2 2.2 %collective-permute-start.17 = (f32[32,16,128]{2,1,0:T(8,128)S(1)}, f32[32,16,128]{2,1,0:T(8,128)S(1)}, u32[]{:S(2)}, u32[]{:S(2)}) collective-permute-start(f32[32,16,128]{2,1,0:T(8,128)S(1)} %pad_maximum_fusion.own), channel_id=1, source_target_pairs={{0,8},{8,0},{16,24},{24,16},{32,40},{40,32},{48,56},{56,48},{1,9},... | collective-permute-start | bytes 786440 | tf_op jit(solution)/shard_map/ppermute | solution.py:543
  25.5 3.5 %fine_kernel.1 = (f32[4,16,128]{2,1,0:T(8,128)S(1)}, f32[24,40,256]{2,1,0:T(8,128)S(1)}, f32[24,40,256]{2,1,0:T(8,128)S(1)}, f32[24,40,256]{2,1,0:T(8,128)S(1)},...) custom-call(s32[3]{0:T(128)S(1)} %pad_add_fusion.pos, ...), custom_call_target="tpu_custom_call" | custom-call | tf_op jit(solution)/shard_map/fine_kernel/pallas_call | solution.py:530
  29.0 0.2 collective-permute-start.6
  29.2 1.5 %collective-permute-start.7 = (f32[4,16,128]{2,1,0:T(8,128)S(1)}, f32[4,16,128]{2,1,0:T(8,128)S(1)}, u32[]{:S(2)}, u32[]{:S(2)}) collective-permute-start(f32[4,16,128]{2,1,0:T(8,128)S(1)} %get-tuple-element.54), channel_id=1, source_target_pairs={{0,128},{64,192},{128,0},{192,64},{1,129},{65,193},{129,1},{193,65... | collective-permute-start | bytes 98312 | tf_op jit(solution)/shard_map/ppermute | solution.py:543
  30.8 3.0 %collective-permute-start.8 = (f32[4,16,128]{2,1,0:T(8,128)S(1)}, f32[4,16,128]{2,1,0:T(8,128)S(1)}, u32[]{:S(2)}, u32[]{:S(2)}) collective-permute-start(f32[4,16,128]{2,1,0:T(8,128)S(1)} %get-tuple-element.54), channel_id=1, source_target_pairs={{0,192},{64,128},{128,64},{192,0},{1,193},{65,129},{129,65},{193,1... | collective-permute-start | bytes 98312 | tf_op jit(solution)/shard_map/ppermute | solution.py:543
  33.8 0.4 pack_z1_kernel.3
  34.2 0.4 collective-permute-done.7
  34.7 1.2 %collective-permute-done.8 = f32[4,16,128]{2,1,0:T(8,128)S(1)} collective-permute-done((f32[4,16,128]{2,1,0:T(8,128)S(1)}, f32[4,16,128]{2,1,0:T(8,128)S(1)}, u32[]{:S(2)}, u32[]{:S(2)}) %collective-permute-start.8) | collective-permute-done | bytes 32800 | tf_op jit(solution)/shard_map/ppermute | solution.py:543
  35.9 1.9 %collective-permute-start.10 = (f32[16,16,128]{2,1,0:T(8,128)S(1)}, f32[16,16,128]{2,1,0:T(8,128)S(1)}, u32[]{:S(2)}, u32[]{:S(2)}) collective-permute-start(f32[16,16,128]{2,1,0:T(8,128)S(1)} %constant_dynamic-update-slice_fusion.own), channel_id=1, source_target_pairs={{0,8},{8,0},{16,24},{24,16},{32,40},{40,32},{48,56},{56,48},{1,9},... | collective-permute-start | bytes 393224 | tf_op jit(solution)/shard_map/ppermute | solution.py:543
  37.8 1.0 %collective-permute-start.9 = (f32[16,16,128]{2,1,0:T(8,128)S(1)}, f32[16,16,128]{2,1,0:T(8,128)S(1)}, u32[]{:S(2)}, u32[]{:S(2)}) collective-permute-start(f32[16,16,128]{2,1,0:T(8,128)S(1)} %constant_dynamic-update-slice_fusion.own), channel_id=1, source_target_pairs={{0,56},{8,16},{16,8},{24,32},{32,24},{40,48},{48,40},{56,0},{1,57}... | collective-permute-start | bytes 393224 | tf_op jit(solution)/shard_map/ppermute | solution.py:560
  38.9 0.3 collective-permute-start.18
  39.1 0.4 collective-permute-start.19
  39.5 1.3 %collective-permute-done.10 = f32[16,16,128]{2,1,0:T(8,128)S(1)} collective-permute-done((f32[16,16,128]{2,1,0:T(8,128)S(1)}, f32[16,16,128]{2,1,0:T(8,128)S(1)}, u32[]{:S(2)}, u32[]{:S(2)}) %collective-permute-start.10) | collective-permute-done | bytes 131104 | tf_op jit(solution)/shard_map/ppermute | solution.py:543
  40.9 1.9 %collective-permute-done.9 = f32[16,16,128]{2,1,0:T(8,128)S(1)} collective-permute-done((f32[16,16,128]{2,1,0:T(8,128)S(1)}, f32[16,16,128]{2,1,0:T(8,128)S(1)}, u32[]{:S(2)}, u32[]{:S(2)}) %collective-permute-start.9) | collective-permute-done | bytes 131104 | tf_op jit(solution)/shard_map/ppermute | solution.py:560
  42.8 0.2 pack_z1_kernel.2
  43.0 0.1 collective-permute-start.11
  43.1 0.4 collective-permute-start.12
  43.5 1.9 %collective-permute-done.18 = f32[8,48,128]{2,1,0:T(8,128)S(1)} collective-permute-done((f32[8,48,128]{2,1,0:T(8,128)S(1)}, f32[8,48,128]{2,1,0:T(8,128)S(1)}, u32[]{:S(2)}, u32[]{:S(2)}) %collective-permute-start.18) | collective-permute-done | bytes 196640 | tf_op jit(solution)/shard_map/ppermute | solution.py:560
  45.5 3.4 %static_kernel.1 = (f32[2,8,128]{2,1,0:T(8,128)S(1)}, f32[40,48,128]{2,1,0:T(8,128)S(1)}, f32[40,48,128]{2,1,0:T(8,128)S(1)}, f32[40,48,128]{2,1,0:T(8,128)S(1)}...) custom-call(s32[3]{0:T(128)S(1)} %pad_add_fusion.pos, ...), custom_call_target="tpu_custom_call" | custom-call | tf_op jit(solution)/shard_map/static_kernel/pallas_call | solution.py:530
  48.9 3.3 %middle_kernel.1 = (f32[3,8,128]{2,1,0:T(8,128)S(1)}, f32[16,24,128]{2,1,0:T(8,128)S(1)}, f32[16,24,128]{2,1,0:T(8,128)S(1)}, f32[12,16,128]{2,1,0:T(8,128)S(1)}, f32[12,16,128]{2,1,0:T(8,128)S(1)}) custom-call(s32[3]{0:T(128)S(1)} %pad_add_fusion.pos, f32[16,16,128]{2,1,0:T(8,128)S(1)} %constant_dynamic-update-slice_fusion.own, ...), custom_call_target="tpu_custom_call" | custom-call | tf_op jit(solution)/shard_map/middle_kernel/pallas_call | solution.py:530
  52.3 0.8 %collective-permute-start.20 = (f32[3,8,128]{2,1,0:T(8,128)S(1)}, f32[3,8,128]{2,1,0:T(8,128)S(1)}, u32[]{:S(2)}, u32[]{:S(2)}) collective-permute-start(f32[3,8,128]{2,1,0:T(8,128)S(1)} %get-tuple-element.70), channel_id=1, source_target_pairs={{0,7},{1,2},{2,1},{3,4},{4,3},{5,6},{6,5},{7,0},{8,15},{9,10},{10,... | collective-permute-start | bytes 36872 | tf_op jit(solution)/shard_map/ppermute | solution.py:560
  53.0 3.7 %collective-permute-done.20 = f32[3,8,128]{2,1,0:T(8,128)S(1)} collective-permute-done((f32[3,8,128]{2,1,0:T(8,128)S(1)}, f32[3,8,128]{2,1,0:T(8,128)S(1)}, u32[]{:S(2)}, u32[]{:S(2)}) %collective-permute-start.20) | collective-permute-done | bytes 12320 | tf_op jit(solution)/shard_map/ppermute | solution.py:560
  56.7 1.7 %collective-permute-start.22 = (f32[9,8,128]{2,1,0:T(8,128)S(1)}, f32[9,8,128]{2,1,0:T(8,128)S(1)}, u32[]{:S(2)}, u32[]{:S(2)}) collective-permute-start(f32[9,8,128]{2,1,0:T(8,128)S(1)} %pad_maximum_fusion.3.own), channel_id=1, source_target_pairs={{0,16},{8,24},{16,0},{24,8},{32,48},{40,56},{48,32},{56,40},{1,17}... | collective-permute-start | bytes 110600 | tf_op jit(solution)/shard_map/ppermute | solution.py:623
  58.4 1.5 %collective-permute-start.23 = (f32[9,8,128]{2,1,0:T(8,128)S(1)}, f32[9,8,128]{2,1,0:T(8,128)S(1)}, u32[]{:S(2)}, u32[]{:S(2)}) collective-permute-start(f32[9,8,128]{2,1,0:T(8,128)S(1)} %pad_maximum_fusion.3.own), channel_id=1, source_target_pairs={{0,8},{8,0},{16,32},{24,40},{32,16},{40,24},{48,56},{56,48},{1,9},... | collective-permute-start | bytes 110600 | tf_op jit(solution)/shard_map/ppermute | solution.py:623
  59.9 1.8 %collective-permute-done.22.first = f32[9,8,128]{2,1,0:T(8,128)S(1)} collective-permute-done((f32[9,8,128]{2,1,0:T(8,128)S(1)}, f32[9,8,128]{2,1,0:T(8,128)S(1)}, u32[]{:S(2)}, u32[]{:S(2)}) %collective-permute-start.22) | collective-permute-done | bytes 36896 | tf_op jit(solution)/shard_map/ppermute | solution.py:623
  61.7 2.8 %collective-permute-done.23.second = f32[9,8,128]{2,1,0:T(8,128)S(1)} collective-permute-done((f32[9,8,128]{2,1,0:T(8,128)S(1)}, f32[9,8,128]{2,1,0:T(8,128)S(1)}, u32[]{:S(2)}, u32[]{:S(2)}) %collective-permute-start.23) | collective-permute-done | bytes 36896 | tf_op jit(solution)/shard_map/ppermute | solution.py:623
  64.4 4.5 %last_kernel.1 = f32[16,32,128]{2,1,0:T(8,128)} custom-call(s32[3]{0:T(128)S(1)} %pad_add_fusion.pos, f32[9,8,128]{2,1,0:T(8,128)S(1)} %pad_maximum_fusion.3.own, f32[9,8,128]{2,1,0:T(8,128)S(1)} %collective-permute-done.22.first, f32[9,8,128]{2,1,0:T(8,128)S(1)} %collective-permute-done.23.second, f32[24,40,256]{2,1,0:T(8,128)S(1)} %get-tuple-element.71.v0, ...), custom_call_target="tpu_custom_call" | custom-call | tf_op jit(solution)/shard_map/last_kernel/pallas_call | solution.py:530
  (38 shorter events, 0.4 us)
Async XLA Ops:
  0.0 1.8 %copy-start.1 = (f32[16,32,128]{2,1,0:T(8,128)S(1)}, f32[16,32,128]{2,1,0:T(8,128)}, u32[]{:S(2)}) copy-start(f32[16,32,128]{2,1,0:T(8,128)} %m.5) | copy-start | bytes 786436
  1.8 3.3 %copy-start = (f32[16,32,128]{2,1,0:T(8,128)S(1)}, f32[16,32,128]{2,1,0:T(8,128)}, u32[]{:S(2)}) copy-start(f32[16,32,128]{2,1,0:T(8,128)} %k.5) | copy-start | bytes 786436
  1.8 8.3 %collective-permute-start = (f32[10,32,128]{2,1,0:T(8,128)S(1)}, f32[10,32,128]{2,1,0:T(8,128)S(1)}, u32[]{:S(2)}, u32[]{:S(2)}) collective-permute-start(f32[10,32,128]{2,1,0:T(8,128)S(1)} %get-tuple-element.98), channel_id=1, source_target_pairs={{0,192},{64,128},{128,64},{192,0},{1,193},{65,129},{129,65},{193,1... | collective-permute-start | bytes 491528 | tf_op jit(solution)/shard_map/ppermute | solution.py:560
  4.9 7.1 %collective-permute-start.1 = (f32[10,32,128]{2,1,0:T(8,128)S(1)}, f32[10,32,128]{2,1,0:T(8,128)S(1)}, u32[]{:S(2)}, u32[]{:S(2)}) collective-permute-start(f32[10,32,128]{2,1,0:T(8,128)S(1)} %get-tuple-element.97), channel_id=1, source_target_pairs={{0,64},{64,0},{128,192},{192,128},{1,65},{65,1},{129,193},{193,129... | collective-permute-start | bytes 491528 | tf_op jit(solution)/shard_map/ppermute | solution.py:543
  5.3 16.8 %collective-permute-start.13 = (f32[8,16,128]{2,1,0:T(8,128)S(1)}, f32[8,16,128]{2,1,0:T(8,128)S(1)}, u32[]{:S(2)}, u32[]{:S(2)}) collective-permute-start(f32[8,16,128]{2,1,0:T(8,128)S(1)} %coarse_kernel.1), channel_id=1, source_target_pairs={{0,64},{64,0},{128,192},{192,128},{1,65},{65,1},{129,193},{193,129... | collective-permute-start | bytes 196616 | tf_op jit(solution)/shard_map/ppermute | solution.py:543
  7.3 14.8 %collective-permute-start.14 = (f32[8,16,128]{2,1,0:T(8,128)S(1)}, f32[8,16,128]{2,1,0:T(8,128)S(1)}, u32[]{:S(2)}, u32[]{:S(2)}) collective-permute-start(f32[8,16,128]{2,1,0:T(8,128)S(1)} %coarse_kernel.1), channel_id=1, source_target_pairs={{0,128},{64,192},{128,0},{192,64},{1,129},{65,193},{129,1},{193,65... | collective-permute-start | bytes 196616 | tf_op jit(solution)/shard_map/ppermute | solution.py:543
  7.9 14.2 %collective-permute-start.15 = (f32[8,16,128]{2,1,0:T(8,128)S(1)}, f32[8,16,128]{2,1,0:T(8,128)S(1)}, u32[]{:S(2)}, u32[]{:S(2)}) collective-permute-start(f32[8,16,128]{2,1,0:T(8,128)S(1)} %coarse_kernel.1), channel_id=1, source_target_pairs={{0,192},{64,128},{128,64},{192,0},{1,193},{65,129},{129,65},{193,1... | collective-permute-start | bytes 196616 | tf_op jit(solution)/shard_map/ppermute | solution.py:543
  10.1 1.9 %copy-start.2 = (f32[16,32,128]{2,1,0:T(8,128)S(1)}, f32[16,32,128]{2,1,0:T(8,128)}, u32[]{:S(2)}) copy-start(f32[16,32,128]{2,1,0:T(8,128)} %f.3) | copy-start | bytes 786436
  12.1 5.2 %collective-permute-start.2 = (f32[184,128]{1,0:T(8,128)S(1)}, f32[184,128]{1,0:T(8,128)S(1)}, u32[]{:S(2)}, u32[]{:S(2)}) collective-permute-start(f32[184,128]{1,0:T(8,128)S(1)} %get-tuple-element.114), channel_id=1, source_target_pairs={{0,56},{8,16},{16,8},{24,32},{32,24},{40,48},{48,40},{56,0},{1,57}... | collective-permute-start | bytes 282632 | tf_op jit(solution)/shard_map/ppermute | solution.py:560
  12.3 7.5 %collective-permute-start.3 = (f32[184,128]{1,0:T(8,128)S(1)}, f32[184,128]{1,0:T(8,128)S(1)}, u32[]{:S(2)}, u32[]{:S(2)}) collective-permute-start(f32[184,128]{1,0:T(8,128)S(1)} %get-tuple-element.113), channel_id=1, source_target_pairs={{0,8},{8,0},{16,24},{24,16},{32,40},{40,32},{48,56},{56,48},{1,9},... | collective-permute-start | bytes 282632 | tf_op jit(solution)/shard_map/ppermute | solution.py:543
  20.4 5.1 %collective-permute-start.4 = (f32[3,40,128]{2,1,0:T(8,128)S(1)}, f32[3,40,128]{2,1,0:T(8,128)S(1)}, u32[]{:S(2)}, u32[]{:S(2)}) collective-permute-start(f32[3,40,128]{2,1,0:T(8,128)S(1)} %get-tuple-element.118), channel_id=1, source_target_pairs={{0,7},{1,2},{2,1},{3,4},{4,3},{5,6},{6,5},{7,0},{8,15},{9,10},{10,... | collective-permute-start | bytes 184328 | tf_op jit(solution)/shard_map/ppermute | solution.py:560
  20.5 5.0 %collective-permute-start.5 = (f32[3,40,128]{2,1,0:T(8,128)S(1)}, f32[3,40,128]{2,1,0:T(8,128)S(1)}, u32[]{:S(2)}, u32[]{:S(2)}) collective-permute-start(f32[3,40,128]{2,1,0:T(8,128)S(1)} %get-tuple-element.117), channel_id=1, source_target_pairs={{0,1},{1,0},{2,3},{3,2},{4,5},{5,4},{6,7},{7,6},{8,9},{9,8},{10,11... | collective-permute-start | bytes 184328 | tf_op jit(solution)/shard_map/ppermute | solution.py:543
  22.1 11.6 %collective-permute-start.16 = (f32[32,16,128]{2,1,0:T(8,128)S(1)}, f32[32,16,128]{2,1,0:T(8,128)S(1)}, u32[]{:S(2)}, u32[]{:S(2)}) collective-permute-start(f32[32,16,128]{2,1,0:T(8,128)S(1)} %pad_maximum_fusion.own), channel_id=1, source_target_pairs={{0,56},{8,16},{16,8},{24,32},{32,24},{40,48},{48,40},{56,0},{1,57}... | collective-permute-start | bytes 786440 | tf_op jit(solution)/shard_map/ppermute | solution.py:560
  23.2 10.5 %collective-permute-start.17 = (f32[32,16,128]{2,1,0:T(8,128)S(1)}, f32[32,16,128]{2,1,0:T(8,128)S(1)}, u32[]{:S(2)}, u32[]{:S(2)}) collective-permute-start(f32[32,16,128]{2,1,0:T(8,128)S(1)} %pad_maximum_fusion.own), channel_id=1, source_target_pairs={{0,8},{8,0},{16,24},{24,16},{32,40},{40,32},{48,56},{56,48},{1,9},... | collective-permute-start | bytes 786440 | tf_op jit(solution)/shard_map/ppermute | solution.py:543
  29.0 5.2 %collective-permute-start.6 = (f32[4,16,128]{2,1,0:T(8,128)S(1)}, f32[4,16,128]{2,1,0:T(8,128)S(1)}, u32[]{:S(2)}, u32[]{:S(2)}) collective-permute-start(f32[4,16,128]{2,1,0:T(8,128)S(1)} %get-tuple-element.54), channel_id=1, source_target_pairs={{0,64},{64,0},{128,192},{192,128},{1,65},{65,1},{129,193},{193,129... | collective-permute-start | bytes 98312 | tf_op jit(solution)/shard_map/ppermute | solution.py:543
  29.2 5.4 %collective-permute-start.7 = (f32[4,16,128]{2,1,0:T(8,128)S(1)}, f32[4,16,128]{2,1,0:T(8,128)S(1)}, u32[]{:S(2)}, u32[]{:S(2)}) collective-permute-start(f32[4,16,128]{2,1,0:T(8,128)S(1)} %get-tuple-element.54), channel_id=1, source_target_pairs={{0,128},{64,192},{128,0},{192,64},{1,129},{65,193},{129,1},{193,65... | collective-permute-start | bytes 98312 | tf_op jit(solution)/shard_map/ppermute | solution.py:543
  30.8 5.1 %collective-permute-start.8 = (f32[4,16,128]{2,1,0:T(8,128)S(1)}, f32[4,16,128]{2,1,0:T(8,128)S(1)}, u32[]{:S(2)}, u32[]{:S(2)}) collective-permute-start(f32[4,16,128]{2,1,0:T(8,128)S(1)} %get-tuple-element.54), channel_id=1, source_target_pairs={{0,192},{64,128},{128,64},{192,0},{1,193},{65,129},{129,65},{193,1... | collective-permute-start | bytes 98312 | tf_op jit(solution)/shard_map/ppermute | solution.py:543
  35.9 5.0 %collective-permute-start.10 = (f32[16,16,128]{2,1,0:T(8,128)S(1)}, f32[16,16,128]{2,1,0:T(8,128)S(1)}, u32[]{:S(2)}, u32[]{:S(2)}) collective-permute-start(f32[16,16,128]{2,1,0:T(8,128)S(1)} %constant_dynamic-update-slice_fusion.own), channel_id=1, source_target_pairs={{0,8},{8,0},{16,24},{24,16},{32,40},{40,32},{48,56},{56,48},{1,9},... | collective-permute-start | bytes 393224 | tf_op jit(solution)/shard_map/ppermute | solution.py:543
  37.8 5.0 %collective-permute-start.9 = (f32[16,16,128]{2,1,0:T(8,128)S(1)}, f32[16,16,128]{2,1,0:T(8,128)S(1)}, u32[]{:S(2)}, u32[]{:S(2)}) collective-permute-start(f32[16,16,128]{2,1,0:T(8,128)S(1)} %constant_dynamic-update-slice_fusion.own), channel_id=1, source_target_pairs={{0,56},{8,16},{16,8},{24,32},{32,24},{40,48},{48,40},{56,0},{1,57}... | collective-permute-start | bytes 393224 | tf_op jit(solution)/shard_map/ppermute | solution.py:560
  38.9 6.6 %collective-permute-start.18 = (f32[8,48,128]{2,1,0:T(8,128)S(1)}, f32[8,48,128]{2,1,0:T(8,128)S(1)}, u32[]{:S(2)}, u32[]{:S(2)}) collective-permute-start(f32[8,48,128]{2,1,0:T(8,128)S(1)} %get-tuple-element.94), channel_id=1, source_target_pairs={{0,7},{1,2},{2,1},{3,4},{4,3},{5,6},{6,5},{7,0},{8,15},{9,10},{10,... | collective-permute-start | bytes 589832 | tf_op jit(solution)/shard_map/ppermute | solution.py:560
  39.1 6.3 %collective-permute-start.19 = (f32[8,48,128]{2,1,0:T(8,128)S(1)}, f32[8,48,128]{2,1,0:T(8,128)S(1)}, u32[]{:S(2)}, u32[]{:S(2)}) collective-permute-start(f32[8,48,128]{2,1,0:T(8,128)S(1)} %get-tuple-element.93), channel_id=1, source_target_pairs={{0,1},{1,0},{2,3},{3,2},{4,5},{5,4},{6,7},{7,6},{8,9},{9,8},{10,11... | collective-permute-start | bytes 589832 | tf_op jit(solution)/shard_map/ppermute | solution.py:543
  43.0 5.8 %collective-permute-start.11 = (f32[4,48,128]{2,1,0:T(8,128)S(1)}, f32[4,48,128]{2,1,0:T(8,128)S(1)}, u32[]{:S(2)}, u32[]{:S(2)}) collective-permute-start(f32[4,48,128]{2,1,0:T(8,128)S(1)} %get-tuple-element.110), channel_id=1, source_target_pairs={{0,7},{1,2},{2,1},{3,4},{4,3},{5,6},{6,5},{7,0},{8,15},{9,10},{10,... | collective-permute-start | bytes 294920 | tf_op jit(solution)/shard_map/ppermute | solution.py:560
  43.1 5.7 %collective-permute-start.12 = (f32[4,48,128]{2,1,0:T(8,128)S(1)}, f32[4,48,128]{2,1,0:T(8,128)S(1)}, u32[]{:S(2)}, u32[]{:S(2)}) collective-permute-start(f32[4,48,128]{2,1,0:T(8,128)S(1)} %get-tuple-element.109), channel_id=1, source_target_pairs={{0,1},{1,0},{2,3},{3,2},{4,5},{5,4},{6,7},{7,6},{8,9},{9,8},{10,11... | collective-permute-start | bytes 294920 | tf_op jit(solution)/shard_map/ppermute | solution.py:543
  52.3 4.4 %collective-permute-start.20 = (f32[3,8,128]{2,1,0:T(8,128)S(1)}, f32[3,8,128]{2,1,0:T(8,128)S(1)}, u32[]{:S(2)}, u32[]{:S(2)}) collective-permute-start(f32[3,8,128]{2,1,0:T(8,128)S(1)} %get-tuple-element.70), channel_id=1, source_target_pairs={{0,7},{1,2},{2,1},{3,4},{4,3},{5,6},{6,5},{7,0},{8,15},{9,10},{10,... | collective-permute-start | bytes 36872 | tf_op jit(solution)/shard_map/ppermute | solution.py:560
  53.0 3.7 %collective-permute-start.21 = (f32[3,8,128]{2,1,0:T(8,128)S(1)}, f32[3,8,128]{2,1,0:T(8,128)S(1)}, u32[]{:S(2)}, u32[]{:S(2)}) collective-permute-start(f32[3,8,128]{2,1,0:T(8,128)S(1)} %get-tuple-element.70), channel_id=1, source_target_pairs={{0,1},{1,0},{2,3},{3,2},{4,5},{5,4},{6,7},{7,6},{8,9},{9,8},{10,11... | collective-permute-start | bytes 36872 | tf_op jit(solution)/shard_map/ppermute | solution.py:543
  56.7 5.0 %collective-permute-start.22 = (f32[9,8,128]{2,1,0:T(8,128)S(1)}, f32[9,8,128]{2,1,0:T(8,128)S(1)}, u32[]{:S(2)}, u32[]{:S(2)}) collective-permute-start(f32[9,8,128]{2,1,0:T(8,128)S(1)} %pad_maximum_fusion.3.own), channel_id=1, source_target_pairs={{0,16},{8,24},{16,0},{24,8},{32,48},{40,56},{48,32},{56,40},{1,17}... | collective-permute-start | bytes 110600 | tf_op jit(solution)/shard_map/ppermute | solution.py:623
  58.4 6.1 %collective-permute-start.23 = (f32[9,8,128]{2,1,0:T(8,128)S(1)}, f32[9,8,128]{2,1,0:T(8,128)S(1)}, u32[]{:S(2)}, u32[]{:S(2)}) collective-permute-start(f32[9,8,128]{2,1,0:T(8,128)S(1)} %pad_maximum_fusion.3.own), channel_id=1, source_target_pairs={{0,8},{8,0},{16,32},{24,40},{32,16},{40,24},{48,56},{56,48},{1,9},... | collective-permute-start | bytes 110600 | tf_op jit(solution)/shard_map/ppermute | solution.py:623

commit v6 on v5

--- a/solution.py
+++ b/solution.py
@@ -91,6 +91,18 @@
     total = total + y * after(centre, 0) + before(y * centre, 0)
     total = total + z * after(centre, 1) + before(z * centre, 1)
     return total, centre
+
+
+def own_neighbours(p, k, cy, cz, v):
+    rows, lanes = slice(0, 32), slice(0, 128)
+    here = k[p, rows, lanes]
+    total = (k[p - 1, rows, lanes] + here) * v[p - 1, rows, lanes]
+    total = total + (here + k[p + 1, rows, lanes]) * v[p + 1, rows, lanes]
+    centre, y = v[p, :, lanes], cy[p, :, lanes]
+    total = total + (y * after(centre, 0) + before(y * centre, 0))[rows]
+    across, z = v[p, rows], cz[p, rows]
+    total = total + (z * after(across, 1) + before(z * across, 1))[:, lanes]
+    return total, centre[rows]
 
 
 def sweep(low, high, group, k, w, g, cy, cz, v, out):
@@ -227,8 +239,8 @@
     sweep(2, 22, 10, k, w, g, cy, cz, g, v_out)
 
     def residual(p):
-        total, centre = neighbours(p, k, cy, cz, v_out)
-        return (f[p] + total - d[p] * centre)[0:32, 0:128]
+        total, centre = own_neighbours(p, k, cy, cz, v_out)
+        return f[p, 0:32, 0:128] + total - d[p, 0:32, 0:128] * centre
 
     def values(i):
         return residual(2 * i + 4) + residual(2 * i + 5)
@@ -506,13 +518,13 @@
     sweep(3, 21, 9, k0, w0, g0, cy0, cz0, a0, b0)
 
     def values(p):
-        total, centre = neighbours(p, k0, cy0, cz0, b0)
-        return (KEEP * centre + g0[p] + w0[p] * total)[0:32, 0:128]
+        total, centre = own_neighbours(p, k0, cy0, cz0, b0)
+        return KEEP * centre + g0[p, 0:32, 0:128] + w0[p, 0:32, 0:128] * total
 
     def store(p, value):
         out[p - 4] = value
 
-    planes(4, 20, values, store, 8)
+    planes(4, 20, values, store, 16)
 
 
 VMEM = pl.BlockSpec(memory_space=pltpu.VMEM)

time: 69.1 us -> 69 us (level)
  no operation moved by 1% of the time
where the time goes in v6:
time: 69 us; the launch traced here: 68.9 us
  starting transfers between devices  30.9 us (45%)
  waiting for transfers between devices  19.5 us (28%)
  Pallas kernels  16 us (23%)
  local copies, waits for them, and re-layouts  1.79 us (3%)
    ppermute x14, starting transfers between devices, swap(): return lax.ppermute(x, axis, [(i, i ^ bits) for i in range(size)])  21.1 us
    pallas_call x9, Pallas kernels, call(): pl.pallas_call(kernel, out_shape=[jax.ShapeDtypeStruct(s, F32) for s in o...  16 us
    ppermute x8, waiting for transfers between devices, both_sides(): there = lax.ppermute(jnp.where(even, down, up), axis, far)  7.48 us
    ppermute x14, waiting for transfers between devices, swap(): return lax.ppermute(x, axis, [(i, i ^ bits) for i in range(size)])  7.43 us
    ppermute x8, starting transfers between devices, both_sides(): there = lax.ppermute(jnp.where(even, down, up), axis, far)  6.65 us
    ppermute x2, waiting for transfers between devices, per_device(): lax.ppermute(own, 'gy', list(enumerate(t)))  4.54 us
    ppermute x2, starting transfers between devices, per_device(): lax.ppermute(own, 'gy', list(enumerate(t)))  3.2 us
    slice x3, local copies, waits for them, and re-layouts, per_device(): down = jnp.concatenate([f[:3], m[:3], k[:4]])  1.76 us
  transfers between devices with their start and end apart: 24, of which 10 were waited for; matrix products, arithmetic and copies ran while one was open for 0% of the time, Pallas kernels for 12%

profile of v6, /device:TPU:64, one launch (start us, length us, event | category | flops | bytes accessed | tf_op | source)
XLA Modules:
  0.0 68.9 jit_solution(16196417114686191739)
XLA Ops:
  0.0 0.9 %fusion.4 = (f32[4,32,128]{2,1,0:T(8,128)S(1)}, f32[4,32,128]{2,1,0:T(8,128)S(1)}) fusion(f32[16,32,128]{2,1,0:T(8,128)} %k.5), kind=kLoop, calls=%fused_computation.37 | loop fusion | bytes 262144 | tf_op jit(solution)/shard_map/slice | solution.py:591
  0.9 0.8 %fusion.2 = (f32[3,32,128]{2,1,0:T(8,128)S(1)}, f32[3,32,128]{2,1,0:T(8,128)S(1)}) fusion(f32[16,32,128]{2,1,0:T(8,128)} %f.3), kind=kLoop, calls=%fused_computation.35 | loop fusion | bytes 196608 | tf_op jit(solution)/shard_map/slice | solution.py:591
  1.8 0.0 copy-start
  1.8 3.1 %collective-permute-start = (f32[10,32,128]{2,1,0:T(8,128)S(1)}, f32[10,32,128]{2,1,0:T(8,128)S(1)}, u32[]{:S(2)}, u32[]{:S(2)}) collective-permute-start(f32[10,32,128]{2,1,0:T(8,128)S(1)} %get-tuple-element.98), channel_id=1, source_target_pairs={{0,192},{64,128},{128,64},{192,0},{1,193},{65,129},{129,65},{193,1... | collective-permute-start | bytes 491528 | tf_op jit(solution)/shard_map/ppermute | solution.py:572
  4.9 0.1 collective-permute-start.1
  5.1 0.2 coarse_kernel.1
  5.3 2.0 %collective-permute-start.13 = (f32[8,16,128]{2,1,0:T(8,128)S(1)}, f32[8,16,128]{2,1,0:T(8,128)S(1)}, u32[]{:S(2)}, u32[]{:S(2)}) collective-permute-start(f32[8,16,128]{2,1,0:T(8,128)S(1)} %coarse_kernel.1), channel_id=1, source_target_pairs={{0,64},{64,0},{128,192},{192,128},{1,65},{65,1},{129,193},{193,129... | collective-permute-start | bytes 196616 | tf_op jit(solution)/shard_map/ppermute | solution.py:555
  7.3 0.6 collective-permute-start.14
  7.9 2.2 %collective-permute-start.15 = (f32[8,16,128]{2,1,0:T(8,128)S(1)}, f32[8,16,128]{2,1,0:T(8,128)S(1)}, u32[]{:S(2)}, u32[]{:S(2)}) collective-permute-start(f32[8,16,128]{2,1,0:T(8,128)S(1)} %coarse_kernel.1), channel_id=1, source_target_pairs={{0,192},{64,128},{128,64},{192,0},{1,193},{65,129},{129,65},{193,1... | collective-permute-start | bytes 196616 | tf_op jit(solution)/shard_map/ppermute | solution.py:555
  10.1 0.0 collective-permute-done
  10.1 1.9 %collective-permute-done.1 = f32[10,32,128]{2,1,0:T(8,128)S(1)} collective-permute-done((f32[10,32,128]{2,1,0:T(8,128)S(1)}, f32[10,32,128]{2,1,0:T(8,128)S(1)}, u32[]{:S(2)}, u32[]{:S(2)}) %collective-permute-start.1) | collective-permute-done | bytes 163872 | tf_op jit(solution)/shard_map/ppermute | solution.py:555
  12.1 0.2 collective-permute-start.2
  12.3 4.9 %collective-permute-start.3 = (f32[184,128]{1,0:T(8,128)S(1)}, f32[184,128]{1,0:T(8,128)S(1)}, u32[]{:S(2)}, u32[]{:S(2)}) collective-permute-start(f32[184,128]{1,0:T(8,128)S(1)} %get-tuple-element.113), channel_id=1, source_target_pairs={{0,8},{8,0},{16,24},{24,16},{32,40},{40,32},{48,56},{56,48},{1,9},... | collective-permute-start | bytes 282632 | tf_op jit(solution)/shard_map/ppermute | solution.py:555
  17.2 0.1 pad_add_fusion.pos
  17.3 2.5 %collective-permute-done.3 = f32[184,128]{1,0:T(8,128)S(1)} collective-permute-done((f32[184,128]{1,0:T(8,128)S(1)}, f32[184,128]{1,0:T(8,128)S(1)}, u32[]{:S(2)}, u32[]{:S(2)}) %collective-permute-start.3) | collective-permute-done | bytes 94240 | tf_op jit(solution)/shard_map/ppermute | solution.py:555
  19.8 0.5 pack_z_kernel.1
  20.4 0.1 collective-permute-start.4
  20.5 1.6 %collective-permute-start.5 = (f32[3,40,128]{2,1,0:T(8,128)S(1)}, f32[3,40,128]{2,1,0:T(8,128)S(1)}, u32[]{:S(2)}, u32[]{:S(2)}) collective-permute-start(f32[3,40,128]{2,1,0:T(8,128)S(1)} %get-tuple-element.117), channel_id=1, source_target_pairs={{0,1},{1,0},{2,3},{3,2},{4,5},{5,4},{6,7},{7,6},{8,9},{9,8},{10,11... | collective-permute-start | bytes 184328 | tf_op jit(solution)/shard_map/ppermute | solution.py:555
  22.1 0.0 collective-permute-done.13
  22.1 0.0 collective-permute-done.14
  22.1 1.1 %collective-permute-start.16 = (f32[32,16,128]{2,1,0:T(8,128)S(1)}, f32[32,16,128]{2,1,0:T(8,128)S(1)}, u32[]{:S(2)}, u32[]{:S(2)}) collective-permute-start(f32[32,16,128]{2,1,0:T(8,128)S(1)} %pad_maximum_fusion.own), channel_id=1, source_target_pairs={{0,56},{8,16},{16,8},{24,32},{32,24},{40,48},{48,40},{56,0},{1,57}... | collective-permute-start | bytes 786440 | tf_op jit(solution)/shard_map/ppermute | solution.py:572
  23.2 2.2 %collective-permute-start.17 = (f32[32,16,128]{2,1,0:T(8,128)S(1)}, f32[32,16,128]{2,1,0:T(8,128)S(1)}, u32[]{:S(2)}, u32[]{:S(2)}) collective-permute-start(f32[32,16,128]{2,1,0:T(8,128)S(1)} %pad_maximum_fusion.own), channel_id=1, source_target_pairs={{0,8},{8,0},{16,24},{24,16},{32,40},{40,32},{48,56},{56,48},{1,9},... | collective-permute-start | bytes 786440 | tf_op jit(solution)/shard_map/ppermute | solution.py:555
  25.5 3.5 %fine_kernel.1 = (f32[4,16,128]{2,1,0:T(8,128)S(1)}, f32[24,40,256]{2,1,0:T(8,128)S(1)}, f32[24,40,256]{2,1,0:T(8,128)S(1)}, f32[24,40,256]{2,1,0:T(8,128)S(1)},...) custom-call(s32[3]{0:T(128)S(1)} %pad_add_fusion.pos, ...), custom_call_target="tpu_custom_call" | custom-call | tf_op jit(solution)/shard_map/fine_kernel/pallas_call | solution.py:542
  29.0 0.2 collective-permute-start.6
  29.2 1.5 %collective-permute-start.7 = (f32[4,16,128]{2,1,0:T(8,128)S(1)}, f32[4,16,128]{2,1,0:T(8,128)S(1)}, u32[]{:S(2)}, u32[]{:S(2)}) collective-permute-start(f32[4,16,128]{2,1,0:T(8,128)S(1)} %get-tuple-element.54), channel_id=1, source_target_pairs={{0,128},{64,192},{128,0},{192,64},{1,129},{65,193},{129,1},{193,65... | collective-permute-start | bytes 98312 | tf_op jit(solution)/shard_map/ppermute | solution.py:555
  30.8 3.0 %collective-permute-start.8 = (f32[4,16,128]{2,1,0:T(8,128)S(1)}, f32[4,16,128]{2,1,0:T(8,128)S(1)}, u32[]{:S(2)}, u32[]{:S(2)}) collective-permute-start(f32[4,16,128]{2,1,0:T(8,128)S(1)} %get-tuple-element.54), channel_id=1, source_target_pairs={{0,192},{64,128},{128,64},{192,0},{1,193},{65,129},{129,65},{193,1... | collective-permute-start | bytes 98312 | tf_op jit(solution)/shard_map/ppermute | solution.py:555
  33.8 0.4 pack_z1_kernel.3
  34.2 0.4 collective-permute-done.7
  34.7 1.2 %collective-permute-done.8 = f32[4,16,128]{2,1,0:T(8,128)S(1)} collective-permute-done((f32[4,16,128]{2,1,0:T(8,128)S(1)}, f32[4,16,128]{2,1,0:T(8,128)S(1)}, u32[]{:S(2)}, u32[]{:S(2)}) %collective-permute-start.8) | collective-permute-done | bytes 32800 | tf_op jit(solution)/shard_map/ppermute | solution.py:555
  35.9 1.9 %collective-permute-start.10 = (f32[16,16,128]{2,1,0:T(8,128)S(1)}, f32[16,16,128]{2,1,0:T(8,128)S(1)}, u32[]{:S(2)}, u32[]{:S(2)}) collective-permute-start(f32[16,16,128]{2,1,0:T(8,128)S(1)} %constant_dynamic-update-slice_fusion.own), channel_id=1, source_target_pairs={{0,8},{8,0},{16,24},{24,16},{32,40},{40,32},{48,56},{56,48},{1,9},... | collective-permute-start | bytes 393224 | tf_op jit(solution)/shard_map/ppermute | solution.py:555
  37.8 1.0 %collective-permute-start.9 = (f32[16,16,128]{2,1,0:T(8,128)S(1)}, f32[16,16,128]{2,1,0:T(8,128)S(1)}, u32[]{:S(2)}, u32[]{:S(2)}) collective-permute-start(f32[16,16,128]{2,1,0:T(8,128)S(1)} %constant_dynamic-update-slice_fusion.own), channel_id=1, source_target_pairs={{0,56},{8,16},{16,8},{24,32},{32,24},{40,48},{48,40},{56,0},{1,57}... | collective-permute-start | bytes 393224 | tf_op jit(solution)/shard_map/ppermute | solution.py:572
  38.9 0.3 collective-permute-start.18
  39.2 0.4 collective-permute-start.19
  39.5 1.3 %collective-permute-done.10 = f32[16,16,128]{2,1,0:T(8,128)S(1)} collective-permute-done((f32[16,16,128]{2,1,0:T(8,128)S(1)}, f32[16,16,128]{2,1,0:T(8,128)S(1)}, u32[]{:S(2)}, u32[]{:S(2)}) %collective-permute-start.10) | collective-permute-done | bytes 131104 | tf_op jit(solution)/shard_map/ppermute | solution.py:555
  40.9 1.9 %collective-permute-done.9 = f32[16,16,128]{2,1,0:T(8,128)S(1)} collective-permute-done((f32[16,16,128]{2,1,0:T(8,128)S(1)}, f32[16,16,128]{2,1,0:T(8,128)S(1)}, u32[]{:S(2)}, u32[]{:S(2)}) %collective-permute-start.9) | collective-permute-done | bytes 131104 | tf_op jit(solution)/shard_map/ppermute | solution.py:572
  42.8 0.2 pack_z1_kernel.2
  43.1 0.1 collective-permute-start.11
  43.2 0.4 collective-permute-start.12
  43.6 1.9 %collective-permute-done.18 = f32[8,48,128]{2,1,0:T(8,128)S(1)} collective-permute-done((f32[8,48,128]{2,1,0:T(8,128)S(1)}, f32[8,48,128]{2,1,0:T(8,128)S(1)}, u32[]{:S(2)}, u32[]{:S(2)}) %collective-permute-start.18) | collective-permute-done | bytes 196640 | tf_op jit(solution)/shard_map/ppermute | solution.py:572
  45.5 3.4 %static_kernel.1 = (f32[2,8,128]{2,1,0:T(8,128)S(1)}, f32[40,48,128]{2,1,0:T(8,128)S(1)}, f32[40,48,128]{2,1,0:T(8,128)S(1)}, f32[40,48,128]{2,1,0:T(8,128)S(1)}...) custom-call(s32[3]{0:T(128)S(1)} %pad_add_fusion.pos, ...), custom_call_target="tpu_custom_call" | custom-call | tf_op jit(solution)/shard_map/static_kernel/pallas_call | solution.py:542
  48.9 3.3 %middle_kernel.1 = (f32[3,8,128]{2,1,0:T(8,128)S(1)}, f32[16,24,128]{2,1,0:T(8,128)S(1)}, f32[16,24,128]{2,1,0:T(8,128)S(1)}, f32[12,16,128]{2,1,0:T(8,128)S(1)}, f32[12,16,128]{2,1,0:T(8,128)S(1)}) custom-call(s32[3]{0:T(128)S(1)} %pad_add_fusion.pos, f32[16,16,128]{2,1,0:T(8,128)S(1)} %constant_dynamic-update-slice_fusion.own, ...), custom_call_target="tpu_custom_call" | custom-call | tf_op jit(solution)/shard_map/middle_kernel/pallas_call | solution.py:542
  52.3 0.8 %collective-permute-start.20 = (f32[3,8,128]{2,1,0:T(8,128)S(1)}, f32[3,8,128]{2,1,0:T(8,128)S(1)}, u32[]{:S(2)}, u32[]{:S(2)}) collective-permute-start(f32[3,8,128]{2,1,0:T(8,128)S(1)} %get-tuple-element.70), channel_id=1, source_target_pairs={{0,7},{1,2},{2,1},{3,4},{4,3},{5,6},{6,5},{7,0},{8,15},{9,10},{10,... | collective-permute-start | bytes 36872 | tf_op jit(solution)/shard_map/ppermute | solution.py:572
  53.0 3.7 %collective-permute-done.20 = f32[3,8,128]{2,1,0:T(8,128)S(1)} collective-permute-done((f32[3,8,128]{2,1,0:T(8,128)S(1)}, f32[3,8,128]{2,1,0:T(8,128)S(1)}, u32[]{:S(2)}, u32[]{:S(2)}) %collective-permute-start.20) | collective-permute-done | bytes 12320 | tf_op jit(solution)/shard_map/ppermute | solution.py:572
  56.7 1.7 %collective-permute-start.22 = (f32[9,8,128]{2,1,0:T(8,128)S(1)}, f32[9,8,128]{2,1,0:T(8,128)S(1)}, u32[]{:S(2)}, u32[]{:S(2)}) collective-permute-start(f32[9,8,128]{2,1,0:T(8,128)S(1)} %pad_maximum_fusion.3.own), channel_id=1, source_target_pairs={{0,16},{8,24},{16,0},{24,8},{32,48},{40,56},{48,32},{56,40},{1,17}... | collective-permute-start | bytes 110600 | tf_op jit(solution)/shard_map/ppermute | solution.py:635
  58.4 1.5 %collective-permute-start.23 = (f32[9,8,128]{2,1,0:T(8,128)S(1)}, f32[9,8,128]{2,1,0:T(8,128)S(1)}, u32[]{:S(2)}, u32[]{:S(2)}) collective-permute-start(f32[9,8,128]{2,1,0:T(8,128)S(1)} %pad_maximum_fusion.3.own), channel_id=1, source_target_pairs={{0,8},{8,0},{16,32},{24,40},{32,16},{40,24},{48,56},{56,48},{1,9},... | collective-permute-start | bytes 110600 | tf_op jit(solution)/shard_map/ppermute | solution.py:635
  59.9 1.8 %collective-permute-done.22.first = f32[9,8,128]{2,1,0:T(8,128)S(1)} collective-permute-done((f32[9,8,128]{2,1,0:T(8,128)S(1)}, f32[9,8,128]{2,1,0:T(8,128)S(1)}, u32[]{:S(2)}, u32[]{:S(2)}) %collective-permute-start.22) | collective-permute-done | bytes 36896 | tf_op jit(solution)/shard_map/ppermute | solution.py:635
  61.7 2.8 %collective-permute-done.23.second = f32[9,8,128]{2,1,0:T(8,128)S(1)} collective-permute-done((f32[9,8,128]{2,1,0:T(8,128)S(1)}, f32[9,8,128]{2,1,0:T(8,128)S(1)}, u32[]{:S(2)}, u32[]{:S(2)}) %collective-permute-start.23) | collective-permute-done | bytes 36896 | tf_op jit(solution)/shard_map/ppermute | solution.py:635
  64.5 4.4 %last_kernel.1 = f32[16,32,128]{2,1,0:T(8,128)} custom-call(s32[3]{0:T(128)S(1)} %pad_add_fusion.pos, f32[9,8,128]{2,1,0:T(8,128)S(1)} %pad_maximum_fusion.3.own, f32[9,8,128]{2,1,0:T(8,128)S(1)} %collective-permute-done.22.first, f32[9,8,128]{2,1,0:T(8,128)S(1)} %collective-permute-done.23.second, f32[24,40,256]{2,1,0:T(8,128)S(1)} %get-tuple-element.71.v0, ...), custom_call_target="tpu_custom_call" | custom-call | tf_op jit(solution)/shard_map/last_kernel/pallas_call | solution.py:542
  (38 shorter events, 0.4 us)
Async XLA Ops:
  0.0 1.8 %copy-start.1 = (f32[16,32,128]{2,1,0:T(8,128)S(1)}, f32[16,32,128]{2,1,0:T(8,128)}, u32[]{:S(2)}) copy-start(f32[16,32,128]{2,1,0:T(8,128)} %m.5) | copy-start | bytes 786436
  1.8 3.3 %copy-start = (f32[16,32,128]{2,1,0:T(8,128)S(1)}, f32[16,32,128]{2,1,0:T(8,128)}, u32[]{:S(2)}) copy-start(f32[16,32,128]{2,1,0:T(8,128)} %k.5) | copy-start | bytes 786436
  1.8 8.3 %collective-permute-start = (f32[10,32,128]{2,1,0:T(8,128)S(1)}, f32[10,32,128]{2,1,0:T(8,128)S(1)}, u32[]{:S(2)}, u32[]{:S(2)}) collective-permute-start(f32[10,32,128]{2,1,0:T(8,128)S(1)} %get-tuple-element.98), channel_id=1, source_target_pairs={{0,192},{64,128},{128,64},{192,0},{1,193},{65,129},{129,65},{193,1... | collective-permute-start | bytes 491528 | tf_op jit(solution)/shard_map/ppermute | solution.py:572
  4.9 7.1 %collective-permute-start.1 = (f32[10,32,128]{2,1,0:T(8,128)S(1)}, f32[10,32,128]{2,1,0:T(8,128)S(1)}, u32[]{:S(2)}, u32[]{:S(2)}) collective-permute-start(f32[10,32,128]{2,1,0:T(8,128)S(1)} %get-tuple-element.97), channel_id=1, source_target_pairs={{0,64},{64,0},{128,192},{192,128},{1,65},{65,1},{129,193},{193,129... | collective-permute-start | bytes 491528 | tf_op jit(solution)/shard_map/ppermute | solution.py:555
  5.3 16.8 %collective-permute-start.13 = (f32[8,16,128]{2,1,0:T(8,128)S(1)}, f32[8,16,128]{2,1,0:T(8,128)S(1)}, u32[]{:S(2)}, u32[]{:S(2)}) collective-permute-start(f32[8,16,128]{2,1,0:T(8,128)S(1)} %coarse_kernel.1), channel_id=1, source_target_pairs={{0,64},{64,0},{128,192},{192,128},{1,65},{65,1},{129,193},{193,129... | collective-permute-start | bytes 196616 | tf_op jit(solution)/shard_map/ppermute | solution.py:555
  7.3 14.8 %collective-permute-start.14 = (f32[8,16,128]{2,1,0:T(8,128)S(1)}, f32[8,16,128]{2,1,0:T(8,128)S(1)}, u32[]{:S(2)}, u32[]{:S(2)}) collective-permute-start(f32[8,16,128]{2,1,0:T(8,128)S(1)} %coarse_kernel.1), channel_id=1, source_target_pairs={{0,128},{64,192},{128,0},{192,64},{1,129},{65,193},{129,1},{193,65... | collective-permute-start | bytes 196616 | tf_op jit(solution)/shard_map/ppermute | solution.py:555
  7.9 14.2 %collective-permute-start.15 = (f32[8,16,128]{2,1,0:T(8,128)S(1)}, f32[8,16,128]{2,1,0:T(8,128)S(1)}, u32[]{:S(2)}, u32[]{:S(2)}) collective-permute-start(f32[8,16,128]{2,1,0:T(8,128)S(1)} %coarse_kernel.1), channel_id=1, source_target_pairs={{0,192},{64,128},{128,64},{192,0},{1,193},{65,129},{129,65},{193,1... | collective-permute-start | bytes 196616 | tf_op jit(solution)/shard_map/ppermute | solution.py:555
  10.1 1.9 %copy-start.2 = (f32[16,32,128]{2,1,0:T(8,128)S(1)}, f32[16,32,128]{2,1,0:T(8,128)}, u32[]{:S(2)}) copy-start(f32[16,32,128]{2,1,0:T(8,128)} %f.3) | copy-start | bytes 786436
  12.1 5.2 %collective-permute-start.2 = (f32[184,128]{1,0:T(8,128)S(1)}, f32[184,128]{1,0:T(8,128)S(1)}, u32[]{:S(2)}, u32[]{:S(2)}) collective-permute-start(f32[184,128]{1,0:T(8,128)S(1)} %get-tuple-element.114), channel_id=1, source_target_pairs={{0,56},{8,16},{16,8},{24,32},{32,24},{40,48},{48,40},{56,0},{1,57}... | collective-permute-start | bytes 282632 | tf_op jit(solution)/shard_map/ppermute | solution.py:572
  12.3 7.5 %collective-permute-start.3 = (f32[184,128]{1,0:T(8,128)S(1)}, f32[184,128]{1,0:T(8,128)S(1)}, u32[]{:S(2)}, u32[]{:S(2)}) collective-permute-start(f32[184,128]{1,0:T(8,128)S(1)} %get-tuple-element.113), channel_id=1, source_target_pairs={{0,8},{8,0},{16,24},{24,16},{32,40},{40,32},{48,56},{56,48},{1,9},... | collective-permute-start | bytes 282632 | tf_op jit(solution)/shard_map/ppermute | solution.py:555
  20.4 5.1 %collective-permute-start.4 = (f32[3,40,128]{2,1,0:T(8,128)S(1)}, f32[3,40,128]{2,1,0:T(8,128)S(1)}, u32[]{:S(2)}, u32[]{:S(2)}) collective-permute-start(f32[3,40,128]{2,1,0:T(8,128)S(1)} %get-tuple-element.118), channel_id=1, source_target_pairs={{0,7},{1,2},{2,1},{3,4},{4,3},{5,6},{6,5},{7,0},{8,15},{9,10},{10,... | collective-permute-start | bytes 184328 | tf_op jit(solution)/shard_map/ppermute | solution.py:572
  20.5 5.0 %collective-permute-start.5 = (f32[3,40,128]{2,1,0:T(8,128)S(1)}, f32[3,40,128]{2,1,0:T(8,128)S(1)}, u32[]{:S(2)}, u32[]{:S(2)}) collective-permute-start(f32[3,40,128]{2,1,0:T(8,128)S(1)} %get-tuple-element.117), channel_id=1, source_target_pairs={{0,1},{1,0},{2,3},{3,2},{4,5},{5,4},{6,7},{7,6},{8,9},{9,8},{10,11... | collective-permute-start | bytes 184328 | tf_op jit(solution)/shard_map/ppermute | solution.py:555
  22.1 11.7 %collective-permute-start.16 = (f32[32,16,128]{2,1,0:T(8,128)S(1)}, f32[32,16,128]{2,1,0:T(8,128)S(1)}, u32[]{:S(2)}, u32[]{:S(2)}) collective-permute-start(f32[32,16,128]{2,1,0:T(8,128)S(1)} %pad_maximum_fusion.own), channel_id=1, source_target_pairs={{0,56},{8,16},{16,8},{24,32},{32,24},{40,48},{48,40},{56,0},{1,57}... | collective-permute-start | bytes 786440 | tf_op jit(solution)/shard_map/ppermute | solution.py:572
  23.2 10.5 %collective-permute-start.17 = (f32[32,16,128]{2,1,0:T(8,128)S(1)}, f32[32,16,128]{2,1,0:T(8,128)S(1)}, u32[]{:S(2)}, u32[]{:S(2)}) collective-permute-start(f32[32,16,128]{2,1,0:T(8,128)S(1)} %pad_maximum_fusion.own), channel_id=1, source_target_pairs={{0,8},{8,0},{16,24},{24,16},{32,40},{40,32},{48,56},{56,48},{1,9},... | collective-permute-start | bytes 786440 | tf_op jit(solution)/shard_map/ppermute | solution.py:555
  29.0 5.2 %collective-permute-start.6 = (f32[4,16,128]{2,1,0:T(8,128)S(1)}, f32[4,16,128]{2,1,0:T(8,128)S(1)}, u32[]{:S(2)}, u32[]{:S(2)}) collective-permute-start(f32[4,16,128]{2,1,0:T(8,128)S(1)} %get-tuple-element.54), channel_id=1, source_target_pairs={{0,64},{64,0},{128,192},{192,128},{1,65},{65,1},{129,193},{193,129... | collective-permute-start | bytes 98312 | tf_op jit(solution)/shard_map/ppermute | solution.py:555
  29.2 5.4 %collective-permute-start.7 = (f32[4,16,128]{2,1,0:T(8,128)S(1)}, f32[4,16,128]{2,1,0:T(8,128)S(1)}, u32[]{:S(2)}, u32[]{:S(2)}) collective-permute-start(f32[4,16,128]{2,1,0:T(8,128)S(1)} %get-tuple-element.54), channel_id=1, source_target_pairs={{0,128},{64,192},{128,0},{192,64},{1,129},{65,193},{129,1},{193,65... | collective-permute-start | bytes 98312 | tf_op jit(solution)/shard_map/ppermute | solution.py:555
  30.8 5.1 %collective-permute-start.8 = (f32[4,16,128]{2,1,0:T(8,128)S(1)}, f32[4,16,128]{2,1,0:T(8,128)S(1)}, u32[]{:S(2)}, u32[]{:S(2)}) collective-permute-start(f32[4,16,128]{2,1,0:T(8,128)S(1)} %get-tuple-element.54), channel_id=1, source_target_pairs={{0,192},{64,128},{128,64},{192,0},{1,193},{65,129},{129,65},{193,1... | collective-permute-start | bytes 98312 | tf_op jit(solution)/shard_map/ppermute | solution.py:555
  35.9 5.0 %collective-permute-start.10 = (f32[16,16,128]{2,1,0:T(8,128)S(1)}, f32[16,16,128]{2,1,0:T(8,128)S(1)}, u32[]{:S(2)}, u32[]{:S(2)}) collective-permute-start(f32[16,16,128]{2,1,0:T(8,128)S(1)} %constant_dynamic-update-slice_fusion.own), channel_id=1, source_target_pairs={{0,8},{8,0},{16,24},{24,16},{32,40},{40,32},{48,56},{56,48},{1,9},... | collective-permute-start | bytes 393224 | tf_op jit(solution)/shard_map/ppermute | solution.py:555
  37.8 5.0 %collective-permute-start.9 = (f32[16,16,128]{2,1,0:T(8,128)S(1)}, f32[16,16,128]{2,1,0:T(8,128)S(1)}, u32[]{:S(2)}, u32[]{:S(2)}) collective-permute-start(f32[16,16,128]{2,1,0:T(8,128)S(1)} %constant_dynamic-update-slice_fusion.own), channel_id=1, source_target_pairs={{0,56},{8,16},{16,8},{24,32},{32,24},{40,48},{48,40},{56,0},{1,57}... | collective-permute-start | bytes 393224 | tf_op jit(solution)/shard_map/ppermute | solution.py:572
  38.9 6.6 %collective-permute-start.18 = (f32[8,48,128]{2,1,0:T(8,128)S(1)}, f32[8,48,128]{2,1,0:T(8,128)S(1)}, u32[]{:S(2)}, u32[]{:S(2)}) collective-permute-start(f32[8,48,128]{2,1,0:T(8,128)S(1)} %get-tuple-element.94), channel_id=1, source_target_pairs={{0,7},{1,2},{2,1},{3,4},{4,3},{5,6},{6,5},{7,0},{8,15},{9,10},{10,... | collective-permute-start | bytes 589832 | tf_op jit(solution)/shard_map/ppermute | solution.py:572
  39.2 6.3 %collective-permute-start.19 = (f32[8,48,128]{2,1,0:T(8,128)S(1)}, f32[8,48,128]{2,1,0:T(8,128)S(1)}, u32[]{:S(2)}, u32[]{:S(2)}) collective-permute-start(f32[8,48,128]{2,1,0:T(8,128)S(1)} %get-tuple-element.93), channel_id=1, source_target_pairs={{0,1},{1,0},{2,3},{3,2},{4,5},{5,4},{6,7},{7,6},{8,9},{9,8},{10,11... | collective-permute-start | bytes 589832 | tf_op jit(solution)/shard_map/ppermute | solution.py:555
  43.1 5.8 %collective-permute-start.11 = (f32[4,48,128]{2,1,0:T(8,128)S(1)}, f32[4,48,128]{2,1,0:T(8,128)S(1)}, u32[]{:S(2)}, u32[]{:S(2)}) collective-permute-start(f32[4,48,128]{2,1,0:T(8,128)S(1)} %get-tuple-element.110), channel_id=1, source_target_pairs={{0,7},{1,2},{2,1},{3,4},{4,3},{5,6},{6,5},{7,0},{8,15},{9,10},{10,... | collective-permute-start | bytes 294920 | tf_op jit(solution)/shard_map/ppermute | solution.py:572
  43.2 5.7 %collective-permute-start.12 = (f32[4,48,128]{2,1,0:T(8,128)S(1)}, f32[4,48,128]{2,1,0:T(8,128)S(1)}, u32[]{:S(2)}, u32[]{:S(2)}) collective-permute-start(f32[4,48,128]{2,1,0:T(8,128)S(1)} %get-tuple-element.109), channel_id=1, source_target_pairs={{0,1},{1,0},{2,3},{3,2},{4,5},{5,4},{6,7},{7,6},{8,9},{9,8},{10,11... | collective-permute-start | bytes 294920 | tf_op jit(solution)/shard_map/ppermute | solution.py:555
  52.3 4.4 %collective-permute-start.20 = (f32[3,8,128]{2,1,0:T(8,128)S(1)}, f32[3,8,128]{2,1,0:T(8,128)S(1)}, u32[]{:S(2)}, u32[]{:S(2)}) collective-permute-start(f32[3,8,128]{2,1,0:T(8,128)S(1)} %get-tuple-element.70), channel_id=1, source_target_pairs={{0,7},{1,2},{2,1},{3,4},{4,3},{5,6},{6,5},{7,0},{8,15},{9,10},{10,... | collective-permute-start | bytes 36872 | tf_op jit(solution)/shard_map/ppermute | solution.py:572
  53.0 3.7 %collective-permute-start.21 = (f32[3,8,128]{2,1,0:T(8,128)S(1)}, f32[3,8,128]{2,1,0:T(8,128)S(1)}, u32[]{:S(2)}, u32[]{:S(2)}) collective-permute-start(f32[3,8,128]{2,1,0:T(8,128)S(1)} %get-tuple-element.70), channel_id=1, source_target_pairs={{0,1},{1,0},{2,3},{3,2},{4,5},{5,4},{6,7},{7,6},{8,9},{9,8},{10,11... | collective-permute-start | bytes 36872 | tf_op jit(solution)/shard_map/ppermute | solution.py:555
  56.7 5.0 %collective-permute-start.22 = (f32[9,8,128]{2,1,0:T(8,128)S(1)}, f32[9,8,128]{2,1,0:T(8,128)S(1)}, u32[]{:S(2)}, u32[]{:S(2)}) collective-permute-start(f32[9,8,128]{2,1,0:T(8,128)S(1)} %pad_maximum_fusion.3.own), channel_id=1, source_target_pairs={{0,16},{8,24},{16,0},{24,8},{32,48},{40,56},{48,32},{56,40},{1,17}... | collective-permute-start | bytes 110600 | tf_op jit(solution)/shard_map/ppermute | solution.py:635
  58.4 6.1 %collective-permute-start.23 = (f32[9,8,128]{2,1,0:T(8,128)S(1)}, f32[9,8,128]{2,1,0:T(8,128)S(1)}, u32[]{:S(2)}, u32[]{:S(2)}) collective-permute-start(f32[9,8,128]{2,1,0:T(8,128)S(1)} %pad_maximum_fusion.3.own), channel_id=1, source_target_pairs={{0,8},{8,0},{16,32},{24,40},{32,16},{40,24},{48,56},{56,48},{1,9},... | collective-permute-start | bytes 110600 | tf_op jit(solution)/shard_map/ppermute | solution.py:635

commit v7 on v6

--- a/solution.py
+++ b/solution.py
@@ -514,7 +514,7 @@
             half[pl.ds(36, 2, stride=2), :] = ahead
             half[pl.ds(37, 2, stride=2), :] = ahead
             for p in (2 * x + 2, 2 * x + 3):
-                a0[p, :, lanes] = v0[p, :, lanes] + half[...]
+                a0[p, :, lanes] = v0[p, :, lanes] + half[0:40]
     sweep(3, 21, 9, k0, w0, g0, cy0, cz0, a0, b0)
 
     def values(p):
@@ -636,8 +636,8 @@
     return call(
         last_kernel,
         [(16, 32, 128)],
-        [THREE] * 8 + [(240, 128), (192, 128)] + [NEAR2] * 2 + [NEAR1] * 2
-        + [(240, 256), (40, 128), (40, 128)] + [FULL] * 2,
+        [THREE] * 8 + [(240, 128), (224, 128)] + [NEAR2] * 2 + [NEAR1] * 2
+        + [(240, 256), (64, 128), (64, 128)] + [FULL] * 2,
         own, first, second, *level0, *vary, *near,
         pos=pos,
     )[0]

time: 69 us -> 69 us (level)
  no operation moved by 1% of the time
where the time goes in v7:
time: 69 us; the launch traced here: 68.8 us
  starting transfers between devices  30.9 us (45%)
  waiting for transfers between devices  19.5 us (28%)
  Pallas kernels  16 us (23%)
  local copies, waits for them, and re-layouts  1.79 us (3%)
    ppermute x14, starting transfers between devices, swap(): return lax.ppermute(x, axis, [(i, i ^ bits) for i in range(size)])  21.1 us
    pallas_call x9, Pallas kernels, call(): pl.pallas_call(kernel, out_shape=[jax.ShapeDtypeStruct(s, F32) for s in o...  16 us
    ppermute x8, waiting for transfers between devices, both_sides(): there = lax.ppermute(jnp.where(even, down, up), axis, far)  7.48 us
    ppermute x14, waiting for transfers between devices, swap(): return lax.ppermute(x, axis, [(i, i ^ bits) for i in range(size)])  7.43 us
    ppermute x8, starting transfers between devices, both_sides(): there = lax.ppermute(jnp.where(even, down, up), axis, far)  6.65 us
    ppermute x2, waiting for transfers between devices, per_device(): lax.ppermute(own, 'gy', list(enumerate(t)))  4.54 us
    ppermute x2, starting transfers between devices, per_device(): lax.ppermute(own, 'gy', list(enumerate(t)))  3.2 us
    slice x3, local copies, waits for them, and re-layouts, per_device(): down = jnp.concatenate([f[:3], m[:3], k[:4]])  1.76 us
  transfers between devices with their start and end apart: 24, of which 10 were waited for; matrix products, arithmetic and copies ran while one was open for 0% of the time, Pallas kernels for 12%

profile of v7, /device:TPU:64, one launch (start us, length us, event | category | flops | bytes accessed | tf_op | source)
XLA Modules:
  0.0 68.8 jit_solution(16618053766895451035)
XLA Ops:
  0.0 0.9 %fusion.4 = (f32[4,32,128]{2,1,0:T(8,128)S(1)}, f32[4,32,128]{2,1,0:T(8,128)S(1)}) fusion(f32[16,32,128]{2,1,0:T(8,128)} %k.5), kind=kLoop, calls=%fused_computation.37 | loop fusion | bytes 262144 | tf_op jit(solution)/shard_map/slice | solution.py:591
  0.9 0.8 %fusion.2 = (f32[3,32,128]{2,1,0:T(8,128)S(1)}, f32[3,32,128]{2,1,0:T(8,128)S(1)}) fusion(f32[16,32,128]{2,1,0:T(8,128)} %f.3), kind=kLoop, calls=%fused_computation.35 | loop fusion | bytes 196608 | tf_op jit(solution)/shard_map/slice | solution.py:591
  1.8 0.0 copy-start
  1.8 3.1 %collective-permute-start = (f32[10,32,128]{2,1,0:T(8,128)S(1)}, f32[10,32,128]{2,1,0:T(8,128)S(1)}, u32[]{:S(2)}, u32[]{:S(2)}) collective-permute-start(f32[10,32,128]{2,1,0:T(8,128)S(1)} %get-tuple-element.98), channel_id=1, source_target_pairs={{0,192},{64,128},{128,64},{192,0},{1,193},{65,129},{129,65},{193,1... | collective-permute-start | bytes 491528 | tf_op jit(solution)/shard_map/ppermute | solution.py:572
  4.9 0.1 collective-permute-start.1
  5.1 0.2 coarse_kernel.1
  5.3 2.0 %collective-permute-start.13 = (f32[8,16,128]{2,1,0:T(8,128)S(1)}, f32[8,16,128]{2,1,0:T(8,128)S(1)}, u32[]{:S(2)}, u32[]{:S(2)}) collective-permute-start(f32[8,16,128]{2,1,0:T(8,128)S(1)} %coarse_kernel.1), channel_id=1, source_target_pairs={{0,64},{64,0},{128,192},{192,128},{1,65},{65,1},{129,193},{193,129... | collective-permute-start | bytes 196616 | tf_op jit(solution)/shard_map/ppermute | solution.py:555
  7.3 0.6 collective-permute-start.14
  7.9 2.2 %collective-permute-start.15 = (f32[8,16,128]{2,1,0:T(8,128)S(1)}, f32[8,16,128]{2,1,0:T(8,128)S(1)}, u32[]{:S(2)}, u32[]{:S(2)}) collective-permute-start(f32[8,16,128]{2,1,0:T(8,128)S(1)} %coarse_kernel.1), channel_id=1, source_target_pairs={{0,192},{64,128},{128,64},{192,0},{1,193},{65,129},{129,65},{193,1... | collective-permute-start | bytes 196616 | tf_op jit(solution)/shard_map/ppermute | solution.py:555
  10.1 0.0 collective-permute-done
  10.1 1.9 %collective-permute-done.1 = f32[10,32,128]{2,1,0:T(8,128)S(1)} collective-permute-done((f32[10,32,128]{2,1,0:T(8,128)S(1)}, f32[10,32,128]{2,1,0:T(8,128)S(1)}, u32[]{:S(2)}, u32[]{:S(2)}) %collective-permute-start.1) | collective-permute-done | bytes 163872 | tf_op jit(solution)/shard_map/ppermute | solution.py:555
  12.1 0.2 collective-permute-start.2
  12.3 4.9 %collective-permute-start.3 = (f32[184,128]{1,0:T(8,128)S(1)}, f32[184,128]{1,0:T(8,128)S(1)}, u32[]{:S(2)}, u32[]{:S(2)}) collective-permute-start(f32[184,128]{1,0:T(8,128)S(1)} %get-tuple-element.113), channel_id=1, source_target_pairs={{0,8},{8,0},{16,24},{24,16},{32,40},{40,32},{48,56},{56,48},{1,9},... | collective-permute-start | bytes 282632 | tf_op jit(solution)/shard_map/ppermute | solution.py:555
  17.2 0.1 pad_add_fusion.pos
  17.3 2.5 %collective-permute-done.3 = f32[184,128]{1,0:T(8,128)S(1)} collective-permute-done((f32[184,128]{1,0:T(8,128)S(1)}, f32[184,128]{1,0:T(8,128)S(1)}, u32[]{:S(2)}, u32[]{:S(2)}) %collective-permute-start.3) | collective-permute-done | bytes 94240 | tf_op jit(solution)/shard_map/ppermute | solution.py:555
  19.8 0.5 pack_z_kernel.1
  20.4 0.1 collective-permute-start.4
  20.5 1.6 %collective-permute-start.5 = (f32[3,40,128]{2,1,0:T(8,128)S(1)}, f32[3,40,128]{2,1,0:T(8,128)S(1)}, u32[]{:S(2)}, u32[]{:S(2)}) collective-permute-start(f32[3,40,128]{2,1,0:T(8,128)S(1)} %get-tuple-element.117), channel_id=1, source_target_pairs={{0,1},{1,0},{2,3},{3,2},{4,5},{5,4},{6,7},{7,6},{8,9},{9,8},{10,11... | collective-permute-start | bytes 184328 | tf_op jit(solution)/shard_map/ppermute | solution.py:555
  22.1 0.0 collective-permute-done.13
  22.1 0.0 collective-permute-done.14
  22.1 1.1 %collective-permute-start.16 = (f32[32,16,128]{2,1,0:T(8,128)S(1)}, f32[32,16,128]{2,1,0:T(8,128)S(1)}, u32[]{:S(2)}, u32[]{:S(2)}) collective-permute-start(f32[32,16,128]{2,1,0:T(8,128)S(1)} %pad_maximum_fusion.own), channel_id=1, source_target_pairs={{0,56},{8,16},{16,8},{24,32},{32,24},{40,48},{48,40},{56,0},{1,57}... | collective-permute-start | bytes 786440 | tf_op jit(solution)/shard_map/ppermute | solution.py:572
  23.2 2.2 %collective-permute-start.17 = (f32[32,16,128]{2,1,0:T(8,128)S(1)}, f32[32,16,128]{2,1,0:T(8,128)S(1)}, u32[]{:S(2)}, u32[]{:S(2)}) collective-permute-start(f32[32,16,128]{2,1,0:T(8,128)S(1)} %pad_maximum_fusion.own), channel_id=1, source_target_pairs={{0,8},{8,0},{16,24},{24,16},{32,40},{40,32},{48,56},{56,48},{1,9},... | collective-permute-start | bytes 786440 | tf_op jit(solution)/shard_map/ppermute | solution.py:555
  25.5 3.5 %fine_kernel.1 = (f32[4,16,128]{2,1,0:T(8,128)S(1)}, f32[24,40,256]{2,1,0:T(8,128)S(1)}, f32[24,40,256]{2,1,0:T(8,128)S(1)}, f32[24,40,256]{2,1,0:T(8,128)S(1)},...) custom-call(s32[3]{0:T(128)S(1)} %pad_add_fusion.pos, ...), custom_call_target="tpu_custom_call" | custom-call | tf_op jit(solution)/shard_map/fine_kernel/pallas_call | solution.py:542
  29.0 0.2 collective-permute-start.6
  29.2 1.5 %collective-permute-start.7 = (f32[4,16,128]{2,1,0:T(8,128)S(1)}, f32[4,16,128]{2,1,0:T(8,128)S(1)}, u32[]{:S(2)}, u32[]{:S(2)}) collective-permute-start(f32[4,16,128]{2,1,0:T(8,128)S(1)} %get-tuple-element.54), channel_id=1, source_target_pairs={{0,128},{64,192},{128,0},{192,64},{1,129},{65,193},{129,1},{193,65... | collective-permute-start | bytes 98312 | tf_op jit(solution)/shard_map/ppermute | solution.py:555
  30.8 3.0 %collective-permute-start.8 = (f32[4,16,128]{2,1,0:T(8,128)S(1)}, f32[4,16,128]{2,1,0:T(8,128)S(1)}, u32[]{:S(2)}, u32[]{:S(2)}) collective-permute-start(f32[4,16,128]{2,1,0:T(8,128)S(1)} %get-tuple-element.54), channel_id=1, source_target_pairs={{0,192},{64,128},{128,64},{192,0},{1,193},{65,129},{129,65},{193,1... | collective-permute-start | bytes 98312 | tf_op jit(solution)/shard_map/ppermute | solution.py:555
  33.8 0.4 pack_z1_kernel.3
  34.2 0.4 collective-permute-done.7
  34.7 1.2 %collective-permute-done.8 = f32[4,16,128]{2,1,0:T(8,128)S(1)} collective-permute-done((f32[4,16,128]{2,1,0:T(8,128)S(1)}, f32[4,16,128]{2,1,0:T(8,128)S(1)}, u32[]{:S(2)}, u32[]{:S(2)}) %collective-permute-start.8) | collective-permute-done | bytes 32800 | tf_op jit(solution)/shard_map/ppermute | solution.py:555
  35.9 1.9 %collective-permute-start.10 = (f32[16,16,128]{2,1,0:T(8,128)S(1)}, f32[16,16,128]{2,1,0:T(8,128)S(1)}, u32[]{:S(2)}, u32[]{:S(2)}) collective-permute-start(f32[16,16,128]{2,1,0:T(8,128)S(1)} %constant_dynamic-update-slice_fusion.own), channel_id=1, source_target_pairs={{0,8},{8,0},{16,24},{24,16},{32,40},{40,32},{48,56},{56,48},{1,9},... | collective-permute-start | bytes 393224 | tf_op jit(solution)/shard_map/ppermute | solution.py:555
  37.8 1.0 %collective-permute-start.9 = (f32[16,16,128]{2,1,0:T(8,128)S(1)}, f32[16,16,128]{2,1,0:T(8,128)S(1)}, u32[]{:S(2)}, u32[]{:S(2)}) collective-permute-start(f32[16,16,128]{2,1,0:T(8,128)S(1)} %constant_dynamic-update-slice_fusion.own), channel_id=1, source_target_pairs={{0,56},{8,16},{16,8},{24,32},{32,24},{40,48},{48,40},{56,0},{1,57}... | collective-permute-start | bytes 393224 | tf_op jit(solution)/shard_map/ppermute | solution.py:572
  38.9 0.3 collective-permute-start.18
  39.2 0.4 collective-permute-start.19
  39.5 1.3 %collective-permute-done.10 = f32[16,16,128]{2,1,0:T(8,128)S(1)} collective-permute-done((f32[16,16,128]{2,1,0:T(8,128)S(1)}, f32[16,16,128]{2,1,0:T(8,128)S(1)}, u32[]{:S(2)}, u32[]{:S(2)}) %collective-permute-start.10) | collective-permute-done | bytes 131104 | tf_op jit(solution)/shard_map/ppermute | solution.py:555
  40.9 1.9 %collective-permute-done.9 = f32[16,16,128]{2,1,0:T(8,128)S(1)} collective-permute-done((f32[16,16,128]{2,1,0:T(8,128)S(1)}, f32[16,16,128]{2,1,0:T(8,128)S(1)}, u32[]{:S(2)}, u32[]{:S(2)}) %collective-permute-start.9) | collective-permute-done | bytes 131104 | tf_op jit(solution)/shard_map/ppermute | solution.py:572
  42.8 0.2 pack_z1_kernel.2
  43.1 0.1 collective-permute-start.11
  43.2 0.4 collective-permute-start.12
  43.6 1.9 %collective-permute-done.18 = f32[8,48,128]{2,1,0:T(8,128)S(1)} collective-permute-done((f32[8,48,128]{2,1,0:T(8,128)S(1)}, f32[8,48,128]{2,1,0:T(8,128)S(1)}, u32[]{:S(2)}, u32[]{:S(2)}) %collective-permute-start.18) | collective-permute-done | bytes 196640 | tf_op jit(solution)/shard_map/ppermute | solution.py:572
  45.5 3.4 %static_kernel.1 = (f32[2,8,128]{2,1,0:T(8,128)S(1)}, f32[40,48,128]{2,1,0:T(8,128)S(1)}, f32[40,48,128]{2,1,0:T(8,128)S(1)}, f32[40,48,128]{2,1,0:T(8,128)S(1)}...) custom-call(s32[3]{0:T(128)S(1)} %pad_add_fusion.pos, ...), custom_call_target="tpu_custom_call" | custom-call | tf_op jit(solution)/shard_map/static_kernel/pallas_call | solution.py:542
  48.9 3.3 %middle_kernel.1 = (f32[3,8,128]{2,1,0:T(8,128)S(1)}, f32[16,24,128]{2,1,0:T(8,128)S(1)}, f32[16,24,128]{2,1,0:T(8,128)S(1)}, f32[12,16,128]{2,1,0:T(8,128)S(1)}, f32[12,16,128]{2,1,0:T(8,128)S(1)}) custom-call(s32[3]{0:T(128)S(1)} %pad_add_fusion.pos, f32[16,16,128]{2,1,0:T(8,128)S(1)} %constant_dynamic-update-slice_fusion.own, ...), custom_call_target="tpu_custom_call" | custom-call | tf_op jit(solution)/shard_map/middle_kernel/pallas_call | solution.py:542
  52.3 0.8 %collective-permute-start.20 = (f32[3,8,128]{2,1,0:T(8,128)S(1)}, f32[3,8,128]{2,1,0:T(8,128)S(1)}, u32[]{:S(2)}, u32[]{:S(2)}) collective-permute-start(f32[3,8,128]{2,1,0:T(8,128)S(1)} %get-tuple-element.70), channel_id=1, source_target_pairs={{0,7},{1,2},{2,1},{3,4},{4,3},{5,6},{6,5},{7,0},{8,15},{9,10},{10,... | collective-permute-start | bytes 36872 | tf_op jit(solution)/shard_map/ppermute | solution.py:572
  53.0 3.7 %collective-permute-done.20 = f32[3,8,128]{2,1,0:T(8,128)S(1)} collective-permute-done((f32[3,8,128]{2,1,0:T(8,128)S(1)}, f32[3,8,128]{2,1,0:T(8,128)S(1)}, u32[]{:S(2)}, u32[]{:S(2)}) %collective-permute-start.20) | collective-permute-done | bytes 12320 | tf_op jit(solution)/shard_map/ppermute | solution.py:572
  56.7 1.7 %collective-permute-start.22 = (f32[9,8,128]{2,1,0:T(8,128)S(1)}, f32[9,8,128]{2,1,0:T(8,128)S(1)}, u32[]{:S(2)}, u32[]{:S(2)}) collective-permute-start(f32[9,8,128]{2,1,0:T(8,128)S(1)} %pad_maximum_fusion.3.own), channel_id=1, source_target_pairs={{0,16},{8,24},{16,0},{24,8},{32,48},{40,56},{48,32},{56,40},{1,17}... | collective-permute-start | bytes 110600 | tf_op jit(solution)/shard_map/ppermute | solution.py:635
  58.4 1.5 %collective-permute-start.23 = (f32[9,8,128]{2,1,0:T(8,128)S(1)}, f32[9,8,128]{2,1,0:T(8,128)S(1)}, u32[]{:S(2)}, u32[]{:S(2)}) collective-permute-start(f32[9,8,128]{2,1,0:T(8,128)S(1)} %pad_maximum_fusion.3.own), channel_id=1, source_target_pairs={{0,8},{8,0},{16,32},{24,40},{32,16},{40,24},{48,56},{56,48},{1,9},... | collective-permute-start | bytes 110600 | tf_op jit(solution)/shard_map/ppermute | solution.py:635
  59.9 1.8 %collective-permute-done.22.first = f32[9,8,128]{2,1,0:T(8,128)S(1)} collective-permute-done((f32[9,8,128]{2,1,0:T(8,128)S(1)}, f32[9,8,128]{2,1,0:T(8,128)S(1)}, u32[]{:S(2)}, u32[]{:S(2)}) %collective-permute-start.22) | collective-permute-done | bytes 36896 | tf_op jit(solution)/shard_map/ppermute | solution.py:635
  61.7 2.8 %collective-permute-done.23.second = f32[9,8,128]{2,1,0:T(8,128)S(1)} collective-permute-done((f32[9,8,128]{2,1,0:T(8,128)S(1)}, f32[9,8,128]{2,1,0:T(8,128)S(1)}, u32[]{:S(2)}, u32[]{:S(2)}) %collective-permute-start.23) | collective-permute-done | bytes 36896 | tf_op jit(solution)/shard_map/ppermute | solution.py:635
  64.5 4.4 %last_kernel.1 = f32[16,32,128]{2,1,0:T(8,128)} custom-call(s32[3]{0:T(128)S(1)} %pad_add_fusion.pos, f32[9,8,128]{2,1,0:T(8,128)S(1)} %pad_maximum_fusion.3.own, f32[9,8,128]{2,1,0:T(8,128)S(1)} %collective-permute-done.22.first, f32[9,8,128]{2,1,0:T(8,128)S(1)} %collective-permute-done.23.second, f32[24,40,256]{2,1,0:T(8,128)S(1)} %get-tuple-element.71.v0, ...), custom_call_target="tpu_custom_call" | custom-call | tf_op jit(solution)/shard_map/last_kernel/pallas_call | solution.py:542
  (38 shorter events, 0.4 us)
Async XLA Ops:
  0.0 1.8 %copy-start.1 = (f32[16,32,128]{2,1,0:T(8,128)S(1)}, f32[16,32,128]{2,1,0:T(8,128)}, u32[]{:S(2)}) copy-start(f32[16,32,128]{2,1,0:T(8,128)} %m.5) | copy-start | bytes 786436
  1.8 3.3 %copy-start = (f32[16,32,128]{2,1,0:T(8,128)S(1)}, f32[16,32,128]{2,1,0:T(8,128)}, u32[]{:S(2)}) copy-start(f32[16,32,128]{2,1,0:T(8,128)} %k.5) | copy-start | bytes 786436
  1.8 8.3 %collective-permute-start = (f32[10,32,128]{2,1,0:T(8,128)S(1)}, f32[10,32,128]{2,1,0:T(8,128)S(1)}, u32[]{:S(2)}, u32[]{:S(2)}) collective-permute-start(f32[10,32,128]{2,1,0:T(8,128)S(1)} %get-tuple-element.98), channel_id=1, source_target_pairs={{0,192},{64,128},{128,64},{192,0},{1,193},{65,129},{129,65},{193,1... | collective-permute-start | bytes 491528 | tf_op jit(solution)/shard_map/ppermute | solution.py:572
  4.9 7.1 %collective-permute-start.1 = (f32[10,32,128]{2,1,0:T(8,128)S(1)}, f32[10,32,128]{2,1,0:T(8,128)S(1)}, u32[]{:S(2)}, u32[]{:S(2)}) collective-permute-start(f32[10,32,128]{2,1,0:T(8,128)S(1)} %get-tuple-element.97), channel_id=1, source_target_pairs={{0,64},{64,0},{128,192},{192,128},{1,65},{65,1},{129,193},{193,129... | collective-permute-start | bytes 491528 | tf_op jit(solution)/shard_map/ppermute | solution.py:555
  5.3 16.8 %collective-permute-start.13 = (f32[8,16,128]{2,1,0:T(8,128)S(1)}, f32[8,16,128]{2,1,0:T(8,128)S(1)}, u32[]{:S(2)}, u32[]{:S(2)}) collective-permute-start(f32[8,16,128]{2,1,0:T(8,128)S(1)} %coarse_kernel.1), channel_id=1, source_target_pairs={{0,64},{64,0},{128,192},{192,128},{1,65},{65,1},{129,193},{193,129... | collective-permute-start | bytes 196616 | tf_op jit(solution)/shard_map/ppermute | solution.py:555
  7.3 14.8 %collective-permute-start.14 = (f32[8,16,128]{2,1,0:T(8,128)S(1)}, f32[8,16,128]{2,1,0:T(8,128)S(1)}, u32[]{:S(2)}, u32[]{:S(2)}) collective-permute-start(f32[8,16,128]{2,1,0:T(8,128)S(1)} %coarse_kernel.1), channel_id=1, source_target_pairs={{0,128},{64,192},{128,0},{192,64},{1,129},{65,193},{129,1},{193,65... | collective-permute-start | bytes 196616 | tf_op jit(solution)/shard_map/ppermute | solution.py:555
  7.9 14.2 %collective-permute-start.15 = (f32[8,16,128]{2,1,0:T(8,128)S(1)}, f32[8,16,128]{2,1,0:T(8,128)S(1)}, u32[]{:S(2)}, u32[]{:S(2)}) collective-permute-start(f32[8,16,128]{2,1,0:T(8,128)S(1)} %coarse_kernel.1), channel_id=1, source_target_pairs={{0,192},{64,128},{128,64},{192,0},{1,193},{65,129},{129,65},{193,1... | collective-permute-start | bytes 196616 | tf_op jit(solution)/shard_map/ppermute | solution.py:555
  10.1 1.9 %copy-start.2 = (f32[16,32,128]{2,1,0:T(8,128)S(1)}, f32[16,32,128]{2,1,0:T(8,128)}, u32[]{:S(2)}) copy-start(f32[16,32,128]{2,1,0:T(8,128)} %f.3) | copy-start | bytes 786436
  12.1 5.2 %collective-permute-start.2 = (f32[184,128]{1,0:T(8,128)S(1)}, f32[184,128]{1,0:T(8,128)S(1)}, u32[]{:S(2)}, u32[]{:S(2)}) collective-permute-start(f32[184,128]{1,0:T(8,128)S(1)} %get-tuple-element.114), channel_id=1, source_target_pairs={{0,56},{8,16},{16,8},{24,32},{32,24},{40,48},{48,40},{56,0},{1,57}... | collective-permute-start | bytes 282632 | tf_op jit(solution)/shard_map/ppermute | solution.py:572
  12.3 7.5 %collective-permute-start.3 = (f32[184,128]{1,0:T(8,128)S(1)}, f32[184,128]{1,0:T(8,128)S(1)}, u32[]{:S(2)}, u32[]{:S(2)}) collective-permute-start(f32[184,128]{1,0:T(8,128)S(1)} %get-tuple-element.113), channel_id=1, source_target_pairs={{0,8},{8,0},{16,24},{24,16},{32,40},{40,32},{48,56},{56,48},{1,9},... | collective-permute-start | bytes 282632 | tf_op jit(solution)/shard_map/ppermute | solution.py:555
  20.4 5.1 %collective-permute-start.4 = (f32[3,40,128]{2,1,0:T(8,128)S(1)}, f32[3,40,128]{2,1,0:T(8,128)S(1)}, u32[]{:S(2)}, u32[]{:S(2)}) collective-permute-start(f32[3,40,128]{2,1,0:T(8,128)S(1)} %get-tuple-element.118), channel_id=1, source_target_pairs={{0,7},{1,2},{2,1},{3,4},{4,3},{5,6},{6,5},{7,0},{8,15},{9,10},{10,... | collective-permute-start | bytes 184328 | tf_op jit(solution)/shard_map/ppermute | solution.py:572
  20.5 5.0 %collective-permute-start.5 = (f32[3,40,128]{2,1,0:T(8,128)S(1)}, f32[3,40,128]{2,1,0:T(8,128)S(1)}, u32[]{:S(2)}, u32[]{:S(2)}) collective-permute-start(f32[3,40,128]{2,1,0:T(8,128)S(1)} %get-tuple-element.117), channel_id=1, source_target_pairs={{0,1},{1,0},{2,3},{3,2},{4,5},{5,4},{6,7},{7,6},{8,9},{9,8},{10,11... | collective-permute-start | bytes 184328 | tf_op jit(solution)/shard_map/ppermute | solution.py:555
  22.1 11.7 %collective-permute-start.16 = (f32[32,16,128]{2,1,0:T(8,128)S(1)}, f32[32,16,128]{2,1,0:T(8,128)S(1)}, u32[]{:S(2)}, u32[]{:S(2)}) collective-permute-start(f32[32,16,128]{2,1,0:T(8,128)S(1)} %pad_maximum_fusion.own), channel_id=1, source_target_pairs={{0,56},{8,16},{16,8},{24,32},{32,24},{40,48},{48,40},{56,0},{1,57}... | collective-permute-start | bytes 786440 | tf_op jit(solution)/shard_map/ppermute | solution.py:572
  23.2 10.5 %collective-permute-start.17 = (f32[32,16,128]{2,1,0:T(8,128)S(1)}, f32[32,16,128]{2,1,0:T(8,128)S(1)}, u32[]{:S(2)}, u32[]{:S(2)}) collective-permute-start(f32[32,16,128]{2,1,0:T(8,128)S(1)} %pad_maximum_fusion.own), channel_id=1, source_target_pairs={{0,8},{8,0},{16,24},{24,16},{32,40},{40,32},{48,56},{56,48},{1,9},... | collective-permute-start | bytes 786440 | tf_op jit(solution)/shard_map/ppermute | solution.py:555
  29.0 5.2 %collective-permute-start.6 = (f32[4,16,128]{2,1,0:T(8,128)S(1)}, f32[4,16,128]{2,1,0:T(8,128)S(1)}, u32[]{:S(2)}, u32[]{:S(2)}) collective-permute-start(f32[4,16,128]{2,1,0:T(8,128)S(1)} %get-tuple-element.54), channel_id=1, source_target_pairs={{0,64},{64,0},{128,192},{192,128},{1,65},{65,1},{129,193},{193,129... | collective-permute-start | bytes 98312 | tf_op jit(solution)/shard_map/ppermute | solution.py:555
  29.2 5.4 %collective-permute-start.7 = (f32[4,16,128]{2,1,0:T(8,128)S(1)}, f32[4,16,128]{2,1,0:T(8,128)S(1)}, u32[]{:S(2)}, u32[]{:S(2)}) collective-permute-start(f32[4,16,128]{2,1,0:T(8,128)S(1)} %get-tuple-element.54), channel_id=1, source_target_pairs={{0,128},{64,192},{128,0},{192,64},{1,129},{65,193},{129,1},{193,65... | collective-permute-start | bytes 98312 | tf_op jit(solution)/shard_map/ppermute | solution.py:555
  30.8 5.1 %collective-permute-start.8 = (f32[4,16,128]{2,1,0:T(8,128)S(1)}, f32[4,16,128]{2,1,0:T(8,128)S(1)}, u32[]{:S(2)}, u32[]{:S(2)}) collective-permute-start(f32[4,16,128]{2,1,0:T(8,128)S(1)} %get-tuple-element.54), channel_id=1, source_target_pairs={{0,192},{64,128},{128,64},{192,0},{1,193},{65,129},{129,65},{193,1... | collective-permute-start | bytes 98312 | tf_op jit(solution)/shard_map/ppermute | solution.py:555
  35.9 5.0 %collective-permute-start.10 = (f32[16,16,128]{2,1,0:T(8,128)S(1)}, f32[16,16,128]{2,1,0:T(8,128)S(1)}, u32[]{:S(2)}, u32[]{:S(2)}) collective-permute-start(f32[16,16,128]{2,1,0:T(8,128)S(1)} %constant_dynamic-update-slice_fusion.own), channel_id=1, source_target_pairs={{0,8},{8,0},{16,24},{24,16},{32,40},{40,32},{48,56},{56,48},{1,9},... | collective-permute-start | bytes 393224 | tf_op jit(solution)/shard_map/ppermute | solution.py:555
  37.8 5.0 %collective-permute-start.9 = (f32[16,16,128]{2,1,0:T(8,128)S(1)}, f32[16,16,128]{2,1,0:T(8,128)S(1)}, u32[]{:S(2)}, u32[]{:S(2)}) collective-permute-start(f32[16,16,128]{2,1,0:T(8,128)S(1)} %constant_dynamic-update-slice_fusion.own), channel_id=1, source_target_pairs={{0,56},{8,16},{16,8},{24,32},{32,24},{40,48},{48,40},{56,0},{1,57}... | collective-permute-start | bytes 393224 | tf_op jit(solution)/shard_map/ppermute | solution.py:572
  38.9 6.6 %collective-permute-start.18 = (f32[8,48,128]{2,1,0:T(8,128)S(1)}, f32[8,48,128]{2,1,0:T(8,128)S(1)}, u32[]{:S(2)}, u32[]{:S(2)}) collective-permute-start(f32[8,48,128]{2,1,0:T(8,128)S(1)} %get-tuple-element.94), channel_id=1, source_target_pairs={{0,7},{1,2},{2,1},{3,4},{4,3},{5,6},{6,5},{7,0},{8,15},{9,10},{10,... | collective-permute-start | bytes 589832 | tf_op jit(solution)/shard_map/ppermute | solution.py:572
  39.2 6.3 %collective-permute-start.19 = (f32[8,48,128]{2,1,0:T(8,128)S(1)}, f32[8,48,128]{2,1,0:T(8,128)S(1)}, u32[]{:S(2)}, u32[]{:S(2)}) collective-permute-start(f32[8,48,128]{2,1,0:T(8,128)S(1)} %get-tuple-element.93), channel_id=1, source_target_pairs={{0,1},{1,0},{2,3},{3,2},{4,5},{5,4},{6,7},{7,6},{8,9},{9,8},{10,11... | collective-permute-start | bytes 589832 | tf_op jit(solution)/shard_map/ppermute | solution.py:555
  43.1 5.8 %collective-permute-start.11 = (f32[4,48,128]{2,1,0:T(8,128)S(1)}, f32[4,48,128]{2,1,0:T(8,128)S(1)}, u32[]{:S(2)}, u32[]{:S(2)}) collective-permute-start(f32[4,48,128]{2,1,0:T(8,128)S(1)} %get-tuple-element.110), channel_id=1, source_target_pairs={{0,7},{1,2},{2,1},{3,4},{4,3},{5,6},{6,5},{7,0},{8,15},{9,10},{10,... | collective-permute-start | bytes 294920 | tf_op jit(solution)/shard_map/ppermute | solution.py:572
  43.2 5.7 %collective-permute-start.12 = (f32[4,48,128]{2,1,0:T(8,128)S(1)}, f32[4,48,128]{2,1,0:T(8,128)S(1)}, u32[]{:S(2)}, u32[]{:S(2)}) collective-permute-start(f32[4,48,128]{2,1,0:T(8,128)S(1)} %get-tuple-element.109), channel_id=1, source_target_pairs={{0,1},{1,0},{2,3},{3,2},{4,5},{5,4},{6,7},{7,6},{8,9},{9,8},{10,11... | collective-permute-start | bytes 294920 | tf_op jit(solution)/shard_map/ppermute | solution.py:555
  52.3 4.4 %collective-permute-start.20 = (f32[3,8,128]{2,1,0:T(8,128)S(1)}, f32[3,8,128]{2,1,0:T(8,128)S(1)}, u32[]{:S(2)}, u32[]{:S(2)}) collective-permute-start(f32[3,8,128]{2,1,0:T(8,128)S(1)} %get-tuple-element.70), channel_id=1, source_target_pairs={{0,7},{1,2},{2,1},{3,4},{4,3},{5,6},{6,5},{7,0},{8,15},{9,10},{10,... | collective-permute-start | bytes 36872 | tf_op jit(solution)/shard_map/ppermute | solution.py:572
  53.0 3.7 %collective-permute-start.21 = (f32[3,8,128]{2,1,0:T(8,128)S(1)}, f32[3,8,128]{2,1,0:T(8,128)S(1)}, u32[]{:S(2)}, u32[]{:S(2)}) collective-permute-start(f32[3,8,128]{2,1,0:T(8,128)S(1)} %get-tuple-element.70), channel_id=1, source_target_pairs={{0,1},{1,0},{2,3},{3,2},{4,5},{5,4},{6,7},{7,6},{8,9},{9,8},{10,11... | collective-permute-start | bytes 36872 | tf_op jit(solution)/shard_map/ppermute | solution.py:555
  56.7 5.0 %collective-permute-start.22 = (f32[9,8,128]{2,1,0:T(8,128)S(1)}, f32[9,8,128]{2,1,0:T(8,128)S(1)}, u32[]{:S(2)}, u32[]{:S(2)}) collective-permute-start(f32[9,8,128]{2,1,0:T(8,128)S(1)} %pad_maximum_fusion.3.own), channel_id=1, source_target_pairs={{0,16},{8,24},{16,0},{24,8},{32,48},{40,56},{48,32},{56,40},{1,17}... | collective-permute-start | bytes 110600 | tf_op jit(solution)/shard_map/ppermute | solution.py:635
  58.4 6.1 %collective-permute-start.23 = (f32[9,8,128]{2,1,0:T(8,128)S(1)}, f32[9,8,128]{2,1,0:T(8,128)S(1)}, u32[]{:S(2)}, u32[]{:S(2)}) collective-permute-start(f32[9,8,128]{2,1,0:T(8,128)S(1)} %pad_maximum_fusion.3.own), channel_id=1, source_target_pairs={{0,8},{8,0},{16,32},{24,40},{32,16},{40,24},{48,56},{56,48},{1,9},... | collective-permute-start | bytes 110600 | tf_op jit(solution)/shard_map/ppermute | solution.py:635
